TPU v7x, 32 devices: a whole 2x2x4 slice. The times are simulated.
32 devices in a mesh: fsdp: 4 (over z), req: 8 (over y, x, core).
Axes of the slice: x: 2, y: 2, z: 4, core: 2. Of those that a mesh axis runs over, the one named last changes fastest.
Arguments:
- drafts: bfloat16 [8, 16, 2560], P('req'), may hold values from -6 to 6
- x_weight: bfloat16 [2560, 5120], P('req', 'fsdp'), may hold values from -0.125 to 0.125
- z_weight: bfloat16 [2560, 5120], P('req', 'fsdp'), may hold values from -0.125 to 0.125
- bc_weight: bfloat16 [2560, 256], P('req'), may hold values from -0.125 to 0.125
- dt_weight: bfloat16 [2560, 80], P('req', 'fsdp'), may hold values from -0.125 to 0.125
- dt_bias: float32 [80], P('fsdp'), may hold values from -3 to 0
- decay_rate: float32 [80], P('fsdp'), may hold values from 0.01 to 0.5
- conv_x_weight: bfloat16 [4, 5120], P(None, 'fsdp'), may hold values from -3 to 3
- conv_x_bias: bfloat16 [5120], P('fsdp'), may hold values from -2 to 2
- conv_bc_weight: bfloat16 [4, 256], replicated, may hold values from -3 to 3
- conv_bc_bias: bfloat16 [256], replicated, may hold values from -2 to 2
- norm_gain: bfloat16 [5120], P('fsdp'), may hold values from 0.5 to 1.5
- out_weight: bfloat16 [5120, 2560], P('fsdp', 'req'), may hold values from -0.078125 to 0.078125
- conv_x_state: bfloat16 [8, 3, 5120], P('req', None, 'fsdp'), may hold values from -6 to 6
- conv_bc_state: bfloat16 [8, 3, 256], P('req'), may hold values from -6 to 6
- ssm_state: float32 [8, 80, 64, 128], P('req', 'fsdp'), may hold values from -6 to 6
- sink_x: bfloat16 [8, 4, 5120], P('req', None, 'fsdp'), may hold values from -12 to 12
- sink_b: bfloat16 [8, 4, 128], P('req'), may hold values from -6 to 6
- page_x: bfloat16 [80, 256, 5120], P('req', None, 'fsdp'), may hold values from -3 to 3
- page_b: bfloat16 [80, 256, 128], P('req'), may hold values from -6 to 6
- page_decay: float32 [80, 80, 256], P('req', 'fsdp')
- slot_req: int32 [80], P('req'), may hold values from -1 to 7, as said below
- slot_page: int32 [80], P('req'), may hold values from 0 to 15, as said below
- page_count: int32 [8], replicated, may hold values from 1 to 16, as said below
- accepted: int32 [8], P('req'), may hold values from 1 to 16
- owner_row: int32 [8], replicated, may hold values from 0 to 7, each once
Outputs:
- mixed: bfloat16 [8, 16, 2560], P('req', None, 'fsdp')
- new_state: float32 [8, 80, 64, 128], P('req', 'fsdp')
- new_conv_x: bfloat16 [8, 3, 5120], P('req', None, 'fsdp')
- new_conv_bc: bfloat16 [8, 3, 256], P('req')
Inputs may be any that keep to these rules, and one draw needn't show every extreme that they name: `page_count`: one request has 16 pages. `slot_req`: -1 marks an empty slot. Each page 0 to page_count - 1 of every request stands in exactly one slot; a request with fewer than 16 pages also has its page numbered page_count in one slot. `slot_page`: 0 in empty slots. `owner_row`: each row once.
All inputs are finite; a program needn't handle non-finite values.
Results may differ from a plain program's by a relative error of at most 0.015.
Values may be sent and summed in bfloat16 or wider, within the bound.
No kernel may reach another device: no remote copies, remote signals or barrier semaphores. Data moves between devices by JAX's collectives and lax.ppermute only.
A program may use at most 64 MiB of HBM per device.

v0:
```python
import jax
import jax.numpy as jnp
from jax import lax
from jax.sharding import PartitionSpec as P

HD = 64
NS = 128
KC = 4
E = 5120


EPSILON = 1e-05


def conv_silu(history, fresh, kernel, offset):
    joined = jnp.concatenate([history, fresh], axis=1).astype(jnp.float32)
    length = fresh.shape[1]
    summed = offset.astype(jnp.float32) + jnp.zeros(fresh.shape, jnp.float32)
    for kernel_tap in range(KC):
        summed = (
            summed
            + kernel[kernel_tap].astype(jnp.float32) * joined[:, kernel_tap : kernel_tap + length]
        )
    return jax.nn.silu(summed).astype(jnp.bfloat16)


def local_terms(c_mat, b_mat, x_act, dtime, cumul, sink_x, sink_b):
    requests, length, head_count = dtime.shape
    inner = jnp.einsum("rtn,run->rtu", c_mat, b_mat, preferred_element_type=jnp.float32)
    later = jnp.arange(length)[:, None] >= jnp.arange(length)[None, :]
    spread = jnp.where(later[None, :, :, None], cumul[:, :, None, :] - cumul[:, None, :, :], 0.0)
    draft_weight = jnp.where(
        later[None, :, :, None], inner[..., None] * jnp.exp(spread) * dtime[:, None, :, :], 0.0
    ).astype(jnp.bfloat16)
    head_values = x_act.reshape(requests, length, head_count, HD)
    own_terms = jnp.einsum(
        "rtuh,ruhp->rthp", draft_weight, head_values, preferred_element_type=jnp.float32
    )
    sink_weight = jnp.einsum(
        "rtn,rsn->rts", c_mat, sink_b, preferred_element_type=jnp.float32
    ).astype(jnp.bfloat16)
    sink_terms = jnp.einsum("rts,rse->rte", sink_weight, sink_x, preferred_element_type=jnp.float32)
    return own_terms.reshape(requests, length, head_count * HD) + sink_terms


def page_batch(c_all, cumul_all, page_x, page_b, page_decay, slot_rows, slot_live, req_total):
    slot_count, page_len, inner_local = page_x.shape
    head_count = page_decay.shape[1]
    length = c_all.shape[1]
    queries = c_all[slot_rows]
    decay_q = cumul_all[slot_rows]
    scores = jnp.einsum("stn,spn->stp", queries, page_b, preferred_element_type=jnp.float32)
    weights = (
        scores[:, None]
        * jnp.exp(jnp.transpose(decay_q, (0, 2, 1))[:, :, :, None] - page_decay[:, :, None, :])
    ).astype(jnp.bfloat16)
    values = page_x.reshape(slot_count, page_len, head_count, HD)
    terms = jnp.einsum(
        "shtp,sphd->sthd", weights, values, preferred_element_type=jnp.float32
    ).reshape(slot_count, length * inner_local)
    selector = ((slot_rows[:, None] == jnp.arange(req_total)[None, :]) & slot_live[:, None]).astype(
        jnp.float32
    )
    summed = jnp.dot(selector.T, terms, precision=lax.Precision.HIGHEST)
    return summed.reshape(req_total, length, inner_local)


def per_device(
    drafts,
    x_weight,
    z_weight,
    bc_weight,
    dt_weight,
    dt_bias,
    decay_rate,
    conv_x_weight,
    conv_x_bias,
    conv_bc_weight,
    conv_bc_bias,
    norm_gain,
    out_weight,
    conv_x_state,
    conv_bc_state,
    ssm_state,
    sink_x,
    sink_b,
    page_x,
    page_b,
    page_decay,
    slot_req,
    slot_page,
    page_count,
    accepted,
    owner_row,
):
    req_total = owner_row.shape[0]
    local_reqs, length, width = drafts.shape
    token_rows = local_reqs * length
    inner_local = x_weight.shape[1]
    head_count = dt_weight.shape[1]
    flat_tokens = drafts.reshape(token_rows, width)
    pieces = (
        lax.all_gather(x_weight, "req", axis=0, tiled=True),
        lax.all_gather(z_weight, "req", axis=0, tiled=True),
        lax.all_gather(bc_weight, "req", axis=0, tiled=True),
        lax.all_gather(dt_weight, "req", axis=0, tiled=True),
    )
    x_proj, z_proj, bc_proj, dt_proj = tuple(
        (
            jnp.dot(flat_tokens, weight_rows, preferred_element_type=jnp.float32)
            for weight_rows in pieces
        )
    )
    x_raw = x_proj.astype(jnp.bfloat16).reshape(local_reqs, length, inner_local)
    z_raw = z_proj.astype(jnp.bfloat16).reshape(local_reqs, length, inner_local)
    bc_raw = bc_proj.astype(jnp.bfloat16).reshape(local_reqs, length, 2 * NS)
    dt_raw = dt_proj.reshape(local_reqs, length, head_count)
    x_act = conv_silu(conv_x_state, x_raw, conv_x_weight, conv_x_bias)
    bc_act = conv_silu(conv_bc_state, bc_raw, conv_bc_weight, conv_bc_bias)
    b_mat = bc_act[:, :, :NS]
    c_mat = bc_act[:, :, NS:]
    dtime = jax.nn.softplus(dt_raw + dt_bias)
    cumul = jnp.cumsum(-decay_rate * dtime, axis=1)
    c_wide, cumul_all = (
        lax.all_gather(c_mat.astype(jnp.float32), "req", axis=0, tiled=True),
        lax.all_gather(cumul, "req", axis=0, tiled=True),
    )
    c_all = c_wide.astype(jnp.bfloat16)
    guarded_query_index = jnp.maximum(slot_req, 0)
    slot_live = (slot_req >= 0) & (slot_page < page_count[guarded_query_index])
    slot_rows = owner_row[guarded_query_index]
    partial_value = page_batch(
        c_all, cumul_all, page_x, page_b, page_decay, slot_rows, slot_live, req_total
    )
    page_sum = lax.psum_scatter(partial_value, "req", scatter_dimension=0, tiled=True)
    head_values = x_act.astype(jnp.float32).reshape(local_reqs, length, head_count, HD)
    mixer_out = page_sum + local_terms(c_mat, b_mat, x_act, dtime, cumul, sink_x, sink_b)
    gated = mixer_out * jax.nn.silu(z_raw.astype(jnp.float32))
    square_sum = lax.psum(jnp.sum(gated * gated, axis=-1), "fsdp")
    normed = (
        gated * lax.rsqrt(square_sum / E + EPSILON)[..., None] * norm_gain.astype(jnp.float32)
    ).astype(jnp.bfloat16)
    normed_flat = normed.reshape(token_rows, inner_local)
    full_out = jnp.dot(
        normed_flat,
        lax.all_gather(out_weight, "req", axis=1, tiled=True),
        preferred_element_type=jnp.float32,
    )
    mixed = (
        lax.psum_scatter(full_out, "fsdp", scatter_dimension=1, tiled=True)
        .astype(jnp.bfloat16)
        .reshape(local_reqs, length, -1)
    )
    positions = jnp.arange(length)
    chosen = positions[None, :] == accepted[:, None] - 1
    cumul_last = jnp.sum(jnp.where(chosen[:, :, None], cumul, 0.0), axis=1)
    kept = positions[None, :] < accepted[:, None]
    state_spread = jnp.where(kept[:, :, None], cumul_last[:, None, :] - cumul, 0.0)
    coeff = jnp.where(kept[:, :, None], jnp.exp(state_spread) * dtime, 0.0)
    fresh_state = jnp.einsum(
        "ruh,ruhp,run->rhpn",
        coeff,
        head_values,
        b_mat.astype(jnp.float32),
        precision=lax.Precision.HIGHEST,
    )
    new_state = jnp.exp(cumul_last)[:, :, None, None] * ssm_state + fresh_state

    def tail_rows(history, fresh_rows):
        joined_rows = jnp.concatenate([history, fresh_rows], axis=1)
        return jax.vmap(
            lambda seq_rows, first_pos: lax.dynamic_slice_in_dim(seq_rows, first_pos, KC - 1, 0)
        )(joined_rows, accepted)

    new_conv_x = tail_rows(conv_x_state, x_raw)
    new_conv_bc = tail_rows(conv_bc_state, bc_raw)
    return (mixed, new_state, new_conv_x, new_conv_bc)


def solution(mesh):
    in_specs = (
        P("req", None, None),
        P("req", "fsdp"),
        P("req", "fsdp"),
        P("req", None),
        P("req", "fsdp"),
        P("fsdp"),
        P("fsdp"),
        P(None, "fsdp"),
        P("fsdp"),
        P(),
        P(),
        P("fsdp"),
        P("fsdp", "req"),
        P("req", None, "fsdp"),
        P("req", None, None),
        P("req", "fsdp", None, None),
        P("req", None, "fsdp"),
        P("req", None, None),
        P("req", None, "fsdp"),
        P("req", None, None),
        P("req", "fsdp", None),
        P("req"),
        P("req"),
        P(),
        P("req"),
        P(),
    )
    out_specs = (
        P("req", None, "fsdp"),
        P("req", "fsdp", None, None),
        P("req", None, "fsdp"),
        P("req", None, None),
    )
    return jax.shard_map(
        per_device, mesh=mesh, in_specs=in_specs, out_specs=out_specs, check_vma=False
    )
```

profile of v0, /device:TPU:0, one launch (start us, length us, event | category | flops | bytes accessed | tf_op | source)
XLA Modules:
  0.0 254.2 jit_solution(14601817807986609091)
XLA Ops:
  7.2 0.7 all-gather.6.cloned.1.call-update
  8.0 0.7 all-gather.8.cloned.1.call-update
  8.7 0.7 all-gather.10.cloned.1.call-update
  9.4 0.7 convert_element_type.158
  10.1 10.9 %all-gather = bf16[8,320,20]{1,2,0:T(8,128)(2,1)S(1)} all-gather(bf16[1,320,20]{1,2,0:T(8,128)(2,1)} %bitcast.110), channel_id=1, replica_groups=mesh['fsdp'=4,'req'=8] {'req'}, dimensions={0}, use_global_device_ids=true | all-gather | bytes 115200 | tf_op jit(solution)/shard_map/all_gather | solution.py:106
  21.1 0.7 neg.21
  21.8 1.1 compare_select_fusion
  22.9 0.7 broadcast_maximum_fusion
  23.6 1.3 gather_fusion
  24.9 9.0 %all_gather.24 = f32[8,16,20]{2,1,0:T(8,128)S(1)} all-gather(f32[1,16,20]{2,1,0:T(8,128)S(1)} %reduce_window_sum.11), channel_id=1, replica_groups=mesh['fsdp'=4,'req'=8] {'req'}, dimensions={0}, use_global_device_ids=true | all-gather | bytes 11520 | tf_op jit(solution)/shard_map/all_gather | solution.py:126
  34.7 9.5 %copy.52 = bf16[10,256,1280]{1,2,0:T(8,128)(2,1)} copy(bf16[10,256,1280]{2,1,0:T(8,128)(2,1)} %param.44) | data formatting | bytes 13107200 | tf_op args[18]
  44.2 0.7 gather_fusion.1
  45.0 1.7 fusion.13
  46.7 8.1 %all_gather.22 = bf16[8,16,128]{2,1,0:T(8,128)(2,1)S(1)} all-gather(bf16[1,16,128]{2,1,0:T(8,128)(2,1)S(1)} %slice.201), channel_id=1, replica_groups=mesh['fsdp'=4,'req'=8] {'req'}, dimensions={0}, use_global_device_ids=true | all-gather | bytes 36864 | tf_op jit(solution)/shard_map/all_gather | solution.py:125
  55.7 4.0 %fusion.9 = f32[10,16,20,64]{3,1,2,0:T(8,128)S(1)} fusion(bf16[10,256,20,64]{1,3,2,0:T(8,128)(2,1)} %bitcast.105, f32[10,20,256]{2,1,0:T(8,128)S(1)} %copy-done.4, f32[10,20,16]{2,1,0:T(8,128)S(1)} %copy.51, f32[10,16,256]{2,1,0:T(8,128)S(1)} %fusion.70), kind=kOutput, calls=%fused_computation.17 | convolution fusion | flops 107315200 | bytes 7754240 | tf_op jit(solution)/shard_map/shtp,sphd->sthd/dot_general | solution.py:58
  60.3 1.6 reshape.367
  61.9 1.7 copy.62
  63.7 1.0 fusion.10
  64.7 1.0 copy.55
  68.2 17.7 %all-gather.8.cloned.1.call-done = bf16[2560,1280]{1,0:T(8,128)(2,1)} async-done(((bf16[320,1280]{1,0:T(8,128)(2,1)}), bf16[2560,1280]{1,0:T(8,128)(2,1)}) %all-gather.8.cloned.1.call-update) | async-done | bytes 6553616 | tf_op jit(solution)/shard_map/all_gather | solution.py:103
  86.0 3.8 %fusion.4 = bf16[1,16,1280]{2,1,0:T(8,128)(2,1)S(1)} fusion(bf16[2560,1280]{1,0:T(8,128)(2,1)} %all-gather.8.cloned.1.call-done, bf16[1,16,2560]{2,1,0:T(8,128)(2,1)S(1)} %copy-done.2), kind=kOutput, calls=%fused_computation.12 | convolution fusion | flops 104878080 | bytes 6676480 | tf_op jit(solution)/shard_map/dot_general | solution.py:110
  90.4 44.1 %all-gather.10.cloned.1.call-done = bf16[2560,1280]{1,0:T(8,128)(2,1)} async-done(((bf16[320,1280]{1,0:T(8,128)(2,1)}), bf16[2560,1280]{1,0:T(8,128)(2,1)}) %all-gather.10.cloned.1.call-update) | async-done | bytes 6553616 | tf_op jit(solution)/shard_map/all_gather | solution.py:104
  134.5 3.8 %fusion.3 = f32[16,1280]{1,0:T(8,128)S(1)} fusion(bf16[2560,1280]{1,0:T(8,128)(2,1)} %all-gather.10.cloned.1.call-done, bf16[1,16,2560]{2,1,0:T(8,128)(2,1)S(1)} %copy-done.2), kind=kOutput, calls=%fused_computation.10 | convolution fusion | flops 104898560 | bytes 6717440 | tf_op jit(solution)/shard_map/dot_general | solution.py:110
  138.3 34.4 %reduce-scatter.3.cloned.1.call-done = f32[1,16,1280]{2,1,0:T(8,128)} async-done(((f32[8,16,1280]{2,1,0:T(8,128)}), f32[1,16,1280]{2,1,0:T(8,128)}) %reduce-scatter.3.cloned.1.call-update) | async-done | bytes 81936 | tf_op jit(solution)/shard_map/reduce_scatter | solution.py:135
  172.7 1.3 multiply_reduce_fusion
  174.1 11.7 %psum.7 = f32[1,16]{1,0:T(1,128)S(1)} all-reduce(f32[1,16]{1,0:T(1,128)S(1)} %bitcast.115), channel_id=1, replica_groups=mesh['fsdp'=4,'req'=8] {'fsdp'}, use_global_device_ids=true, to_apply=%region_3.4 | all-reduce | flops 16 | bytes 128 | tf_op jit(solution)/shard_map/psum | solution.py:139
  185.8 35.4 %all-gather.12.cloned.1.call-done = bf16[1280,2560]{0,1:T(8,128)(2,1)} async-done(((bf16[1280,320]{0,1:T(8,128)(2,1)}), bf16[1280,2560]{0,1:T(8,128)(2,1)}) %all-gather.12.cloned.1.call-update) | async-done | bytes 6553616 | tf_op jit(solution)/shard_map/all_gather | solution.py:146
  221.2 5.4 %fusion.32 = f32[16,2560]{1,0:T(8,128)} fusion(bf16[1280,2560]{0,1:T(8,128)(2,1)} %all-gather.12.cloned.1.call-done, f32[1,16,1280]{2,1,0:T(8,128)S(1)} %get-tuple-element.35, f32[1280]{0:T(1024)S(1)} %convert_element_type.189, f32[16]{0:T(128)S(1)} %rsqrt_bitcast_fusion), kind=kOutput, calls=%fused_computation.58 | convolution fusion | flops 104919040 | bytes 6804544 | tf_op jit(solution)/shard_map/dot_general | solution.py:144
  226.7 0.6 fusion.41
  227.3 1.6 fusion.12
  228.9 17.1 %reduce-scatter.5.cloned.1.call-done = f32[16,640]{1,0:T(8,128)} async-done(((f32[16,2560]{1,0:T(8,128)}), f32[16,640]{1,0:T(8,128)}) %reduce-scatter.5.cloned.1.call-update) | async-done | bytes 40976 | tf_op jit(solution)/shard_map/reduce_scatter | solution.py:150
  246.0 1.4 convert_bitcast_fusion
  (79 shorter events, 5.2 us)
Async XLA Ops:
  7.2 48.3 %copy-start = (bf16[10,256,128]{2,1,0:T(8,128)(2,1)S(1)}, bf16[10,256,128]{2,1,0:T(8,128)(2,1)}, u32[]{:S(2)}) copy-start(bf16[10,256,128]{2,1,0:T(8,128)(2,1)} %param.45) | copy-start | bytes 1966084
  7.2 37.8 %all-gather.6.cloned.1.call-start = ((), (), s32[]{:S(2)}) async-start(), calls=%async_computation.2 | async-start | bytes 1474560 | tf_op jit(solution)/shard_map/all_gather | solution.py:105
  7.9 78.0 %all-gather.8.cloned.1.call-start = ((), (), s32[]{:S(2)}) async-start(), calls=%async_computation.4 | async-start | bytes 7372800 | tf_op jit(solution)/shard_map/all_gather | solution.py:103
  8.7 125.9 %all-gather.10.cloned.1.call-start = ((), (), s32[]{:S(2)}) async-start(), calls=%async_computation.5 | async-start | bytes 7372800 | tf_op jit(solution)/shard_map/all_gather | solution.py:104
  9.4 163.3 %reduce-scatter.3.cloned.1.call-start = ((), (), s32[]{:S(2)}) async-start(), calls=%async_computation.3 | async-start | bytes 737280 | tf_op jit(solution)/shard_map/reduce_scatter | solution.py:135
  34.6 9.6 %copy-start.1 = (s32[8]{0:T(128)S(1)}, s32[8]{0:T(128)}, u32[]{:S(2)}) copy-start(s32[8]{0:T(128)} %param.49) | copy-start | bytes 100
  34.6 10.3 %copy-start.11 = (s32[10]{0:T(128)S(1)}, s32[10]{0:T(128)}, u32[]{:S(2)}) copy-start(s32[10]{0:T(128)} %param.47) | copy-start | bytes 124
  34.6 10.2 %copy-start.12 = (s32[10]{0:T(128)S(1)}, s32[10]{0:T(128)}, u32[]{:S(2)}) copy-start(s32[10]{0:T(128)} %param.48) | copy-start | bytes 124
  34.6 10.3 %copy-start.8 = (bf16[4,256]{1,0:T(4,128)(2,1)S(1)}, bf16[4,256]{1,0:T(4,128)(2,1)}, u32[]{:S(2)}) copy-start(bf16[4,256]{1,0:T(4,128)(2,1)} %param.35) | copy-start | bytes 6148
  34.7 10.3 %copy-start.2 = (bf16[1,16,2560]{2,1,0:T(8,128)(2,1)S(1)}, bf16[1,16,2560]{2,1,0:T(8,128)(2,1)}, u32[]{:S(2)}) copy-start(bf16[1,16,2560]{2,1,0:T(8,128)(2,1)} %param.26) | copy-start | bytes 245764
  34.7 12.0 %copy-start.7 = (bf16[1,3,256]{2,1,0:T(4,128)(2,1)S(1)}, bf16[1,3,256]{2,1,0:T(4,128)(2,1)}, u32[]{:S(2)}) copy-start(bf16[1,3,256]{2,1,0:T(4,128)(2,1)} %param.40) | copy-start | bytes 4612
  34.7 21.0 %copy-start.4 = (f32[10,20,256]{2,1,0:T(8,128)S(1)}, f32[10,20,256]{2,1,0:T(8,128)}, u32[]{:S(2)}) copy-start(f32[10,20,256]{2,1,0:T(8,128)} %param.46) | copy-start | bytes 614404
  63.6 2.9 %copy-start.9 = (bf16[1280]{0:T(1024)(128)(2,1)S(1)}, bf16[1280]{0:T(1024)(128)(2,1)}, u32[]{:S(2)}) copy-start(bf16[1280]{0:T(1024)(128)(2,1)} %param.34) | copy-start | bytes 7684
  63.6 2.9 %copy-start.10 = (bf16[1280]{0:T(1024)(128)(2,1)S(1)}, bf16[1280]{0:T(1024)(128)(2,1)}, u32[]{:S(2)}) copy-start(bf16[1280]{0:T(1024)(128)(2,1)} %param.37) | copy-start | bytes 7684
  63.6 3.7 %copy-start.5 = (bf16[4,1280]{1,0:T(4,128)(2,1)S(1)}, bf16[4,1280]{1,0:T(4,128)(2,1)}, u32[]{:S(2)}) copy-start(bf16[4,1280]{1,0:T(4,128)(2,1)} %param.33) | copy-start | bytes 30724
  65.7 155.4 %all-gather.12.cloned.1.call-start = ((), (), s32[]{:S(2)}) async-start(), calls=%async_computation.6 | async-start | bytes 7372800 | tf_op jit(solution)/shard_map/all_gather | solution.py:146
  66.3 179.6 %reduce-scatter.5.cloned.1.call-start = ((), (), s32[]{:S(2)}) async-start(), calls=%async_computation.7 | async-start | bytes 204800 | tf_op jit(solution)/shard_map/reduce_scatter | solution.py:150
  68.2 21.6 %copy-start.6 = (bf16[1,3,1280]{2,1,0:T(4,128)(2,1)S(1)}, bf16[1,3,1280]{2,1,0:T(4,128)(2,1)}, u32[]{:S(2)}) copy-start(bf16[1,3,1280]{2,1,0:T(4,128)(2,1)} %param.39) | copy-start | bytes 23044
  90.4 82.3 %copy-start.13 = (bf16[1,4,1280]{2,1,0:T(4,128)(2,1)S(1)}, bf16[1,4,1280]{2,1,0:T(4,128)(2,1)}, u32[]{:S(2)}) copy-start(bf16[1,4,1280]{2,1,0:T(4,128)(2,1)} %param.42) | copy-start | bytes 30724
  90.4 82.3 %copy-start.14 = (bf16[1,4,128]{2,1,0:T(4,128)(2,1)S(1)}, bf16[1,4,128]{2,1,0:T(4,128)(2,1)}, u32[]{:S(2)}) copy-start(bf16[1,4,128]{2,1,0:T(4,128)(2,1)} %param.43) | copy-start | bytes 3076
  221.2 6.2 %copy-start.3 = (f32[1,20,64,128]{3,2,1,0:T(8,128)S(1)}, f32[1,20,64,128]{3,2,1,0:T(8,128)}, u32[]{:S(2)}) copy-start(f32[1,20,64,128]{3,2,1,0:T(8,128)} %param.41) | copy-start | bytes 1966084
Sparse Core Ops, SparseCore 0:
  9.9 27.3 all-gather.5
  39.2 46.7 all-gather.7
  87.8 46.6 all-gather.9
  138.1 34.6 reduce-scatter.2
  174.5 46.6 all-gather.11
  226.7 19.2 reduce-scatter.4
where the time goes:
time: 255 us; the launch traced here: 254 us
  waiting for transfers between devices  151 us (59%)
  blocking collectives  39.7 us (16%)
  matrix products  24.3 us (10%)
  local copies, waits for them, and re-layouts  18.4 us (7%)
  between operations  15.1 us (6%)
  other arithmetic  5.18 us (2%)
    all_gather x1, waiting for transfers between devices, per_device(): lax.all_gather(z_weight, 'req', axis=0, tiled=True)  44.1 us
    all_gather x1, waiting for transfers between devices, per_device(): lax.all_gather(out_weight, 'req', axis=1, tiled=True)  35.4 us
    reduce_scatter x1, waiting for transfers between devices, per_device(): lax.psum_scatter(partial_value, 'req', scatter_dimension=0, tiled=True)  34.4 us
    all_gather x1, waiting for transfers between devices, per_device(): lax.all_gather(x_weight, 'req', axis=0, tiled=True)  17.7 us
    reduce_scatter x1, waiting for transfers between devices, per_device(): lax.psum_scatter(full_out, 'fsdp', scatter_dimension=1, tiled=True)  17.1 us
    psum x1, blocking collectives, per_device(): square_sum = lax.psum(jnp.sum(gated * gated, axis=-1), 'fsdp')  11.7 us
    unnamed x33, local copies, waits for them, and re-layouts  11.4 us
    all_gather x1, blocking collectives, per_device(): lax.all_gather(dt_weight, 'req', axis=0, tiled=True)  10.9 us
  transfers between devices with their start and end apart: 6, of which 5 were waited for; matrix products, arithmetic and copies ran while one was open for 16% of the time, Pallas kernels for 0%

commit v1 on v0

v1 whole, which is shorter than its diff:
```python
import functools

import jax
import jax.numpy as jnp
from jax import lax
from jax.experimental import pallas as pl
from jax.experimental.pallas import tpu as pltpu
from jax.sharding import PartitionSpec as P

HD = 64
NS = 128
KC = 4
EPSILON = 1e-05
BF = jnp.bfloat16
F32 = jnp.float32
VMEM_LIMIT = 40 * 1024 * 1024
BCW = 3 * NS


def vmem():
    return pl.BlockSpec(memory_space=pltpu.VMEM)


def smem():
    return pl.BlockSpec(memory_space=pltpu.SMEM)


def call(body, out_shape, in_specs, *args, flops=0, nbytes=0, scratch=()):
    return pl.pallas_call(
        body,
        out_shape=out_shape,
        in_specs=in_specs,
        out_specs=jax.tree.map(lambda _: vmem(), out_shape),
        scratch_shapes=list(scratch),
        compiler_params=pltpu.CompilerParams(vmem_limit_bytes=VMEM_LIMIT),
        cost_estimate=pl.CostEstimate(flops=flops, bytes_accessed=nbytes, transcendentals=0),
    )(*args)


def sds(shape, dtype):
    return jax.ShapeDtypeStruct(shape, dtype)


def silu(v):
    return v / (1.0 + jnp.exp(-v))


def softplus(v):
    return jnp.maximum(v, 0.0) + jnp.log1p(jnp.exp(-jnp.abs(v)))


def conv(history, fresh, taps, offset):
    length = fresh.shape[0]
    joined = jnp.concatenate([history, fresh], axis=0)
    total = offset + taps[0:1] * joined[0:length]
    for k in range(1, KC):
        total = total + taps[k : k + 1] * joined[k : k + length]
    return silu(total)


def running_sum(v):
    length = v.shape[0]
    step = 1
    while step < length:
        v = v + jnp.concatenate([jnp.zeros((step, v.shape[1]), v.dtype), v[: length - step]], axis=0)
        step *= 2
    return v


def head_diag(weights, values):
    heads = len(weights)
    length = weights[0].shape[0]
    if heads == 1:
        return jnp.dot(weights[0], values, preferred_element_type=F32)
    full = jnp.dot(jnp.concatenate(weights, axis=0), values, preferred_element_type=F32)
    owner = lax.broadcasted_iota(jnp.int32, (length, heads * HD), 1) // HD
    out = jnp.where(owner == 0, full[:length], 0.0)
    for i in range(1, heads):
        out = jnp.where(owner == i, full[i * length : (i + 1) * length], out)
    return out


def project_kernel(length, fan, scalar, *refs):
    blocks = refs[:fan]
    xo, xp, zo, zp, bo, bp, do, dp = refs[fan : fan + 8]
    outs = refs[fan + 8 :]
    half = xo.shape[0]
    inner = xo.shape[1]
    heads = do.shape[1]
    tokens = jnp.concatenate([b[0:length, : 2 * half] for b in blocks], axis=0)
    first = scalar[0] == 0
    low, high = tokens[:, :half], tokens[:, half:]
    own = jnp.where(first, low, high)
    other = jnp.where(first, high, low)

    def proj(wo, wp):
        return jnp.dot(own, wo[...], preferred_element_type=F32) + jnp.dot(
            other, wp[...], preferred_element_type=F32
        )

    bc = proj(bo, bp).astype(BF)
    dt = proj(do, dp)
    dt_hi = dt.astype(BF)
    dt_lo = (dt - dt_hi.astype(F32)).astype(BF)
    tail = jnp.concatenate(
        [bc, dt_hi, dt_lo, jnp.zeros((fan * length, NS - 2 * heads), BF)], axis=1
    )
    x = proj(xo, xp).astype(BF)
    z = proj(zo, zp).astype(BF)
    for s, out in enumerate(outs):
        rows = slice(s * length, (s + 1) * length)
        out[:, :inner] = x[rows]
        out[:, inner : 2 * inner] = z[rows]
        for t in range(fan):
            base = 2 * inner + BCW * t
            out[:, base : base + BCW] = tail[t * length : (t + 1) * length]


def mix_kernel(
    length, fan, inner, heads, *refs
):
    parts = refs[:fan]
    blocks = refs[fan : 2 * fan]
    (xs, xw, xb, bw, bb, dt_bias, rate) = refs[2 * fan : 2 * fan + 7]
    packed, x_raw_o, z_raw_o, x_act_o, bc_raw_o, bc_act_o, dtime_o = refs[2 * fan + 7 :]
    bw_f = bw[...].astype(F32)
    bb_f = bb[...].astype(F32)
    for t in range(fan):
        acc = None
        for s in range(fan):
            base = 2 * inner + BCW * ((t + s) % fan)
            piece = parts[s][:, base : base + BCW].astype(F32)
            acc = piece if acc is None else acc + piece
        bc_raw = acc[:, : 2 * NS].astype(BF)
        dt = acc[:, 2 * NS : 2 * NS + heads] + acc[:, 2 * NS + heads : 2 * NS + 2 * heads]
        history = blocks[t][length : 2 * length, : 2 * NS].astype(F32)[: KC - 1]
        bc_act = conv(history, bc_raw.astype(F32), bw_f, bb_f).astype(BF)
        dtime = softplus(dt + dt_bias[...])
        cumul = running_sum(-rate[...] * dtime)
        packed[t * length : (t + 1) * length, :NS] = bc_act[:, NS:].astype(F32)
        packed[t * length : (t + 1) * length, NS:] = jnp.concatenate(
            [cumul, jnp.zeros((length, NS - heads), F32)], axis=1
        )
        if t == 0:
            bc_raw_o[...] = bc_raw
            bc_act_o[...] = bc_act
            dtime_o[...] = dtime
    acc = parts[0][:, : 2 * inner].astype(F32)
    for s in range(1, fan):
        acc = acc + parts[s][:, : 2 * inner].astype(F32)
    x_raw = acc[:, :inner].astype(BF)
    x_raw_o[...] = x_raw
    z_raw_o[...] = acc[:, inner:].astype(BF)
    x_act_o[...] = conv(
        xs[...].astype(F32), x_raw.astype(F32), xw[...].astype(F32), xb[...].astype(F32)
    ).astype(BF)


def page_kernel(
    length, heads, where_ref, live_ref, own_ref, other_ref, b_ref, decay_ref, x_hbm,
    mine_out, other_out, query, total, pages, sems,
):
    slots = x_hbm.shape[0]
    half = own_ref.shape[0]

    def copy(s):
        return pltpu.make_async_copy(x_hbm.at[s], pages.at[s], sems.at[s])

    for s in range(slots):
        @pl.when(live_ref[s] > 0)
        def _():
            copy(s).start()

    query[0:half] = own_ref[...]
    query[half:] = other_ref[...]
    total[...] = jnp.zeros_like(total)

    def visit(s, carry):
        @pl.when(live_ref[s] > 0)
        def _():
            rows = pl.ds(pl.multiple_of(where_ref[s] * length, length), length)
            packed = query[rows, :]
            c_mat = packed[:, :NS].astype(BF)
            cumul = packed[:, NS:]
            scores = lax.dot_general(
                c_mat, b_ref[s], (((1,), (1,)), ((), ())), preferred_element_type=F32
            )
            decay = decay_ref[s]
            copy(s).wait()
            for first in range(0, heads, 4):
                last = min(first + 4, heads)
                weights = [
                    (scores * jnp.exp(cumul[:, h : h + 1] - decay[h : h + 1, :])).astype(BF)
                    for h in range(first, last)
                ]
                cols = slice(first * HD, last * HD)
                total[rows, cols] += head_diag(weights, pages[s, :, cols])
        return carry

    lax.fori_loop(0, slots, visit, 0)
    mine_out[...] = total[0:half].astype(BF)
    other_out[...] = total[half:].astype(BF)


def local_kernel(length, heads, packed, x_act, bc_act, dtime_ref, sink_x, sink_b, out):
    c_mat = bc_act[:, NS:]
    b_mat = bc_act[:, :NS]
    inner = lax.dot_general(c_mat, b_mat, (((1,), (1,)), ((), ())), preferred_element_type=F32)
    cumul = packed[0:length, NS:]
    dtime = jnp.concatenate(
        [dtime_ref[...], jnp.zeros((length, NS - heads), F32)], axis=1
    )
    cumul_t = jnp.transpose(cumul)
    dtime_t = jnp.transpose(dtime)
    row = lax.broadcasted_iota(jnp.int32, (length, length), 0)
    col = lax.broadcasted_iota(jnp.int32, (length, length), 1)
    later = row >= col
    sink_w = lax.dot_general(
        c_mat, sink_b[...], (((1,), (1,)), ((), ())), preferred_element_type=F32
    ).astype(BF).astype(F32)
    for first in range(0, heads, 4):
        last = min(first + 4, heads)
        weights = []
        for h in range(first, last):
            spread = jnp.where(later, cumul[:, h : h + 1] - cumul_t[h : h + 1, :], 0.0)
            weights.append(
                jnp.where(later, inner * jnp.exp(spread) * dtime_t[h : h + 1, :], 0.0).astype(BF)
            )
        cols = slice(first * HD, last * HD)
        acc = head_diag(weights, x_act[:, cols])
        sinks = sink_x[:, cols].astype(F32)
        for q in range(sinks.shape[0]):
            acc = acc + sink_w[:, q : q + 1] * sinks[q : q + 1]
        out[:, cols] = acc


def state_kernel(length, heads, accepted, packed, dtime_ref, x_act, bc_act, ssm, out):
    cumul = packed[0:length, NS : NS + heads]
    count = accepted[0]
    place = lax.broadcasted_iota(jnp.int32, (length, heads), 0)
    last = jnp.sum(jnp.where(place == count - 1, cumul, 0.0), axis=0, keepdims=True)
    kept = place < count
    coeff = jnp.where(kept, jnp.exp(jnp.where(kept, last - cumul, 0.0)) * dtime_ref[...], 0.0)
    factor = jnp.exp(last)
    b_mat = bc_act[:, :NS]
    twice_b = jnp.concatenate([b_mat, b_mat], axis=0)
    for h in range(heads):
        scaled = x_act[:, h * HD : (h + 1) * HD].astype(F32) * coeff[:, h : h + 1]
        high = scaled.astype(BF)
        low = (scaled - high.astype(F32)).astype(BF)
        fresh = lax.dot_general(
            jnp.concatenate([high, low], axis=0), twice_b,
            (((0,), (0,)), ((), ())), preferred_element_type=F32,
        )
        out[h] = factor[:, h : h + 1] * ssm[h] + fresh


def gate_kernel(fan, *refs):
    mine, parts, local, z_raw, out = refs[0], refs[1:fan], refs[fan], refs[fan + 1], refs[fan + 2]
    acc = local[...] + mine[...].astype(F32)
    for p in parts:
        acc = acc + p[...].astype(F32)
    out[...] = (acc * silu(z_raw[...].astype(F32))).astype(BF)


def out_kernel(length, fan, scalar, *refs):
    blocks = refs[:fan]
    gain, wo, wp = refs[fan : fan + 3]
    outs = refs[fan + 3 : 2 * fan + 3]
    whole = refs[2 * fan + 3]
    cols = wo.shape[1]
    g = jnp.concatenate([b[...] for b in blocks], axis=0).astype(F32)
    squares = jnp.sum(g * g, axis=1, keepdims=True)
    scaled = (g * gain[...].astype(F32)).astype(BF)
    own = jnp.dot(scaled, wo[...], preferred_element_type=F32)
    other = jnp.dot(scaled, wp[...], preferred_element_type=F32)
    first = scalar[0] == 0
    high = squares.astype(BF).astype(F32)
    low = squares - high
    lane = lax.broadcasted_iota(jnp.int32, (fan * length, NS), 1)
    whole[:, :cols] = jnp.where(first, own, other)
    whole[:, cols : 2 * cols] = jnp.where(first, other, own)
    whole[:, 2 * cols :] = jnp.where(lane == 0, high, jnp.where(lane == 1, low, 0.0))
    for s, out in enumerate(outs):
        rows = pl.ds(pl.multiple_of(scalar[1 + s] * length, length), length)
        out[...] = whole[rows, :].astype(BF)


def final_kernel(width, inner_total, *refs):
    parts, out = refs[:-1], refs[-1]
    acc = parts[0][...].astype(F32)
    for p in parts[1:]:
        acc = acc + p[...].astype(F32)
    squares = acc[:, width : width + 1] + acc[:, width + 1 : width + 2]
    out[...] = (acc[:, :width] * lax.rsqrt(squares / inner_total + EPSILON)).astype(BF)


def per_device(
    reqs, fan,
    drafts, x_weight, z_weight, bc_weight, dt_weight, dt_bias, decay_rate,
    conv_x_weight, conv_x_bias, conv_bc_weight, conv_bc_bias, norm_gain, out_weight,
    conv_x_state, conv_bc_state, ssm_state, sink_x, sink_b, page_x, page_b, page_decay,
    slot_req, slot_page, page_count, accepted, owner_row,
):
    _, length, width = drafts.shape
    inner = x_weight.shape[1]
    heads = dt_weight.shape[1]
    slots = page_x.shape[0]
    me = lax.axis_index("req")
    zed = lax.axis_index("fsdp")
    pair, side = me // 2, me % 2

    def swap(v):
        return lax.ppermute(v, "req", [(j, j ^ 1) for j in range(reqs)])

    def shift(v, step):
        return lax.ppermute(
            v, "req", [(j, 2 * ((j // 2 + step) % fan) + j % 2) for j in range(reqs)]
        )

    xp, zp, bp, dp = swap(x_weight), swap(z_weight), swap(bc_weight), swap(dt_weight)

    share = width // fan
    wide = max(share, 2 * NS)
    history = jnp.pad(conv_bc_state[0], ((0, length - (KC - 1)), (0, wide - 2 * NS)))

    def draft_block(step):
        start = ((pair + step) % fan) * share
        piece = lax.dynamic_slice(drafts[0], (0, start), (length, share))
        return jnp.concatenate([jnp.pad(piece, ((0, 0), (0, wide - share))), history], axis=0)

    blocks = [draft_block(0)] + [shift(draft_block(s), s) for s in range(1, fan)]

    message = sds((length, 2 * inner + BCW * fan), BF)
    n_cols = 2 * inner + 2 * NS + heads
    parts = call(
        functools.partial(project_kernel, length, fan),
        [message] * fan,
        [smem()] + [vmem()] * (fan + 8),
        side.astype(jnp.int32)[None],
        *blocks, x_weight, xp, z_weight, zp, bc_weight, bp, dt_weight, dp,
        flops=2 * fan * length * share * n_cols, nbytes=2 * share * n_cols,
    )
    parts = [parts[0]] + [shift(parts[s], -s) for s in range(1, fan)]

    packed, x_raw, z_raw, x_act, bc_raw, bc_act, dtime = call(
        functools.partial(mix_kernel, length, fan, inner, heads),
        [
            sds((fan * length, 2 * NS), F32),
            sds((length, inner), BF), sds((length, inner), BF), sds((length, inner), BF),
            sds((length, 2 * NS), BF), sds((length, 2 * NS), BF), sds((length, heads), F32),
        ],
        [vmem()] * (2 * fan + 7),
        *parts, *blocks, conv_x_state[0], conv_x_weight, conv_x_bias[None],
        conv_bc_weight, conv_bc_bias[None], dt_bias[None], decay_rate[None],
        flops=100 * length * inner, nbytes=length * inner * 20,
    )
    packed_other = swap(packed)

    guarded = jnp.maximum(slot_req, 0)
    live = (slot_req >= 0) & (slot_page < page_count[guarded])
    rows = owner_row[guarded]
    where = (rows % 2 != side).astype(jnp.int32) * fan + (pair - rows // 2) % fan
    partial = sds((fan * length, inner), BF)
    mine, others = pl.pallas_call(
        functools.partial(page_kernel, length, heads),
        out_shape=[partial, partial],
        in_specs=[smem(), smem()] + [vmem()] * 4 + [pl.BlockSpec(memory_space=pl.ANY)],
        out_specs=[vmem(), vmem()],
        scratch_shapes=[
            pltpu.VMEM((2 * fan * length, 2 * NS), F32),
            pltpu.VMEM((2 * fan * length, inner), F32),
            pltpu.VMEM(page_x.shape, BF),
            pltpu.SemaphoreType.DMA((slots,)),
        ],
        compiler_params=pltpu.CompilerParams(vmem_limit_bytes=VMEM_LIMIT),
        cost_estimate=pl.CostEstimate(
            flops=8 * slots * length * page_x.shape[1] * inner,
            bytes_accessed=2 * page_x.size, transcendentals=0,
        ),
    )(where.astype(jnp.int32), live.astype(jnp.int32), packed, packed_other, page_b, page_decay, page_x)
    others = swap(others)
    page_parts = (mine.astype(F32) + others.astype(F32)).astype(BF).reshape(fan, length, inner)
    page_parts = [page_parts[0]] + [shift(page_parts[s], -s) for s in range(1, fan)]

    local = call(
        functools.partial(local_kernel, length, heads),
        sds((length, inner), F32), [vmem()] * 6,
        packed, x_act, bc_act, dtime, sink_x[0], sink_b[0],
        flops=40 * length * inner, nbytes=length * inner * 8,
    )
    gated = call(
        functools.partial(gate_kernel, fan),
        sds((length, inner), BF), [vmem()] * (fan + 2),
        *page_parts, local, z_raw,
        flops=40 * length * inner, nbytes=length * inner * 8,
    )

    gated_all = [gated] + [shift(gated, s) for s in range(1, fan)]
    new_state = call(
        functools.partial(state_kernel, length, heads),
        sds(ssm_state.shape[1:], F32), [smem()] + [vmem()] * 5,
        accepted, packed, dtime, x_act, bc_act, ssm_state[0],
        flops=64 * inner * NS, nbytes=8 * inner * NS,
    )

    cols = out_weight.shape[1]
    send = jnp.stack([side] + [(pair - zed - s) % fan for s in range(fan)]).astype(jnp.int32)
    out_shape = sds((length, 2 * cols + NS), BF)
    out_parts = call(
        functools.partial(out_kernel, length, fan),
        [out_shape] * fan,
        [smem()] + [vmem()] * (fan + 3),
        send, *gated_all, norm_gain[None], out_weight, swap(out_weight),
        flops=4 * fan * length * inner * cols, nbytes=4 * inner * cols,
        scratch=[pltpu.VMEM((fan * length, 2 * cols + NS), F32)],
    )

    def to_owner(v, step):
        moves = [
            (f * reqs + j, (j // 2) * reqs + 2 * ((f + step) % fan) + j % 2)
            for f in range(fan)
            for j in range(reqs)
        ]
        return lax.ppermute(v, ("fsdp", "req"), moves)

    arrived = [to_owner(out_parts[s], s) for s in range(fan)]
    mixed = call(
        functools.partial(final_kernel, 2 * cols, inner * fan),
        sds((length, 2 * cols), BF), [vmem()] * fan, *arrived,
        flops=length * cols * 10, nbytes=length * cols * 10,
    )

    def tail_rows(past, fresh):
        joined = jnp.concatenate([past, fresh], axis=0)
        return lax.dynamic_slice_in_dim(joined, accepted[0], KC - 1, 0)[None]

    return (
        mixed[None],
        new_state[None],
        tail_rows(conv_x_state[0], x_raw),
        tail_rows(conv_bc_state[0], bc_raw),
    )


def solution(mesh):
    in_specs = (
        P("req", None, None),
        P("req", "fsdp"),
        P("req", "fsdp"),
        P("req", None),
        P("req", "fsdp"),
        P("fsdp"),
        P("fsdp"),
        P(None, "fsdp"),
        P("fsdp"),
        P(),
        P(),
        P("fsdp"),
        P("fsdp", "req"),
        P("req", None, "fsdp"),
        P("req", None, None),
        P("req", "fsdp", None, None),
        P("req", None, "fsdp"),
        P("req", None, None),
        P("req", None, "fsdp"),
        P("req", None, None),
        P("req", "fsdp", None),
        P("req"),
        P("req"),
        P(),
        P("req"),
        P(),
    )
    out_specs = (
        P("req", None, "fsdp"),
        P("req", "fsdp", None, None),
        P("req", None, "fsdp"),
        P("req", None, None),
    )
    reqs, fan = mesh.shape["req"], mesh.shape["fsdp"]
    assert reqs == 2 * fan
    return jax.shard_map(
        functools.partial(per_device, reqs, fan),
        mesh=mesh, in_specs=in_specs, out_specs=out_specs, check_vma=False,
    )
```

time: 255 us -> 73 us (0.29)
  waiting for transfers between devices: 151 us -> 14.6 us
  blocking collectives: 39.7 us -> 0 us
  starting transfers between devices: 0.23 us -> 26.9 us
  matrix products: 24.3 us -> 0 us
  between operations: 15.1 us -> 1.58 us
  Pallas kernels: 0 us -> 8.32 us
    all_gather x4 -> x0, waiting for transfers between devices: 97.2 us -> none  [the longest x1 44.1 us: per_device(): lax.all_gather(z_weight, 'req', axis=0, tiled=True)]
    reduce_scatter x2 -> x0, waiting for transfers between devices: 51.5 us -> none  [the longest x1 34.4 us: per_device(): lax.psum_scatter(partial_value, 'req', scatter_dimension=0, tiled=True)]
    all_gather x3 -> x0, blocking collectives: 28 us -> none  [the longest x1 10.9 us: per_device(): lax.all_gather(dt_weight, 'req', axis=0, tiled=True)]
    ppermute x0 -> x23, starting transfers between devices: none -> 26.9 us  [the longest x12 15.7 us: shift(): lax.ppermute(v, 'req', [(j, 2 * ((j // 2 + step) % fan) + j % 2) for j in...]
    dot_general x12 -> x0, matrix products: 24.3 us -> none  [the longest x4 10.4 us: per_device(): jnp.dot(flat_tokens, weight_rows, preferred_element_type=jnp.float32)]
    ppermute x0 -> x23, waiting for transfers between devices: none -> 14.6 us  [the longest x12 10.4 us: shift(): lax.ppermute(v, 'req', [(j, 2 * ((j // 2 + step) % fan) + j % 2) for j in...]
    psum x1 -> x0, blocking collectives: 11.7 us -> none  [per_device(): square_sum = lax.psum(jnp.sum(gated * gated, axis=-1), 'fsdp')]
    pallas_call x0 -> x8, Pallas kernels: none -> 8.32 us  [the longest x7 4.85 us: call(): pl.pallas_call(body, out_shape=out_shape, in_specs=in_specs, out_specs=ja...]
  transfers between devices with their start and end apart: 6 -> 23, of which waited for: 5 -> 10; matrix products, arithmetic and copies ran while one was open for 16% -> 16% of each run, Pallas kernels for 0% -> 2%
where the time goes in v1:
time: 73 us; the launch traced here: 73.3 us
  starting transfers between devices  26.9 us (37%)
  local copies, waits for them, and re-layouts  18.6 us (25%)
  waiting for transfers between devices  14.6 us (20%)
  Pallas kernels  8.32 us (11%)
  other arithmetic  3.32 us (5%)
  between operations  1.58 us (2%)
    ppermute x12, starting transfers between devices, shift(): lax.ppermute(v, 'req', [(j, 2 * ((j // 2 + step) % fan) + j % 2) for j in...  15.7 us
    unnamed x38, local copies, waits for them, and re-layouts  12.8 us
    ppermute x12, waiting for transfers between devices, shift(): lax.ppermute(v, 'req', [(j, 2 * ((j // 2 + step) % fan) + j % 2) for j in...  10.4 us
    ppermute x4, starting transfers between devices, to_owner(): return lax.ppermute(v, ('fsdp', 'req'), moves)  8.39 us
    pallas_call x7, Pallas kernels, call(): pl.pallas_call(body, out_shape=out_shape, in_specs=in_specs, out_specs=ja...  4.85 us
    pallas_call x1, Pallas kernels, per_device(): pl.pallas_call(functools.partial(page_kernel, length, heads), out_shape=[...  3.47 us
    ppermute x7, starting transfers between devices, swap(): return lax.ppermute(v, 'req', [(j, j ^ 1) for j in range(reqs)])  2.79 us
    ppermute x7, waiting for transfers between devices, swap(): return lax.ppermute(v, 'req', [(j, j ^ 1) for j in range(reqs)])  2.29 us
  transfers between devices with their start and end apart: 23, of which 10 were waited for; matrix products, arithmetic and copies ran while one was open for 16% of the time, Pallas kernels for 2%

profile of v1, /device:TPU:0, one launch (start us, length us, event | category | flops | bytes accessed | tf_op | source)
XLA Modules:
  0.0 73.3 jit_solution(14605041489670116790)
XLA Ops:
  1.3 0.8 %dynamic-slice_bitcast_fusion = (bf16[16,640]{1,0:T(8,128)(2,1)S(1)}, bf16[16,640]{1,0:T(8,128)(2,1)S(1)}, bf16[16,640]{1,0:T(8,128)(2,1)S(1)}, bf16[16,640]{1,0:T(8,128)(2,1)S(1)}) fusion(bf16[1,16,2560]{2,1,0:T(8,128)(2,1)} %param.26, s32[]{:T(128)S(6)} %select_n.92, s32[]{:T(128)S(6)} %select_n.88, s32[]{:T(128)S(6)} %select_n.86, s32[]{:T(128)S(6)} %select_n.90), kind=kLoop, calls=%fused_computation.11 | loop fusion | bytes 163856 | tf_op jit(solution)/shard_map/dynamic_slice | solution.py:329
  2.7 3.9 %collective-permute-start.2 = (bf16[32,640]{1,0:T(8,128)(2,1)S(1)}, bf16[32,640]{1,0:T(8,128)(2,1)S(1)}, u32[]{:S(2)}, u32[]{:S(2)}) collective-permute-start(bf16[32,640]{1,0:T(8,128)(2,1)S(1)} %get-tuple-element.46), channel_id=1, source_target_pairs={{0,6},{1,7},{2,0},{3,1},{4,2},{5,3},{6,4},{7,5},{8,14},{9,15},{10,... | collective-permute-start | bytes 122888 | tf_op jit(solution)/shard_map/ppermute | solution.py:317
  6.7 0.9 %copy.39.refs_10_ = bf16[320,20]{1,0:T(8,128)(2,1)S(1)} copy(bf16[320,20]{0,1:T(8,128)(2,1)} %param.30) | data formatting | bytes 25600 | tf_op args[4]
  8.9 1.1 %collective-permute-start.1 = (bf16[32,640]{1,0:T(8,128)(2,1)S(1)}, bf16[32,640]{1,0:T(8,128)(2,1)S(1)}, u32[]{:S(2)}, u32[]{:S(2)}) collective-permute-start(bf16[32,640]{1,0:T(8,128)(2,1)S(1)} %get-tuple-element.49), channel_id=1, source_target_pairs={{0,4},{1,5},{2,6},{3,7},{4,0},{5,1},{6,2},{7,3},{8,12},{9,13},{10,... | collective-permute-start | bytes 122888 | tf_op jit(solution)/shard_map/ppermute | solution.py:317
  11.3 1.3 %gather_fusion = s32[10]{0:T(128)S(1)} fusion(s32[8]{0:T(128)} %param.51, s32[1024]{0:T(1024)S(1)} %pad_clamp_fusion), kind=kCustom, calls=%fused_computation | custom fusion | bytes 120 | tf_op jit(solution)/shard_map/gather | solution.py:362
  13.8 1.1 %copy-done.2 = bf16[320,1280]{1,0:T(8,128)(2,1)S(1)} copy-done((bf16[320,1280]{1,0:T(8,128)(2,1)S(1)}, bf16[320,1280]{1,0:T(8,128)(2,1)}, u32[]{:S(2)}) %copy-start.2) | copy-done | bytes 819224
  14.9 1.1 %copy-done.3 = bf16[320,1280]{1,0:T(8,128)(2,1)S(1)} copy-done((bf16[320,1280]{1,0:T(8,128)(2,1)S(1)}, bf16[320,1280]{1,0:T(8,128)(2,1)}, u32[]{:S(2)}) %copy-start.3) | copy-done | bytes 819224
  16.1 0.9 %copy-done.7 = bf16[320,256]{1,0:T(8,128)(2,1)S(1)} copy-done((bf16[320,256]{1,0:T(8,128)(2,1)S(1)}, bf16[320,256]{1,0:T(8,128)(2,1)}, u32[]{:S(2)}) %copy-start.7) | copy-done | bytes 163864
  17.0 1.0 %shard_map.273 = (bf16[16,4096]{1,0:T(8,128)(2,1)S(1)}, bf16[16,4096]{1,0:T(8,128)(2,1)S(1)}, bf16[16,4096]{1,0:T(8,128)(2,1)S(1)}, bf16[16,4096]{1,0:T(8,128)(2,1)S(1)}) custom-call(s32[1]{0:T(128)} %bitcast.scalar, bf16[32,640]{1,0:T(8,128)(2,1)S(1)} %get-tuple-element.47.refs_0_.refs_4_, bf16[32,640]{1,0:T(8,128)(2,1)S(1)} %collective-permute-done.refs_1_.refs_5_, ...), custom_call_target="tpu_custom_call" | custom-call | flops 232325120 | bytes 3630080 | tf_op jit(solution)/shard_map/pallas_call | solution.py:29
  18.0 2.1 %collective-permute-start.7 = (bf16[16,4096]{1,0:T(8,128)(2,1)S(1)}, bf16[16,4096]{1,0:T(8,128)(2,1)S(1)}, u32[]{:S(2)}, u32[]{:S(2)}) collective-permute-start(bf16[16,4096]{1,0:T(8,128)(2,1)S(1)} %get-tuple-element.22), channel_id=1, source_target_pairs={{0,6},{1,7},{2,0},{3,1},{4,2},{5,3},{6,4},{7,5},{8,14},{9,15},{10,... | collective-permute-start | bytes 393224 | tf_op jit(solution)/shard_map/ppermute | solution.py:317
  20.1 1.4 %collective-permute-start.8 = (bf16[16,4096]{1,0:T(8,128)(2,1)S(1)}, bf16[16,4096]{1,0:T(8,128)(2,1)S(1)}, u32[]{:S(2)}, u32[]{:S(2)}) collective-permute-start(bf16[16,4096]{1,0:T(8,128)(2,1)S(1)} %get-tuple-element.23), channel_id=1, source_target_pairs={{0,4},{1,5},{2,6},{3,7},{4,0},{5,1},{6,2},{7,3},{8,12},{9,13},{10,... | collective-permute-start | bytes 393224 | tf_op jit(solution)/shard_map/ppermute | solution.py:317
  22.2 1.8 %collective-permute-done.7.refs_1_ = bf16[16,4096]{1,0:T(8,128)(2,1)S(1)} collective-permute-done((bf16[16,4096]{1,0:T(8,128)(2,1)S(1)}, bf16[16,4096]{1,0:T(8,128)(2,1)S(1)}, u32[]{:S(2)}, u32[]{:S(2)}) %collective-permute-start.7) | collective-permute-done | bytes 131104 | tf_op jit(solution)/shard_map/ppermute | solution.py:317
  24.0 3.9 %collective-permute-done.8.refs_2_ = bf16[16,4096]{1,0:T(8,128)(2,1)S(1)} collective-permute-done((bf16[16,4096]{1,0:T(8,128)(2,1)S(1)}, bf16[16,4096]{1,0:T(8,128)(2,1)S(1)}, u32[]{:S(2)}, u32[]{:S(2)}) %collective-permute-start.8) | collective-permute-done | bytes 131104 | tf_op jit(solution)/shard_map/ppermute | solution.py:317
  31.7 1.2 %collective-permute-done.10.other_ref = f32[64,256]{1,0:T(8,128)S(1)} collective-permute-done((f32[64,256]{1,0:T(8,128)S(1)}, f32[64,256]{1,0:T(8,128)S(1)}, u32[]{:S(2)}, u32[]{:S(2)}) %collective-permute-start.10) | collective-permute-done | bytes 65568 | tf_op jit(solution)/shard_map/ppermute | solution.py:314
  32.9 2.9 %copy-done.1 = bf16[10,256,1280]{2,1,0:T(8,128)(2,1)S(1)} copy-done((bf16[10,256,1280]{2,1,0:T(8,128)(2,1)S(1)}, bf16[10,256,1280]{2,1,0:T(8,128)(2,1)}, u32[]{:S(2)}) %copy-start.1) | copy-done | bytes 6553624
  35.7 0.9 %copy-done.6 = f32[10,20,256]{2,1,0:T(8,128)S(1)} copy-done((f32[10,20,256]{2,1,0:T(8,128)S(1)}, f32[10,20,256]{2,1,0:T(8,128)}, u32[]{:S(2)}) %copy-start.6) | copy-done | bytes 204824
  36.7 3.5 %shard_map.275 = (bf16[64,1280]{1,0:T(8,128)(2,1)S(1)}, bf16[64,1280]{1,0:T(8,128)(2,1)S(1)}) custom-call(s32[10]{0:T(128)S(1)} %fusion.9.where_ref, s32[10]{0:T(128)S(1)} %and_convert_fusion.live_ref, f32[64,256]{1,0:T(8,128)S(1)} %get-tuple-element.25.own_ref.packed, f32[64,256]{1,0:T(8,128)S(1)} %collective-permute-done.10.other_ref, ...), custom_call_target="tpu_custom_call" | custom-call | flops 419430400 | bytes 6553600 | tf_op jit(solution)/shard_map/pallas_call | solution.py:365
  40.2 1.5 %collective-permute-start.11 = (bf16[64,1280]{1,0:T(8,128)(2,1)S(1)}, bf16[64,1280]{1,0:T(8,128)(2,1)S(1)}, u32[]{:S(2)}, u32[]{:S(2)}) collective-permute-start(bf16[64,1280]{1,0:T(8,128)(2,1)S(1)} %get-tuple-element.27), channel_id=1, source_target_pairs={{0,1},{1,0},{2,3},{3,2},{4,5},{5,4},{6,7},{7,6},{8,9},{9,8},{10,11... | collective-permute-start | bytes 491528 | tf_op jit(solution)/shard_map/ppermute | solution.py:314
  41.7 0.9 %collective-permute-done.11 = bf16[64,1280]{1,0:T(8,128)(2,1)S(1)} collective-permute-done((bf16[64,1280]{1,0:T(8,128)(2,1)S(1)}, bf16[64,1280]{1,0:T(8,128)(2,1)S(1)}, u32[]{:S(2)}, u32[]{:S(2)}) %collective-permute-start.11) | collective-permute-done | bytes 163872 | tf_op jit(solution)/shard_map/ppermute | solution.py:314
  42.8 3.6 %collective-permute-start.13 = (bf16[16,1280]{1,0:T(8,128)(2,1)S(1)}, bf16[16,1280]{1,0:T(8,128)(2,1)S(1)}, u32[]{:S(2)}, u32[]{:S(2)}) collective-permute-start(bf16[16,1280]{1,0:T(8,128)(2,1)S(1)} %get-tuple-element.39), channel_id=1, source_target_pairs={{0,4},{1,5},{2,6},{3,7},{4,0},{5,1},{6,2},{7,3},{8,12},{9,13},{10,... | collective-permute-start | bytes 122888 | tf_op jit(solution)/shard_map/ppermute | solution.py:317
  47.1 1.5 %copy.40.refs_5_ = bf16[1280,320]{1,0:T(8,128)(2,1)S(1)} copy(bf16[1280,320]{0,1:T(8,128)(2,1)} %param.38) | data formatting | bytes 1638400 | tf_op args[12]
  49.4 1.5 %copy.41.refs_6_ = bf16[1280,320]{1,0:T(8,128)(2,1)S(1)} copy(bf16[1280,320]{0,1:T(8,128)(2,1)} %collective-permute-done.18) | data formatting | bytes 1638400 | tf_op jit(solution)/shard_map/ppermute | solution.py:314
  51.4 0.8 %collective-permute-start.17 = (bf16[16,1280]{1,0:T(8,128)(2,1)S(1)}, bf16[16,1280]{1,0:T(8,128)(2,1)S(1)}, u32[]{:S(2)}, u32[]{:S(2)}) collective-permute-start(bf16[16,1280]{1,0:T(8,128)(2,1)S(1)} %shard_map.277.refs_0_), channel_id=1, source_target_pairs={{0,6},{1,7},{2,0},{3,1},{4,2},{5,3},{6,4},{7,5},{8,14},{9,15},{10,... | collective-permute-start | bytes 122888 | tf_op jit(solution)/shard_map/ppermute | solution.py:317
  52.2 2.0 %collective-permute-start.16 = (bf16[16,1280]{1,0:T(8,128)(2,1)S(1)}, bf16[16,1280]{1,0:T(8,128)(2,1)S(1)}, u32[]{:S(2)}, u32[]{:S(2)}) collective-permute-start(bf16[16,1280]{1,0:T(8,128)(2,1)S(1)} %shard_map.277.refs_0_), channel_id=1, source_target_pairs={{0,4},{1,5},{2,6},{3,7},{4,0},{5,1},{6,2},{7,3},{8,12},{9,13},{10,... | collective-permute-start | bytes 122888 | tf_op jit(solution)/shard_map/ppermute | solution.py:317
  56.2 2.9 %collective-permute-done.15.refs_1_ = bf16[16,1280]{1,0:T(8,128)(2,1)S(1)} collective-permute-done((bf16[16,1280]{1,0:T(8,128)(2,1)S(1)}, bf16[16,1280]{1,0:T(8,128)(2,1)S(1)}, u32[]{:S(2)}, u32[]{:S(2)}) %collective-permute-start.15) | collective-permute-done | bytes 40992 | tf_op jit(solution)/shard_map/ppermute | solution.py:317
  59.2 1.0 %shard_map.278 = (bf16[16,768]{1,0:T(8,128)(2,1)S(1)}, bf16[16,768]{1,0:T(8,128)(2,1)S(1)}, bf16[16,768]{1,0:T(8,128)(2,1)S(1)}, bf16[16,768]{1,0:T(8,128)(2,1)S(1)}) custom-call(s32[5]{0:T(128)S(1)} %stack.23.scalar, bf16[16,1280]{1,0:T(8,128)(2,1)S(1)} %shard_map.277.refs_0_, bf16[16,1280]{1,0:T(8,128)(2,1)S(1)} %collective-permute-done.15.refs_1_, ...), custom_call_target="tpu_custom_call" | custom-call | flops 104857600 | bytes 1638400 | tf_op jit(solution)/shard_map/pallas_call | solution.py:29
  60.9 4.3 %collective-permute-start.20 = (bf16[16,768]{1,0:T(8,128)(2,1)S(1)}, bf16[16,768]{1,0:T(8,128)(2,1)S(1)}, u32[]{:S(2)}, u32[]{:S(2)}) collective-permute-start(bf16[16,768]{1,0:T(8,128)(2,1)S(1)} %get-tuple-element.33), channel_id=1, source_target_pairs={{0,2},{1,3},{2,10},{3,11},{4,18},{5,19},{6,26},{7,27},{8,4},{9,5},... | collective-permute-start | bytes 73736 | tf_op jit(solution)/shard_map/ppermute | solution.py:425
  65.2 1.8 %collective-permute-start.21 = (bf16[16,768]{1,0:T(8,128)(2,1)S(1)}, bf16[16,768]{1,0:T(8,128)(2,1)S(1)}, u32[]{:S(2)}, u32[]{:S(2)}) collective-permute-start(bf16[16,768]{1,0:T(8,128)(2,1)S(1)} %get-tuple-element.34), channel_id=1, source_target_pairs={{0,4},{1,5},{2,12},{3,13},{4,20},{5,21},{6,28},{7,29},{8,6},{9,7},... | collective-permute-start | bytes 73736 | tf_op jit(solution)/shard_map/ppermute | solution.py:425
  67.0 1.6 %collective-permute-start.22 = (bf16[16,768]{1,0:T(8,128)(2,1)S(1)}, bf16[16,768]{1,0:T(8,128)(2,1)S(1)}, u32[]{:S(2)}, u32[]{:S(2)}) collective-permute-start(bf16[16,768]{1,0:T(8,128)(2,1)S(1)} %get-tuple-element.35), channel_id=1, source_target_pairs={{0,6},{1,7},{2,14},{3,15},{4,22},{5,23},{6,30},{7,31},{8,0},{9,1},... | collective-permute-start | bytes 73736 | tf_op jit(solution)/shard_map/ppermute | solution.py:425
  69.2 1.4 %shard_map.280 = f32[20,64,128]{2,1,0:T(8,128)} custom-call(s32[1]{0:T(128)} %copy.42.accepted, f32[64,256]{1,0:T(8,128)S(1)} %get-tuple-element.25.own_ref.packed, f32[16,20]{1,0:T(8,128)S(1)} %get-tuple-element.30.dtime_ref, bf16[16,1280]{1,0:T(8,128)(2,1)S(1)} %get-tuple-element.28.x_act, bf16[16,256]{1,0:T(8,128)(2,1)S(1)} %get-tuple-element.29.bc_act, ...), custom_call_target="tpu_custom_call" | custom-call | flops 10485760 | bytes 1310720 | tf_op jit(solution)/shard_map/pallas_call | solution.py:29
  70.6 1.9 %collective-permute-done.21.refs_2_ = bf16[16,768]{1,0:T(8,128)(2,1)S(1)} collective-permute-done((bf16[16,768]{1,0:T(8,128)(2,1)S(1)}, bf16[16,768]{1,0:T(8,128)(2,1)S(1)}, u32[]{:S(2)}, u32[]{:S(2)}) %collective-permute-start.21) | collective-permute-done | bytes 24608 | tf_op jit(solution)/shard_map/ppermute | solution.py:425
  72.6 0.8 %shard_map.279 = bf16[16,640]{1,0:T(8,128)(2,1)} custom-call(bf16[16,768]{1,0:T(8,128)(2,1)S(1)} %collective-permute-done.19.refs_0_, bf16[16,768]{1,0:T(8,128)(2,1)S(1)} %collective-permute-done.20.refs_1_, bf16[16,768]{1,0:T(8,128)(2,1)S(1)} %collective-permute-done.21.refs_2_, bf16[16,768]{1,0:T(8,128)(2,1)S(1)} %collective-permute-done.22.refs_3_), custom_call_target="tpu_custom_call" | custom-call | flops 51200 | bytes 51200 | tf_op jit(solution)/shard_map/pallas_call | solution.py:29
  (77 shorter events, 14.2 us)
Async XLA Ops:
  0.6 10.0 %copy-start = (s32[8]{0:T(128)S(1)}, s32[8]{0:T(128)}, u32[]{:S(2)}) copy-start(s32[8]{0:T(128)} %param.49) | copy-start | bytes 100
  0.6 32.2 %copy-start.5 = (bf16[10,256,128]{2,1,0:T(8,128)(2,1)S(1)}, bf16[10,256,128]{2,1,0:T(8,128)(2,1)}, u32[]{:S(2)}) copy-start(bf16[10,256,128]{2,1,0:T(8,128)(2,1)} %b_ref.1) | copy-start | bytes 1966084
  0.7 13.1 %collective-permute-start.3 = (bf16[320,1280]{1,0:T(8,128)(2,1)}, bf16[320,1280]{1,0:T(8,128)(2,1)S(1)}, u32[]{:S(2)}, u32[]{:S(2)}) collective-permute-start(bf16[320,1280]{1,0:T(8,128)(2,1)} %refs_4_.1), channel_id=1, source_target_pairs={{0,1},{1,0},{2,3},{3,2},{4,5},{5,4},{6,7},{7,6},{8,9},{9,8},{10,11... | collective-permute-start | bytes 2457608 | tf_op jit(solution)/shard_map/ppermute | solution.py:314
  1.2 12.6 %collective-permute-start.4 = (bf16[320,1280]{1,0:T(8,128)(2,1)}, bf16[320,1280]{1,0:T(8,128)(2,1)S(1)}, u32[]{:S(2)}, u32[]{:S(2)}) collective-permute-start(bf16[320,1280]{1,0:T(8,128)(2,1)} %refs_6_.1), channel_id=1, source_target_pairs={{0,1},{1,0},{2,3},{3,2},{4,5},{5,4},{6,7},{7,6},{8,9},{9,8},{10,11... | collective-permute-start | bytes 2457608 | tf_op jit(solution)/shard_map/ppermute | solution.py:314
  2.7 6.1 %collective-permute-start.2 = (bf16[32,640]{1,0:T(8,128)(2,1)S(1)}, bf16[32,640]{1,0:T(8,128)(2,1)S(1)}, u32[]{:S(2)}, u32[]{:S(2)}) collective-permute-start(bf16[32,640]{1,0:T(8,128)(2,1)S(1)} %get-tuple-element.46), channel_id=1, source_target_pairs={{0,6},{1,7},{2,0},{3,1},{4,2},{5,3},{6,4},{7,5},{8,14},{9,15},{10,... | collective-permute-start | bytes 122888 | tf_op jit(solution)/shard_map/ppermute | solution.py:317
  7.5 1.3 %collective-permute-start.6 = (bf16[320,20]{1,0:T(8,128)(2,1)S(1)}, bf16[320,20]{1,0:T(8,128)(2,1)S(1)}, u32[]{:S(2)}, u32[]{:S(2)}) collective-permute-start(bf16[320,20]{1,0:T(8,128)(2,1)S(1)} %copy.39.refs_10_), channel_id=1, source_target_pairs={{0,1},{1,0},{2,3},{3,2},{4,5},{5,4},{6,7},{7,6},{8,9},{9,8},{10,11... | collective-permute-start | bytes 38408 | tf_op jit(solution)/shard_map/ppermute | solution.py:314
  7.6 6.2 %collective-permute-start.5 = (bf16[320,256]{1,0:T(8,128)(2,1)}, bf16[320,256]{1,0:T(8,128)(2,1)S(1)}, u32[]{:S(2)}, u32[]{:S(2)}) collective-permute-start(bf16[320,256]{1,0:T(8,128)(2,1)} %refs_8_.1), channel_id=1, source_target_pairs={{0,1},{1,0},{2,3},{3,2},{4,5},{5,4},{6,7},{7,6},{8,9},{9,8},{10,11... | collective-permute-start | bytes 491528 | tf_op jit(solution)/shard_map/ppermute | solution.py:314
  8.9 4.9 %collective-permute-start = (bf16[32,640]{1,0:T(8,128)(2,1)S(1)}, bf16[32,640]{1,0:T(8,128)(2,1)S(1)}, u32[]{:S(2)}, u32[]{:S(2)}) collective-permute-start(bf16[32,640]{1,0:T(8,128)(2,1)S(1)} %get-tuple-element.48), channel_id=1, source_target_pairs={{0,2},{1,3},{2,4},{3,5},{4,6},{5,7},{6,0},{7,1},{8,10},{9,11},{10,... | collective-permute-start | bytes 122888 | tf_op jit(solution)/shard_map/ppermute | solution.py:317
  8.9 4.9 %collective-permute-start.1 = (bf16[32,640]{1,0:T(8,128)(2,1)S(1)}, bf16[32,640]{1,0:T(8,128)(2,1)S(1)}, u32[]{:S(2)}, u32[]{:S(2)}) collective-permute-start(bf16[32,640]{1,0:T(8,128)(2,1)S(1)} %get-tuple-element.49), channel_id=1, source_target_pairs={{0,4},{1,5},{2,6},{3,7},{4,0},{5,1},{6,2},{7,3},{8,12},{9,13},{10,... | collective-permute-start | bytes 122888 | tf_op jit(solution)/shard_map/ppermute | solution.py:317
  17.0 32.3 %copy-start.17 = (bf16[1280]{0:T(1024)(128)(2,1)S(1)}, bf16[1280]{0:T(1024)(128)(2,1)}, u32[]{:S(2)}) copy-start(bf16[1280]{0:T(1024)(128)(2,1)} %param.37) | copy-start | bytes 7684
  18.0 33.0 %copy-start.10 = (bf16[1,4,1280]{2,1,0:T(4,128)(2,1)S(1)}, bf16[1,4,1280]{2,1,0:T(4,128)(2,1)}, u32[]{:S(2)}) copy-start(bf16[1,4,1280]{2,1,0:T(4,128)(2,1)} %param.42) | copy-start | bytes 30724
  18.0 33.0 %copy-start.13 = (bf16[1,4,128]{2,1,0:T(4,128)(2,1)S(1)}, bf16[1,4,128]{2,1,0:T(4,128)(2,1)}, u32[]{:S(2)}) copy-start(bf16[1,4,128]{2,1,0:T(4,128)(2,1)} %param.43) | copy-start | bytes 3076
  18.0 5.9 %collective-permute-start.7 = (bf16[16,4096]{1,0:T(8,128)(2,1)S(1)}, bf16[16,4096]{1,0:T(8,128)(2,1)S(1)}, u32[]{:S(2)}, u32[]{:S(2)}) collective-permute-start(bf16[16,4096]{1,0:T(8,128)(2,1)S(1)} %get-tuple-element.22), channel_id=1, source_target_pairs={{0,6},{1,7},{2,0},{3,1},{4,2},{5,3},{6,4},{7,5},{8,14},{9,15},{10,... | collective-permute-start | bytes 393224 | tf_op jit(solution)/shard_map/ppermute | solution.py:317
  20.1 7.8 %collective-permute-start.8 = (bf16[16,4096]{1,0:T(8,128)(2,1)S(1)}, bf16[16,4096]{1,0:T(8,128)(2,1)S(1)}, u32[]{:S(2)}, u32[]{:S(2)}) collective-permute-start(bf16[16,4096]{1,0:T(8,128)(2,1)S(1)} %get-tuple-element.23), channel_id=1, source_target_pairs={{0,4},{1,5},{2,6},{3,7},{4,0},{5,1},{6,2},{7,3},{8,12},{9,13},{10,... | collective-permute-start | bytes 393224 | tf_op jit(solution)/shard_map/ppermute | solution.py:317
  21.5 6.4 %collective-permute-start.9 = (bf16[16,4096]{1,0:T(8,128)(2,1)S(1)}, bf16[16,4096]{1,0:T(8,128)(2,1)S(1)}, u32[]{:S(2)}, u32[]{:S(2)}) collective-permute-start(bf16[16,4096]{1,0:T(8,128)(2,1)S(1)} %get-tuple-element.24), channel_id=1, source_target_pairs={{0,2},{1,3},{2,4},{3,5},{4,6},{5,7},{6,0},{7,1},{8,10},{9,11},{10,... | collective-permute-start | bytes 393224 | tf_op jit(solution)/shard_map/ppermute | solution.py:317
  31.3 23.0 %copy-start.9 = (bf16[1,3,1280]{2,1,0:T(4,128)(2,1)S(1)}, bf16[1,3,1280]{2,1,0:T(4,128)(2,1)}, u32[]{:S(2)}) copy-start(bf16[1,3,1280]{2,1,0:T(4,128)(2,1)} %param.39) | copy-start | bytes 23044
  31.6 1.3 %collective-permute-start.10 = (f32[64,256]{1,0:T(8,128)S(1)}, f32[64,256]{1,0:T(8,128)S(1)}, u32[]{:S(2)}, u32[]{:S(2)}) collective-permute-start(f32[64,256]{1,0:T(8,128)S(1)} %get-tuple-element.25.own_ref.packed), channel_id=1, source_target_pairs={{0,1},{1,0},{2,3},{3,2},{4,5},{5,4},{6,7},{7,6},{8,9},{9,8},{10,11... | collective-permute-start | bytes 196616 | tf_op jit(solution)/shard_map/ppermute | solution.py:314
  32.9 2.9 %copy-start.1 = (bf16[10,256,1280]{2,1,0:T(8,128)(2,1)S(1)}, bf16[10,256,1280]{2,1,0:T(8,128)(2,1)}, u32[]{:S(2)}) copy-start(bf16[10,256,1280]{2,1,0:T(8,128)(2,1)} %x_hbm.1) | copy-start | bytes 19660804
  36.7 31.9 %copy-start.16 = (bf16[1,3,256]{2,1,0:T(4,128)(2,1)S(1)}, bf16[1,3,256]{2,1,0:T(4,128)(2,1)}, u32[]{:S(2)}) copy-start(bf16[1,3,256]{2,1,0:T(4,128)(2,1)} %param.40) | copy-start | bytes 4612
  36.7 32.5 %copy-start.4 = (f32[1,20,64,128]{3,2,1,0:T(8,128)S(1)}, f32[1,20,64,128]{3,2,1,0:T(8,128)}, u32[]{:S(2)}) copy-start(f32[1,20,64,128]{3,2,1,0:T(8,128)} %param.41) | copy-start | bytes 1966084
  40.2 2.5 %collective-permute-start.11 = (bf16[64,1280]{1,0:T(8,128)(2,1)S(1)}, bf16[64,1280]{1,0:T(8,128)(2,1)S(1)}, u32[]{:S(2)}, u32[]{:S(2)}) collective-permute-start(bf16[64,1280]{1,0:T(8,128)(2,1)S(1)} %get-tuple-element.27), channel_id=1, source_target_pairs={{0,1},{1,0},{2,3},{3,2},{4,5},{5,4},{6,7},{7,6},{8,9},{9,8},{10,11... | collective-permute-start | bytes 491528 | tf_op jit(solution)/shard_map/ppermute | solution.py:314
  41.6 7.8 %collective-permute-start.18 = (bf16[1280,320]{0,1:T(8,128)(2,1)}, bf16[1280,320]{0,1:T(8,128)(2,1)}, u32[]{:S(2)}, u32[]{:S(2)}) collective-permute-start(bf16[1280,320]{0,1:T(8,128)(2,1)} %param.38), channel_id=1, source_target_pairs={{0,1},{1,0},{2,3},{3,2},{4,5},{5,4},{6,7},{7,6},{8,9},{9,8},{10,11... | collective-permute-start | bytes 2457608 | tf_op jit(solution)/shard_map/ppermute | solution.py:314
  42.7 8.6 %collective-permute-start.14 = (bf16[16,1280]{1,0:T(8,128)(2,1)S(1)}, bf16[16,1280]{1,0:T(8,128)(2,1)S(1)}, u32[]{:S(2)}, u32[]{:S(2)}) collective-permute-start(bf16[16,1280]{1,0:T(8,128)(2,1)S(1)} %get-tuple-element.38), channel_id=1, source_target_pairs={{0,2},{1,3},{2,4},{3,5},{4,6},{5,7},{6,0},{7,1},{8,10},{9,11},{10,... | collective-permute-start | bytes 122888 | tf_op jit(solution)/shard_map/ppermute | solution.py:317
  42.8 8.5 %collective-permute-start.13 = (bf16[16,1280]{1,0:T(8,128)(2,1)S(1)}, bf16[16,1280]{1,0:T(8,128)(2,1)S(1)}, u32[]{:S(2)}, u32[]{:S(2)}) collective-permute-start(bf16[16,1280]{1,0:T(8,128)(2,1)S(1)} %get-tuple-element.39), channel_id=1, source_target_pairs={{0,4},{1,5},{2,6},{3,7},{4,0},{5,1},{6,2},{7,3},{8,12},{9,13},{10,... | collective-permute-start | bytes 122888 | tf_op jit(solution)/shard_map/ppermute | solution.py:317
  46.4 5.0 %collective-permute-start.12 = (bf16[16,1280]{1,0:T(8,128)(2,1)S(1)}, bf16[16,1280]{1,0:T(8,128)(2,1)S(1)}, u32[]{:S(2)}, u32[]{:S(2)}) collective-permute-start(bf16[16,1280]{1,0:T(8,128)(2,1)S(1)} %get-tuple-element.40), channel_id=1, source_target_pairs={{0,6},{1,7},{2,0},{3,1},{4,2},{5,3},{6,4},{7,5},{8,14},{9,15},{10,... | collective-permute-start | bytes 122888 | tf_op jit(solution)/shard_map/ppermute | solution.py:317
  51.4 4.2 %collective-permute-start.17 = (bf16[16,1280]{1,0:T(8,128)(2,1)S(1)}, bf16[16,1280]{1,0:T(8,128)(2,1)S(1)}, u32[]{:S(2)}, u32[]{:S(2)}) collective-permute-start(bf16[16,1280]{1,0:T(8,128)(2,1)S(1)} %shard_map.277.refs_0_), channel_id=1, source_target_pairs={{0,6},{1,7},{2,0},{3,1},{4,2},{5,3},{6,4},{7,5},{8,14},{9,15},{10,... | collective-permute-start | bytes 122888 | tf_op jit(solution)/shard_map/ppermute | solution.py:317
  52.2 4.0 %collective-permute-start.16 = (bf16[16,1280]{1,0:T(8,128)(2,1)S(1)}, bf16[16,1280]{1,0:T(8,128)(2,1)S(1)}, u32[]{:S(2)}, u32[]{:S(2)}) collective-permute-start(bf16[16,1280]{1,0:T(8,128)(2,1)S(1)} %shard_map.277.refs_0_), channel_id=1, source_target_pairs={{0,4},{1,5},{2,6},{3,7},{4,0},{5,1},{6,2},{7,3},{8,12},{9,13},{10,... | collective-permute-start | bytes 122888 | tf_op jit(solution)/shard_map/ppermute | solution.py:317
  54.3 4.9 %collective-permute-start.15 = (bf16[16,1280]{1,0:T(8,128)(2,1)S(1)}, bf16[16,1280]{1,0:T(8,128)(2,1)S(1)}, u32[]{:S(2)}, u32[]{:S(2)}) collective-permute-start(bf16[16,1280]{1,0:T(8,128)(2,1)S(1)} %shard_map.277.refs_0_), channel_id=1, source_target_pairs={{0,2},{1,3},{2,4},{3,5},{4,6},{5,7},{6,0},{7,1},{8,10},{9,11},{10,... | collective-permute-start | bytes 122888 | tf_op jit(solution)/shard_map/ppermute | solution.py:317
  60.2 10.4 %collective-permute-start.19 = (bf16[16,768]{1,0:T(8,128)(2,1)S(1)}, bf16[16,768]{1,0:T(8,128)(2,1)S(1)}, u32[]{:S(2)}, u32[]{:S(2)}) collective-permute-start(bf16[16,768]{1,0:T(8,128)(2,1)S(1)} %get-tuple-element.32), channel_id=1, source_target_pairs={{0,0},{1,1},{2,8},{3,9},{4,16},{5,17},{6,24},{7,25},{8,2},{9,3},{1... | collective-permute-start | bytes 73736 | tf_op jit(solution)/shard_map/ppermute | solution.py:425
  60.9 9.8 %collective-permute-start.20 = (bf16[16,768]{1,0:T(8,128)(2,1)S(1)}, bf16[16,768]{1,0:T(8,128)(2,1)S(1)}, u32[]{:S(2)}, u32[]{:S(2)}) collective-permute-start(bf16[16,768]{1,0:T(8,128)(2,1)S(1)} %get-tuple-element.33), channel_id=1, source_target_pairs={{0,2},{1,3},{2,10},{3,11},{4,18},{5,19},{6,26},{7,27},{8,4},{9,5},... | collective-permute-start | bytes 73736 | tf_op jit(solution)/shard_map/ppermute | solution.py:425
  65.2 7.4 %collective-permute-start.21 = (bf16[16,768]{1,0:T(8,128)(2,1)S(1)}, bf16[16,768]{1,0:T(8,128)(2,1)S(1)}, u32[]{:S(2)}, u32[]{:S(2)}) collective-permute-start(bf16[16,768]{1,0:T(8,128)(2,1)S(1)} %get-tuple-element.34), channel_id=1, source_target_pairs={{0,4},{1,5},{2,12},{3,13},{4,20},{5,21},{6,28},{7,29},{8,6},{9,7},... | collective-permute-start | bytes 73736 | tf_op jit(solution)/shard_map/ppermute | solution.py:425
  67.0 5.6 %collective-permute-start.22 = (bf16[16,768]{1,0:T(8,128)(2,1)S(1)}, bf16[16,768]{1,0:T(8,128)(2,1)S(1)}, u32[]{:S(2)}, u32[]{:S(2)}) collective-permute-start(bf16[16,768]{1,0:T(8,128)(2,1)S(1)} %get-tuple-element.35), channel_id=1, source_target_pairs={{0,6},{1,7},{2,14},{3,15},{4,22},{5,23},{6,30},{7,31},{8,0},{9,1},... | collective-permute-start | bytes 73736 | tf_op jit(solution)/shard_map/ppermute | solution.py:425
  (9 other events, 7.6 us)

commit v2 on v1

v2 whole, which is shorter than its diff:
```python
import functools

import jax
import jax.numpy as jnp
from jax import lax
from jax.experimental import pallas as pl
from jax.experimental.pallas import tpu as pltpu
from jax.sharding import PartitionSpec as P

HD = 64
NS = 128
KC = 4
EPSILON = 1e-05
BF = jnp.bfloat16
F32 = jnp.float32
VMEM_LIMIT = 20 * 1024 * 1024
BCW = 3 * NS


def vmem():
    return pl.BlockSpec(memory_space=pltpu.VMEM)


def smem():
    return pl.BlockSpec(memory_space=pltpu.SMEM)


def call(body, out_shape, in_specs, *args, flops=0, nbytes=0, scratch=()):
    return pl.pallas_call(
        body,
        out_shape=out_shape,
        in_specs=in_specs,
        out_specs=jax.tree.map(lambda _: vmem(), out_shape),
        scratch_shapes=list(scratch),
        compiler_params=pltpu.CompilerParams(vmem_limit_bytes=VMEM_LIMIT),
        cost_estimate=pl.CostEstimate(flops=flops, bytes_accessed=nbytes, transcendentals=0),
    )(*args)


def hbm():
    return pl.BlockSpec(memory_space=pltpu.HBM)


def in_hbm(v):
    return pltpu.with_memory_space_constraint(v, pltpu.HBM)


def sds(shape, dtype):
    return jax.ShapeDtypeStruct(shape, dtype)


def silu(v):
    return v / (1.0 + jnp.exp(-v))


def softplus(v):
    return jnp.maximum(v, 0.0) + jnp.log1p(jnp.exp(-jnp.abs(v)))


def conv(history, fresh, taps, offset):
    length = fresh.shape[0]
    joined = jnp.concatenate([history, fresh], axis=0)
    total = offset + taps[0:1] * joined[0:length]
    for k in range(1, KC):
        total = total + taps[k : k + 1] * joined[k : k + length]
    return silu(total)


def running_sum(v):
    length = v.shape[0]
    step = 1
    while step < length:
        v = v + jnp.concatenate([jnp.zeros((step, v.shape[1]), v.dtype), v[: length - step]], axis=0)
        step *= 2
    return v


def head_diag(weights, values):
    heads = len(weights)
    length = weights[0].shape[0]
    if heads == 1:
        return jnp.dot(weights[0], values, preferred_element_type=F32)
    full = jnp.dot(jnp.concatenate(weights, axis=0), values, preferred_element_type=F32)
    owner = lax.broadcasted_iota(jnp.int32, (length, heads * HD), 1) // HD
    out = jnp.where(owner == 0, full[:length], 0.0)
    for i in range(1, heads):
        out = jnp.where(owner == i, full[i * length : (i + 1) * length], out)
    return out


def draft_kernel(fan, share, drafts_hbm, history_hbm, bc_hbm, dt_hbm, x_hbm, z_hbm, out_hbm, *refs):
    outs, (narrow_out, xz_out, drafts, history, steps, sems) = refs[:fan], refs[fan:]
    half, heads = bc_hbm.shape[0], steps.shape[0]
    copies = [
        pltpu.make_async_copy(source, target, sems.at[i])
        for i, (source, target) in enumerate(
            (
                (drafts_hbm, drafts), (history_hbm, history), (dt_hbm, steps),
                (bc_hbm, narrow_out.at[0:half, 0 : 2 * NS]),
                (x_hbm, xz_out.at[0:half]), (z_hbm, xz_out.at[half : 2 * half]),
                (out_hbm, xz_out.at[2 * half : 3 * half]),
            )
        )
    ]
    for c in copies:
        c.start()
    for out in outs:
        out[...] = jnp.zeros_like(out)
    for c in copies[:4]:
        c.wait()
    narrow_out[half : half + heads, :half] = steps[...]
    length = drafts.shape[1]
    pair = lax.axis_index("req") // 2
    past = history[0].astype(F32)
    past = jnp.concatenate([past, jnp.zeros((length - past.shape[0], past.shape[1]), F32)], axis=0)
    if share % 128:
        width = drafts.shape[2]
        whole = pltpu.roll(drafts[0].astype(F32), width - pair * share, 1)
    for s, out in enumerate(outs):
        if share % 128:
            piece = whole[:, s * share : (s + 1) * share].astype(BF)
        else:
            start = pl.multiple_of(((pair + s) % fan) * share, 128)
            piece = drafts[0, :, pl.ds(start, share)]
        out[0:length, :share] = piece
        out[length : 2 * length, : 2 * NS] = past.astype(BF)
    for c in copies[4:]:
        c.wait()


def stage_kernel(count, *refs):
    outs, sems = refs[-1 - count : -1], refs[-1]
    copies = [pltpu.make_async_copy(refs[i], outs[i], sems.at[i]) for i in range(count)]
    for c in copies:
        c.start()
    for c in copies:
        c.wait()


def stage(arrays, after):
    return call(
        functools.partial(stage_kernel, len(arrays)),
        [sds(v.shape, v.dtype) for v in arrays],
        [hbm()] * len(arrays) + [pl.BlockSpec(memory_space=pl.ANY)],
        *[in_hbm(v) for v in arrays], after,
        flops=0, nbytes=sum(2 * v.size for v in arrays),
        scratch=[pltpu.SemaphoreType.DMA((len(arrays),))],
    )


def own_and_other(length, half, blocks):
    tokens = jnp.concatenate([b[0:length, : 2 * half] for b in blocks], axis=0)
    first = lax.axis_index("req") % 2 == 0
    low, high = tokens[:, :half], tokens[:, half:]
    return jnp.where(first, low, high), jnp.where(first, high, low)


def project_bc_kernel(length, fan, half, heads, *refs):
    blocks = refs[:fan]
    mine, theirs, out = refs[fan:]
    own, other = own_and_other(length, half, blocks)
    bc = jnp.dot(own, mine[:half, : 2 * NS], preferred_element_type=F32) + jnp.dot(
        other, theirs[:half, : 2 * NS], preferred_element_type=F32
    )
    turned = (((1,), (1,)), ((), ()))
    rows = slice(half, half + heads)
    dt = lax.dot_general(
        own, mine[rows, :half], turned, preferred_element_type=F32
    ) + lax.dot_general(other, theirs[rows, :half], turned, preferred_element_type=F32)
    dt_hi = dt.astype(BF)
    dt_lo = (dt - dt_hi.astype(F32)).astype(BF)
    out[...] = jnp.concatenate(
        [bc.astype(BF), dt_hi, dt_lo, jnp.zeros((fan * length, NS - 2 * heads), BF)], axis=1
    )


def project_xz_kernel(length, fan, *refs):
    blocks = refs[:fan]
    mine, theirs = refs[fan : fan + 2]
    outs = refs[fan + 2 :]
    half, inner = mine.shape[0] // 3, mine.shape[1]
    own, other = own_and_other(length, half, blocks)
    for i in range(2):
        rows = slice(i * half, (i + 1) * half)
        v = jnp.dot(own, mine[rows], preferred_element_type=F32) + jnp.dot(
            other, theirs[rows], preferred_element_type=F32
        )
        v = v.astype(BF)
        for s, out in enumerate(outs):
            out[:, i * inner : (i + 1) * inner] = v[s * length : (s + 1) * length]


def mix_bc_kernel(length, fan, heads, *refs):
    parts = refs[:fan]
    blocks = refs[fan : 2 * fan]
    taps_ref, offset_ref, bias_ref, rate_ref = refs[2 * fan : 2 * fan + 4]
    packed, bc_raw_o, bc_act_o, dtime_o = refs[2 * fan + 5 :]
    taps, offset = taps_ref[...].astype(F32), offset_ref[...].astype(F32)[None]
    dt_bias, rate = bias_ref[...][None], rate_ref[...][None]
    for t in range(fan):
        acc = None
        for s in range(fan):
            first = length * ((t + s) % fan)
            piece = parts[s][first : first + length].astype(F32)
            acc = piece if acc is None else acc + piece
        bc_raw = acc[:, : 2 * NS].astype(BF)
        dt = acc[:, 2 * NS : 2 * NS + heads] + acc[:, 2 * NS + heads : 2 * NS + 2 * heads]
        history = blocks[t][length : 2 * length, : 2 * NS].astype(F32)[: KC - 1]
        bc_act = conv(history, bc_raw.astype(F32), taps, offset).astype(BF)
        dtime = softplus(dt + dt_bias)
        cumul = running_sum(-rate * dtime)
        packed[t * length : (t + 1) * length, :NS] = bc_act[:, NS:].astype(F32)
        packed[t * length : (t + 1) * length, NS:] = jnp.concatenate(
            [cumul, jnp.zeros((length, NS - heads), F32)], axis=1
        )
        if t == 0:
            bc_raw_o[...] = bc_raw
            bc_act_o[...] = bc_act
            dtime_o[...] = dtime


def page_kernel(
    length, heads, slot_req, slot_page, page_count, owner_row,
    own_ref, other_ref, b_ref, decay_ref, x_hbm, total,
    query, pages, order, scores_ref, sems,
):
    slots = x_hbm.shape[0]
    half = own_ref.shape[0]
    fan = half // length
    me = lax.axis_index("req")

    def request(s):
        return jnp.maximum(slot_req[s], 0)

    def copy(s):
        return pltpu.make_async_copy(x_hbm.at[s], pages.at[s], sems.at[s])

    def place(s):
        row = owner_row[request(s)]
        away = jnp.where(row % 2 == me % 2, 0, fan)
        return (away + (me // 2 - row // 2 + fan) % fan) * length

    count = jnp.int32(0)
    for s in range(slots):
        live = (slot_req[s] >= 0) & (slot_page[s] < page_count[request(s)])

        @pl.when(live)
        def _():
            copy(s).start()
            order[count] = s

        count = count + live.astype(jnp.int32)

    query[0:half] = own_ref[...]
    query[half:] = other_ref[...]
    total[...] = jnp.zeros_like(total)
    for s in range(slots):
        at = pl.ds(pl.multiple_of(place(s), length), length)
        scores_ref[s] = lax.dot_general(
            query[at, :NS].astype(BF), b_ref[s], (((1,), (1,)), ((), ())),
            preferred_element_type=F32,
        )

    def visit(s):
        rows = pl.ds(pl.multiple_of(place(s), length), length)
        scores = scores_ref[s]
        cumul = query[rows, NS:]
        decay = decay_ref[s]
        terms = []
        for first in range(0, heads, 4):
            last = min(first + 4, heads)
            weights = [
                (scores * jnp.exp(cumul[:, h : h + 1] - decay[h : h + 1, :])).astype(BF)
                for h in range(first, last)
            ]
            terms.append(head_diag(weights, pages[s, :, first * HD : last * HD]))
        return rows, terms

    def add(rows, terms):
        first = 0
        for term in terms:
            cols = slice(first, first + term.shape[1])
            total[rows, cols] += term
            first += term.shape[1]

    def two(i, carry):
        one, other = order[2 * i], order[2 * i + 1]
        copy(one).wait()
        copy(other).wait()
        first, second = visit(one), visit(other)
        add(*first)
        add(*second)
        return carry

    lax.fori_loop(0, count // 2, two, 0)

    @pl.when(count % 2 == 1)
    def _():
        s = order[count - 1]
        copy(s).wait()
        add(*visit(s))


def halve_kernel(total, *refs):
    mine, other = refs[-2:]
    half = mine.shape[0]
    mine[...] = total[0:half].astype(BF)
    other[...] = total[half:].astype(BF)


def join_kernel(length, mine, other, _, *outs):
    for s, out in enumerate(outs):
        rows = slice(s * length, (s + 1) * length)
        out[...] = (mine[rows].astype(F32) + other[rows].astype(F32)).astype(BF)


def local_kernel(length, fan, heads, *refs):
    parts = refs[:fan]
    packed, bc_act, dtime_ref, taps, offset, history, sink_x, sink_b = refs[fan : fan + 8]
    out, x_raw_o, x_act_o, silu_z_o = refs[fan + 8 :]
    inner_cols = out.shape[1]
    acc = parts[0][...].astype(F32)
    for s in range(1, fan):
        acc = acc + parts[s][...].astype(F32)
    x_raw = acc[:, :inner_cols].astype(BF)
    x_raw_o[...] = x_raw
    silu_z_o[...] = silu(acc[:, inner_cols:].astype(BF).astype(F32))
    x_act = conv(
        history[0].astype(F32), x_raw.astype(F32), taps[...].astype(F32),
        offset[...].astype(F32)[None],
    ).astype(BF)
    x_act_o[...] = x_act

    c_mat = bc_act[:, NS:]
    b_mat = bc_act[:, :NS]
    turned = (((1,), (1,)), ((), ()))
    inner = lax.dot_general(c_mat, b_mat, turned, preferred_element_type=F32)
    cumul = packed[0:length, NS:]
    dtime = jnp.concatenate(
        [dtime_ref[...], jnp.zeros((length, NS - heads), F32)], axis=1
    )
    cumul_t = jnp.transpose(cumul)
    dtime_t = jnp.transpose(dtime)
    row = lax.broadcasted_iota(jnp.int32, (length, length), 0)
    col = lax.broadcasted_iota(jnp.int32, (length, length), 1)
    later = row >= col
    sink_values = sink_x[0].astype(F32)
    sink_w = lax.dot_general(
        c_mat, sink_b[0], turned, preferred_element_type=F32
    ).astype(BF).astype(F32)
    for first in range(0, heads, 4):
        last = min(first + 4, heads)
        weights = []
        for h in range(first, last):
            spread = jnp.where(later, cumul[:, h : h + 1] - cumul_t[h : h + 1, :], 0.0)
            weights.append(
                jnp.where(later, inner * jnp.exp(spread) * dtime_t[h : h + 1, :], 0.0).astype(BF)
            )
        cols = slice(first * HD, last * HD)
        acc = head_diag(weights, x_act[:, cols])
        for q in range(sink_values.shape[0]):
            acc = acc + sink_w[:, q : q + 1] * sink_values[q : q + 1, cols]
        out[:, cols] = acc


def state_kernel(length, heads, accepted, packed, dtime_ref, x_act, bc_act, ssm, out):
    cumul = packed[0:length, NS : NS + heads]
    count = accepted[0]
    place = lax.broadcasted_iota(jnp.int32, (length, heads), 0)
    last = jnp.sum(jnp.where(place == count - 1, cumul, 0.0), axis=0, keepdims=True)
    kept = place < count
    coeff = jnp.where(kept, jnp.exp(jnp.where(kept, last - cumul, 0.0)) * dtime_ref[...], 0.0)
    factor = jnp.exp(last)
    b_mat = bc_act[:, :NS]
    twice_b = jnp.concatenate([b_mat, b_mat], axis=0)
    for h in range(heads):
        scaled = x_act[:, h * HD : (h + 1) * HD].astype(F32) * coeff[:, h : h + 1]
        high = scaled.astype(BF)
        low = (scaled - high.astype(F32)).astype(BF)
        fresh = lax.dot_general(
            jnp.concatenate([high, low], axis=0), twice_b,
            (((0,), (0,)), ((), ())), preferred_element_type=F32,
        )
        out[h] = factor[:, h : h + 1] * ssm[h] + fresh


def gate_kernel(fan, *refs):
    parts, local, silu_z, out = refs[:fan], refs[fan], refs[fan + 1], refs[fan + 2]
    acc = local[...]
    for p in parts:
        acc = acc + p[...].astype(F32)
    out[...] = (acc * silu_z[...]).astype(BF)


def out_kernel(length, fan, *refs):
    blocks = refs[:fan]
    gain, mine, theirs = refs[fan : fan + 3]
    outs = refs[fan + 3 : 2 * fan + 3]
    whole = refs[2 * fan + 3]
    cols = mine.shape[0] // 3
    me, zed = lax.axis_index("req"), lax.axis_index("fsdp")
    g = jnp.concatenate([b[...] for b in blocks], axis=0).astype(F32)
    squares = jnp.sum(g * g, axis=1, keepdims=True)
    scaled = (g * gain[...].astype(F32)[None]).astype(BF)
    turned = (((1,), (1,)), ((), ()))
    own = lax.dot_general(scaled, mine[2 * cols :], turned, preferred_element_type=F32)
    other = lax.dot_general(scaled, theirs[2 * cols :], turned, preferred_element_type=F32)
    first = me % 2 == 0
    high = squares.astype(BF).astype(F32)
    low = squares - high
    lane = lax.broadcasted_iota(jnp.int32, (fan * length, NS), 1)
    whole[:, :cols] = jnp.where(first, own, other)
    whole[:, cols : 2 * cols] = jnp.where(first, other, own)
    whole[:, 2 * cols :] = jnp.where(lane == 0, high, jnp.where(lane == 1, low, 0.0))
    for s, out in enumerate(outs):
        block = (me // 2 - zed - s + 2 * fan) % fan
        rows = pl.ds(pl.multiple_of(block * length, length), length)
        out[...] = whole[rows, :].astype(BF)


def final_kernel(width, inner_total, *refs):
    parts, out = refs[:-1], refs[-1]
    acc = parts[0][...].astype(F32)
    for p in parts[1:]:
        acc = acc + p[...].astype(F32)
    squares = acc[:, width : width + 1] + acc[:, width + 1 : width + 2]
    out[...] = (acc[:, :width] * lax.rsqrt(squares / inner_total + EPSILON)).astype(BF)


def per_device(
    reqs, fan,
    drafts, x_weight, z_weight, bc_weight, dt_weight, dt_bias, decay_rate,
    conv_x_weight, conv_x_bias, conv_bc_weight, conv_bc_bias, norm_gain, out_weight,
    conv_x_state, conv_bc_state, ssm_state, sink_x, sink_b, page_x, page_b, page_decay,
    slot_req, slot_page, page_count, accepted, owner_row,
):
    _, length, width = drafts.shape
    inner = x_weight.shape[1]
    heads = dt_weight.shape[1]
    slots = page_x.shape[0]

    def swap(v):
        return lax.ppermute(v, "req", [(j, j ^ 1) for j in range(reqs)])

    def shift(v, step):
        return lax.ppermute(
            v, "req", [(j, 2 * ((j // 2 + step) % fan) + j % 2) for j in range(reqs)]
        )

    share = width // fan
    wide = max(share, 2 * NS)
    dt_turned = dt_weight.T
    half = x_weight.shape[0]
    *blocks, narrow, xz_weight = call(
        functools.partial(draft_kernel, fan, share),
        [sds((2 * length, wide), BF)] * fan
        + [sds((half + 2 * length, max(2 * NS, -(-half // 128) * 128)), BF), sds((3 * half, inner), BF)],
        [hbm()] * 7,
        *[in_hbm(v) for v in (drafts, conv_bc_state, bc_weight, dt_turned, x_weight, z_weight, out_weight.T)],
        flops=10, nbytes=2 * length * width,
        scratch=[
            pltpu.VMEM(drafts.shape, BF), pltpu.VMEM(conv_bc_state.shape, BF),
            pltpu.VMEM(dt_turned.shape, BF), pltpu.SemaphoreType.DMA((7,)),
        ],
    )
    blocks = [blocks[0]] + [shift(blocks[s], s) for s in range(1, fan)]

    xz_other = swap(xz_weight)
    bc_cols = 2 * NS + heads
    bc_part = call(
        functools.partial(project_bc_kernel, length, fan, x_weight.shape[0], heads),
        sds((fan * length, BCW), BF), [vmem()] * (fan + 2),
        *blocks, narrow, swap(narrow),
        flops=2 * fan * length * share * bc_cols, nbytes=2 * share * bc_cols,
    )
    bc_parts = [bc_part] + [shift(bc_part, -s) for s in range(1, fan)]
    (
        bc_taps, bc_offset, step_bias, rate,
        x_taps, x_offset, gain, x_past, sinks_x, sinks_b, page_b_here, page_decay_here, *lists,
    ) = stage(
        (
            conv_bc_weight, conv_bc_bias, dt_bias,
            decay_rate, conv_x_weight, conv_x_bias, norm_gain, conv_x_state, sink_x, sink_b,
            page_b, page_decay, slot_req, slot_page, page_count, owner_row,
        ),
        bc_part,
    )
    xz_parts = call(
        functools.partial(project_xz_kernel, length, fan),
        [sds((length, 2 * inner), BF)] * fan,
        [vmem()] * (fan + 2),
        *blocks, xz_weight, xz_other,
        flops=4 * fan * length * share * inner, nbytes=4 * share * inner,
    )
    xz_parts = [xz_parts[0]] + [shift(xz_parts[s], -s) for s in range(1, fan)]
    packed, bc_raw, bc_act, dtime = call(
        functools.partial(mix_bc_kernel, length, fan, heads),
        [
            sds((fan * length, 2 * NS), F32),
            sds((length, 2 * NS), BF), sds((length, 2 * NS), BF), sds((length, heads), F32),
        ],
        [vmem()] * (2 * fan + 4) + [pl.BlockSpec(memory_space=pl.ANY)],
        *bc_parts, *blocks, bc_taps, bc_offset, step_bias, rate, xz_parts[0],
        flops=100 * length * NS, nbytes=length * NS * 20,
    )
    packed_other = swap(packed)

    total = call(
        functools.partial(page_kernel, length, heads),
        sds((2 * fan * length, inner), F32), [smem()] * 4 + [vmem()] * 4 + [hbm()],
        *lists, packed, packed_other, page_b_here, page_decay_here, in_hbm(page_x),
        flops=8 * slots * length * page_x.shape[1] * inner, nbytes=2 * page_x.size,
        scratch=[
            pltpu.VMEM((2 * fan * length, 2 * NS), F32),
            pltpu.VMEM(page_x.shape, BF),
            pltpu.SMEM((slots,), jnp.int32),
            pltpu.VMEM((slots, length, page_x.shape[1]), F32),
            pltpu.SemaphoreType.DMA((slots,)),
        ],
    )
    mine, others = call(
        halve_kernel, [sds((fan * length, inner), BF)] * 2,
        [vmem()] + [pl.BlockSpec(memory_space=pl.ANY)] * fan, total, *xz_parts,
    )
    others = swap(others)
    local, x_raw, x_act, silu_z = call(
        functools.partial(local_kernel, length, fan, heads),
        [sds((length, inner), F32), sds((length, inner), BF), sds((length, inner), BF), sds((length, inner), F32)],
        [vmem()] * (fan + 8),
        *xz_parts, packed, bc_act, dtime, x_taps, x_offset, x_past, sinks_x, sinks_b,
        flops=40 * length * inner, nbytes=length * inner * 8,
    )
    parts = call(
        functools.partial(join_kernel, length),
        [sds((length, inner), BF)] * fan, [vmem()] * 2 + [pl.BlockSpec(memory_space=pl.ANY)],
        mine, others, local,
        flops=fan * length * inner, nbytes=fan * length * inner * 6,
    )
    parts = [parts[0]] + [shift(parts[s], -s) for s in range(1, fan)]
    gated = call(
        functools.partial(gate_kernel, fan),
        sds((length, inner), BF), [vmem()] * (fan + 2),
        *parts, local, silu_z,
        flops=40 * length * inner, nbytes=length * inner * 8,
    )

    gated_all = [gated] + [shift(gated, s) for s in range(1, fan)]
    new_state = call(
        functools.partial(state_kernel, length, heads),
        sds(ssm_state.shape[1:], F32), [smem()] + [vmem()] * 5,
        accepted, packed, dtime, x_act, bc_act, ssm_state[0],
        flops=64 * inner * NS, nbytes=8 * inner * NS,
    )

    cols = out_weight.shape[1]
    out_shape = sds((length, 2 * cols + NS), BF)
    out_parts = call(
        functools.partial(out_kernel, length, fan),
        [out_shape] * fan, [vmem()] * (fan + 3),
        *gated_all, gain, xz_weight, xz_other,
        flops=4 * fan * length * inner * cols, nbytes=4 * inner * cols,
        scratch=[pltpu.VMEM((fan * length, 2 * cols + NS), F32)],
    )

    def to_owner(v, step):
        moves = [
            (f * reqs + j, (j // 2) * reqs + 2 * ((f + step) % fan) + j % 2)
            for f in range(fan)
            for j in range(reqs)
        ]
        return lax.ppermute(v, ("fsdp", "req"), moves)

    arrived = [to_owner(out_parts[s], s) for s in range(fan)]
    mixed = call(
        functools.partial(final_kernel, 2 * cols, inner * fan),
        sds((length, 2 * cols), BF), [vmem()] * fan, *arrived,
        flops=length * cols * 10, nbytes=length * cols * 10,
    )

    def tail_rows(past, fresh):
        joined = jnp.concatenate([past, fresh], axis=0)
        return lax.dynamic_slice_in_dim(joined, accepted[0], KC - 1, 0)[None]

    return (
        mixed[None],
        new_state[None],
        tail_rows(conv_x_state[0], x_raw),
        tail_rows(conv_bc_state[0], bc_raw),
    )


def solution(mesh):
    in_specs = (
        P("req", None, None),
        P("req", "fsdp"),
        P("req", "fsdp"),
        P("req", None),
        P("req", "fsdp"),
        P("fsdp"),
        P("fsdp"),
        P(None, "fsdp"),
        P("fsdp"),
        P(),
        P(),
        P("fsdp"),
        P("fsdp", "req"),
        P("req", None, "fsdp"),
        P("req", None, None),
        P("req", "fsdp", None, None),
        P("req", None, "fsdp"),
        P("req", None, None),
        P("req", None, "fsdp"),
        P("req", None, None),
        P("req", "fsdp", None),
        P("req"),
        P("req"),
        P(),
        P("req"),
        P(),
    )
    out_specs = (
        P("req", None, "fsdp"),
        P("req", "fsdp", None, None),
        P("req", None, "fsdp"),
        P("req", None, None),
    )
    reqs, fan = mesh.shape["req"], mesh.shape["fsdp"]
    assert reqs == 2 * fan
    return jax.shard_map(
        functools.partial(per_device, reqs, fan),
        mesh=mesh, in_specs=in_specs, out_specs=out_specs, check_vma=False,
    )
```

time: 73 us -> 58.3 us (0.80)
  local copies, waits for them, and re-layouts: 18.6 us -> 2.29 us
  Pallas kernels: 8.32 us -> 11.9 us
  other arithmetic: 3.32 us -> 1.22 us
  waiting for transfers between devices: 14.6 us -> 13.1 us
  starting transfers between devices: 26.9 us -> 28.1 us
    unnamed x38 -> x10, local copies, waits for them, and re-layouts: 12.8 us -> 2.29 us
    pallas_call x7 -> x13, Pallas kernels: 4.85 us -> 11.9 us  [call(): pl.pallas_call(body, out_shape=out_shape, in_specs=in_specs, out_specs=ja...]
    pallas_call x1 -> x0, Pallas kernels: 3.47 us -> none  [per_device(): pl.pallas_call(functools.partial(page_kernel, length, heads), out_shape=[...]
    ppermute x12 -> x15, starting transfers between devices: 15.7 us -> 18.2 us  [shift(): lax.ppermute(v, 'req', [(j, 2 * ((j // 2 + step) % fan) + j % 2) for j in...]
    ppermute x7 -> x4, starting transfers between devices: 2.79 us -> 0.74 us  [swap(): return lax.ppermute(v, 'req', [(j, j ^ 1) for j in range(reqs)])]
    gather x2 -> x0, local copies, waits for them, and re-layouts: 1.98 us -> none  [the longest x1 1.32 us: per_device(): rows = owner_row[guarded]]
    ppermute x1 -> x0, local copies, waits for them, and re-layouts: 1.54 us -> none  [swap(): return lax.ppermute(v, 'req', [(j, j ^ 1) for j in range(reqs)])]
    broadcast_in_dim x3 -> x0, local copies, waits for them, and re-layouts: 1.36 us -> none  [the longest x1 0.7 us: per_device(): conv_x_bias[None]]
  transfers between devices with their start and end apart: 23 -> 23, of which waited for: 10 -> 13; matrix products, arithmetic and copies ran while one was open for 16% -> 2% of each run, Pallas kernels for 2% -> 14%
where the time goes in v2:
time: 58.3 us; the launch traced here: 58.1 us
  starting transfers between devices  28.1 us (48%)
  waiting for transfers between devices  13.1 us (22%)
  Pallas kernels  11.9 us (20%)
  local copies, waits for them, and re-layouts  2.29 us (4%)
  between operations  1.44 us (2%)
  other arithmetic  1.22 us (2%)
    ppermute x15, starting transfers between devices, shift(): lax.ppermute(v, 'req', [(j, 2 * ((j // 2 + step) % fan) + j % 2) for j in...  18.2 us
    pallas_call x13, Pallas kernels, call(): pl.pallas_call(body, out_shape=out_shape, in_specs=in_specs, out_specs=ja...  11.9 us
    ppermute x15, waiting for transfers between devices, shift(): lax.ppermute(v, 'req', [(j, 2 * ((j // 2 + step) % fan) + j % 2) for j in...  11 us
    ppermute x4, starting transfers between devices, to_owner(): return lax.ppermute(v, ('fsdp', 'req'), moves)  9.24 us
    unnamed x10, local copies, waits for them, and re-layouts  2.29 us
    broadcast_in_dim x2, other arithmetic, tail_rows(): return lax.dynamic_slice_in_dim(joined, accepted[0], KC - 1, 0)[None]  1.22 us
  transfers between devices with their start and end apart: 23, of which 13 were waited for; matrix products, arithmetic and copies ran while one was open for 2% of the time, Pallas kernels for 14%

profile of v2, /device:TPU:0, one launch (start us, length us, event | category | flops | bytes accessed | tf_op | source)
XLA Modules:
  0.0 58.1 jit_solution(638356231343192352)
XLA Ops:
  0.6 1.9 %shard_map.273 = (bf16[32,640]{1,0:T(8,128)(2,1)S(1)}, bf16[32,640]{1,0:T(8,128)(2,1)S(1)}, bf16[32,640]{1,0:T(8,128)(2,1)S(1)}, bf16[32,640]{1,0:T(8,128)(2,1)S...) custom-call(bf16[1,16,2560]{2,1,0:T(8,128)(2,1)} %drafts_hbm.1, bf16[1,3,256]{2,1,0:T(4,128)(2,1)} %history_hbm.1, ...), custom_call_target="tpu_custom_call" | custom-call | flops 10 | bytes 81920 | tf_op jit(solution)/shard_map/pallas_call | solution.py:29
  3.1 2.9 %collective-permute-start = (bf16[32,640]{1,0:T(8,128)(2,1)S(1)}, bf16[32,640]{1,0:T(8,128)(2,1)S(1)}, u32[]{:S(2)}, u32[]{:S(2)}) collective-permute-start(bf16[32,640]{1,0:T(8,128)(2,1)S(1)} %get-tuple-element.49), channel_id=1, source_target_pairs={{0,2},{1,3},{2,4},{3,5},{4,6},{5,7},{6,0},{7,1},{8,10},{9,11},{10,... | collective-permute-start | bytes 122888 | tf_op jit(solution)/shard_map/ppermute | solution.py:446
  6.0 1.5 %collective-permute-start.1 = (bf16[32,640]{1,0:T(8,128)(2,1)S(1)}, bf16[32,640]{1,0:T(8,128)(2,1)S(1)}, u32[]{:S(2)}, u32[]{:S(2)}) collective-permute-start(bf16[32,640]{1,0:T(8,128)(2,1)S(1)} %get-tuple-element.50), channel_id=1, source_target_pairs={{0,4},{1,5},{2,6},{3,7},{4,0},{5,1},{6,2},{7,3},{8,12},{9,13},{10,... | collective-permute-start | bytes 122888 | tf_op jit(solution)/shard_map/ppermute | solution.py:446
  7.5 1.4 %collective-permute-start.2 = (bf16[32,640]{1,0:T(8,128)(2,1)S(1)}, bf16[32,640]{1,0:T(8,128)(2,1)S(1)}, u32[]{:S(2)}, u32[]{:S(2)}) collective-permute-start(bf16[32,640]{1,0:T(8,128)(2,1)S(1)} %get-tuple-element.51), channel_id=1, source_target_pairs={{0,6},{1,7},{2,0},{3,1},{4,2},{5,3},{6,4},{7,5},{8,14},{9,15},{10,... | collective-permute-start | bytes 122888 | tf_op jit(solution)/shard_map/ppermute | solution.py:446
  9.1 1.0 %collective-permute-done.1.refs_2_.refs_6_ = bf16[32,640]{1,0:T(8,128)(2,1)S(1)} collective-permute-done((bf16[32,640]{1,0:T(8,128)(2,1)S(1)}, bf16[32,640]{1,0:T(8,128)(2,1)S(1)}, u32[]{:S(2)}, u32[]{:S(2)}) %collective-permute-start.1) | collective-permute-done | bytes 40992 | tf_op jit(solution)/shard_map/ppermute | solution.py:446
  10.0 1.5 %collective-permute-done.2.refs_3_.refs_7_ = bf16[32,640]{1,0:T(8,128)(2,1)S(1)} collective-permute-done((bf16[32,640]{1,0:T(8,128)(2,1)S(1)}, bf16[32,640]{1,0:T(8,128)(2,1)S(1)}, u32[]{:S(2)}, u32[]{:S(2)}) %collective-permute-start.2) | collective-permute-done | bytes 40992 | tf_op jit(solution)/shard_map/ppermute | solution.py:446
  12.0 0.9 %collective-permute-start.6 = (bf16[64,384]{1,0:T(8,128)(2,1)S(1)}, bf16[64,384]{1,0:T(8,128)(2,1)S(1)}, u32[]{:S(2)}, u32[]{:S(2)}) collective-permute-start(bf16[64,384]{1,0:T(8,128)(2,1)S(1)} %shard_map.274.refs_16_.refs_0_), channel_id=1, source_target_pairs={{0,2},{1,3},{2,4},{3,5},{4,6},{5,7},{6,0},{7,1},{8,10},{9,11},{10,... | collective-permute-start | bytes 147464 | tf_op jit(solution)/shard_map/ppermute | solution.py:446
  12.9 2.0 %collective-permute-start.5 = (bf16[64,384]{1,0:T(8,128)(2,1)S(1)}, bf16[64,384]{1,0:T(8,128)(2,1)S(1)}, u32[]{:S(2)}, u32[]{:S(2)}) collective-permute-start(bf16[64,384]{1,0:T(8,128)(2,1)S(1)} %shard_map.274.refs_16_.refs_0_), channel_id=1, source_target_pairs={{0,4},{1,5},{2,6},{3,7},{4,0},{5,1},{6,2},{7,3},{8,12},{9,13},{10,... | collective-permute-start | bytes 147464 | tf_op jit(solution)/shard_map/ppermute | solution.py:446
  15.4 1.4 %shard_map.275 = (bf16[4,256]{1,0:T(4,128)(2,1)S(1)}, bf16[256]{0:T(256)(128)(2,1)S(1)}, f32[20]{0:T(128)S(1)}, f32[20]{0:T(128)S(1)}, bf16[4,1280]{1,0:T(4,128)...) custom-call(bf16[4,256]{1,0:T(4,128)(2,1)} %refs_0_.1, ...), custom_call_target="tpu_custom_call" | custom-call | bytes 794776 | tf_op jit(solution)/shard_map/pallas_call | solution.py:29
  16.9 0.9 %shard_map.276 = (bf16[16,2560]{1,0:T(8,128)(2,1)S(1)}, bf16[16,2560]{1,0:T(8,128)(2,1)S(1)}, bf16[16,2560]{1,0:T(8,128)(2,1)S(1)}, bf16[16,2560]{1,0:T(8,128)(2,1)S(1)}) custom-call(bf16[32,640]{1,0:T(8,128)(2,1)S(1)} %get-tuple-element.48.refs_0_.refs_4_, bf16[32,640]{1,0:T(8,128)(2,1)S(1)} %collective-permute-done.refs_1_.refs_5_, ...), custom_call_target="tpu_custom_call" | custom-call | flops 209715200 | bytes 3276800 | tf_op jit(solution)/shard_map/pallas_call | solution.py:29
  19.2 1.5 %collective-permute-start.9 = (bf16[16,2560]{1,0:T(8,128)(2,1)S(1)}, bf16[16,2560]{1,0:T(8,128)(2,1)S(1)}, u32[]{:S(2)}, u32[]{:S(2)}) collective-permute-start(bf16[16,2560]{1,0:T(8,128)(2,1)S(1)} %get-tuple-element.66), channel_id=1, source_target_pairs={{0,6},{1,7},{2,0},{3,1},{4,2},{5,3},{6,4},{7,5},{8,14},{9,15},{10,... | collective-permute-start | bytes 245768 | tf_op jit(solution)/shard_map/ppermute | solution.py:446
  20.7 1.5 %collective-permute-start.10 = (bf16[16,2560]{1,0:T(8,128)(2,1)S(1)}, bf16[16,2560]{1,0:T(8,128)(2,1)S(1)}, u32[]{:S(2)}, u32[]{:S(2)}) collective-permute-start(bf16[16,2560]{1,0:T(8,128)(2,1)S(1)} %get-tuple-element.67), channel_id=1, source_target_pairs={{0,4},{1,5},{2,6},{3,7},{4,0},{5,1},{6,2},{7,3},{8,12},{9,13},{10,... | collective-permute-start | bytes 245768 | tf_op jit(solution)/shard_map/ppermute | solution.py:446
  22.2 3.8 %shard_map.278.total = f32[128,1280]{1,0:T(8,128)S(1)} custom-call(s32[10]{0:T(128)S(1)} %get-tuple-element.53.slot_req, s32[10]{0:T(128)S(1)} %get-tuple-element.54.slot_page, s32[8]{0:T(128)S(1)} %get-tuple-element.55.page_count, s32[8]{0:T(128)S(1)} %get-tuple-element.56.owner_row, f32[64,256]{1,0:T(8,128)S(1)} %get-tuple-element.63.own_ref.refs_4_.packed, ...), custom_call_target="tpu_custom_call" | custom-call | flops 419430400 | bytes 6553600 | tf_op jit(solution)/shard_map/pallas_call | solution.py:29
  26.1 1.5 %collective-permute-done.11.refs_3_ = bf16[16,2560]{1,0:T(8,128)(2,1)S(1)} collective-permute-done((bf16[16,2560]{1,0:T(8,128)(2,1)S(1)}, bf16[16,2560]{1,0:T(8,128)(2,1)S(1)}, u32[]{:S(2)}, u32[]{:S(2)}) %collective-permute-start.11) | collective-permute-done | bytes 81952 | tf_op jit(solution)/shard_map/ppermute | solution.py:446
  28.1 1.0 %collective-permute-done.12.other = bf16[64,1280]{1,0:T(8,128)(2,1)S(1)} collective-permute-done((bf16[64,1280]{1,0:T(8,128)(2,1)S(1)}, bf16[64,1280]{1,0:T(8,128)(2,1)S(1)}, u32[]{:S(2)}, u32[]{:S(2)}) %collective-permute-start.12) | collective-permute-done | bytes 163872 | tf_op jit(solution)/shard_map/ppermute | solution.py:443
  29.1 0.7 %collective-permute-start.13 = (bf16[16,1280]{1,0:T(8,128)(2,1)S(1)}, bf16[16,1280]{1,0:T(8,128)(2,1)S(1)}, u32[]{:S(2)}, u32[]{:S(2)}) collective-permute-start(bf16[16,1280]{1,0:T(8,128)(2,1)S(1)} %get-tuple-element.80), channel_id=1, source_target_pairs={{0,6},{1,7},{2,0},{3,1},{4,2},{5,3},{6,4},{7,5},{8,14},{9,15},{10,... | collective-permute-start | bytes 122888 | tf_op jit(solution)/shard_map/ppermute | solution.py:446
  29.9 1.3 %collective-permute-start.14 = (bf16[16,1280]{1,0:T(8,128)(2,1)S(1)}, bf16[16,1280]{1,0:T(8,128)(2,1)S(1)}, u32[]{:S(2)}, u32[]{:S(2)}) collective-permute-start(bf16[16,1280]{1,0:T(8,128)(2,1)S(1)} %get-tuple-element.81), channel_id=1, source_target_pairs={{0,4},{1,5},{2,6},{3,7},{4,0},{5,1},{6,2},{7,3},{8,12},{9,13},{10,... | collective-permute-start | bytes 122888 | tf_op jit(solution)/shard_map/ppermute | solution.py:446
  31.1 1.0 %collective-permute-start.15 = (bf16[16,1280]{1,0:T(8,128)(2,1)S(1)}, bf16[16,1280]{1,0:T(8,128)(2,1)S(1)}, u32[]{:S(2)}, u32[]{:S(2)}) collective-permute-start(bf16[16,1280]{1,0:T(8,128)(2,1)S(1)} %get-tuple-element.82), channel_id=1, source_target_pairs={{0,2},{1,3},{2,4},{3,5},{4,6},{5,7},{6,0},{7,1},{8,10},{9,11},{10,... | collective-permute-start | bytes 122888 | tf_op jit(solution)/shard_map/ppermute | solution.py:446
  33.2 0.7 %collective-permute-done.14.refs_2_ = bf16[16,1280]{1,0:T(8,128)(2,1)S(1)} collective-permute-done((bf16[16,1280]{1,0:T(8,128)(2,1)S(1)}, bf16[16,1280]{1,0:T(8,128)(2,1)S(1)}, u32[]{:S(2)}, u32[]{:S(2)}) %collective-permute-start.14) | collective-permute-done | bytes 40992 | tf_op jit(solution)/shard_map/ppermute | solution.py:446
  33.9 2.2 %collective-permute-done.15.refs_3_ = bf16[16,1280]{1,0:T(8,128)(2,1)S(1)} collective-permute-done((bf16[16,1280]{1,0:T(8,128)(2,1)S(1)}, bf16[16,1280]{1,0:T(8,128)(2,1)S(1)}, u32[]{:S(2)}, u32[]{:S(2)}) %collective-permute-start.15) | collective-permute-done | bytes 40992 | tf_op jit(solution)/shard_map/ppermute | solution.py:446
  36.1 0.7 %collective-permute-start.18 = (bf16[16,1280]{1,0:T(8,128)(2,1)S(1)}, bf16[16,1280]{1,0:T(8,128)(2,1)S(1)}, u32[]{:S(2)}, u32[]{:S(2)}) collective-permute-start(bf16[16,1280]{1,0:T(8,128)(2,1)S(1)} %shard_map.282.refs_0_), channel_id=1, source_target_pairs={{0,6},{1,7},{2,0},{3,1},{4,2},{5,3},{6,4},{7,5},{8,14},{9,15},{10,... | collective-permute-start | bytes 122888 | tf_op jit(solution)/shard_map/ppermute | solution.py:446
  36.8 0.9 %collective-permute-start.17 = (bf16[16,1280]{1,0:T(8,128)(2,1)S(1)}, bf16[16,1280]{1,0:T(8,128)(2,1)S(1)}, u32[]{:S(2)}, u32[]{:S(2)}) collective-permute-start(bf16[16,1280]{1,0:T(8,128)(2,1)S(1)} %shard_map.282.refs_0_), channel_id=1, source_target_pairs={{0,4},{1,5},{2,6},{3,7},{4,0},{5,1},{6,2},{7,3},{8,12},{9,13},{10,... | collective-permute-start | bytes 122888 | tf_op jit(solution)/shard_map/ppermute | solution.py:446
  37.7 1.2 %collective-permute-start.16 = (bf16[16,1280]{1,0:T(8,128)(2,1)S(1)}, bf16[16,1280]{1,0:T(8,128)(2,1)S(1)}, u32[]{:S(2)}, u32[]{:S(2)}) collective-permute-start(bf16[16,1280]{1,0:T(8,128)(2,1)S(1)} %shard_map.282.refs_0_), channel_id=1, source_target_pairs={{0,2},{1,3},{2,4},{3,5},{4,6},{5,7},{6,0},{7,1},{8,10},{9,11},{10,... | collective-permute-start | bytes 122888 | tf_op jit(solution)/shard_map/ppermute | solution.py:446
  40.8 1.8 %collective-permute-done.16.refs_1_ = bf16[16,1280]{1,0:T(8,128)(2,1)S(1)} collective-permute-done((bf16[16,1280]{1,0:T(8,128)(2,1)S(1)}, bf16[16,1280]{1,0:T(8,128)(2,1)S(1)}, u32[]{:S(2)}, u32[]{:S(2)}) %collective-permute-start.16) | collective-permute-done | bytes 40992 | tf_op jit(solution)/shard_map/ppermute | solution.py:446
  42.6 1.7 %copy-done.1 = bf16[960,1280]{1,0:T(8,128)(2,1)S(1)} copy-done((bf16[960,1280]{1,0:T(8,128)(2,1)S(1)}, bf16[960,1280]{1,0:T(8,128)(2,1)}, u32[]{:S(2)}) %copy-start.1) | copy-done | bytes 2457624
  45.0 0.7 %collective-permute-start.19 = (bf16[16,768]{1,0:T(8,128)(2,1)S(1)}, bf16[16,768]{1,0:T(8,128)(2,1)S(1)}, u32[]{:S(2)}, u32[]{:S(2)}) collective-permute-start(bf16[16,768]{1,0:T(8,128)(2,1)S(1)} %get-tuple-element.85), channel_id=1, source_target_pairs={{0,0},{1,1},{2,8},{3,9},{4,16},{5,17},{6,24},{7,25},{8,2},{9,3},{1... | collective-permute-start | bytes 73736 | tf_op jit(solution)/shard_map/ppermute | solution.py:571
  45.6 4.3 %collective-permute-start.20 = (bf16[16,768]{1,0:T(8,128)(2,1)S(1)}, bf16[16,768]{1,0:T(8,128)(2,1)S(1)}, u32[]{:S(2)}, u32[]{:S(2)}) collective-permute-start(bf16[16,768]{1,0:T(8,128)(2,1)S(1)} %get-tuple-element.86), channel_id=1, source_target_pairs={{0,2},{1,3},{2,10},{3,11},{4,18},{5,19},{6,26},{7,27},{8,4},{9,5},... | collective-permute-start | bytes 73736 | tf_op jit(solution)/shard_map/ppermute | solution.py:571
  50.0 2.9 %collective-permute-start.21 = (bf16[16,768]{1,0:T(8,128)(2,1)S(1)}, bf16[16,768]{1,0:T(8,128)(2,1)S(1)}, u32[]{:S(2)}, u32[]{:S(2)}) collective-permute-start(bf16[16,768]{1,0:T(8,128)(2,1)S(1)} %get-tuple-element.87), channel_id=1, source_target_pairs={{0,4},{1,5},{2,12},{3,13},{4,20},{5,21},{6,28},{7,29},{8,6},{9,7},... | collective-permute-start | bytes 73736 | tf_op jit(solution)/shard_map/ppermute | solution.py:571
  52.9 1.3 %collective-permute-start.22 = (bf16[16,768]{1,0:T(8,128)(2,1)S(1)}, bf16[16,768]{1,0:T(8,128)(2,1)S(1)}, u32[]{:S(2)}, u32[]{:S(2)}) collective-permute-start(bf16[16,768]{1,0:T(8,128)(2,1)S(1)} %get-tuple-element.88), channel_id=1, source_target_pairs={{0,6},{1,7},{2,14},{3,15},{4,22},{5,23},{6,30},{7,31},{8,0},{9,1},... | collective-permute-start | bytes 73736 | tf_op jit(solution)/shard_map/ppermute | solution.py:571
  54.8 1.4 %shard_map.285 = f32[20,64,128]{2,1,0:T(8,128)} custom-call(s32[1]{0:T(128)} %copy.30.accepted, f32[64,256]{1,0:T(8,128)S(1)} %get-tuple-element.63.own_ref.refs_4_.packed, f32[16,20]{1,0:T(8,128)S(1)} %get-tuple-element.72.refs_6_.dtime_ref, bf16[16,1280]{1,0:T(8,128)(2,1)S(1)} %get-tuple-element.89.x_act, ...), custom_call_target="tpu_custom_call" | custom-call | flops 10485760 | bytes 1310720 | tf_op jit(solution)/shard_map/pallas_call | solution.py:29
  56.3 1.0 %collective-permute-done.21.refs_2_ = bf16[16,768]{1,0:T(8,128)(2,1)S(1)} collective-permute-done((bf16[16,768]{1,0:T(8,128)(2,1)S(1)}, bf16[16,768]{1,0:T(8,128)(2,1)S(1)}, u32[]{:S(2)}, u32[]{:S(2)}) %collective-permute-start.21) | collective-permute-done | bytes 24608 | tf_op jit(solution)/shard_map/ppermute | solution.py:571
  57.3 0.8 %shard_map.284 = bf16[16,640]{1,0:T(8,128)(2,1)} custom-call(bf16[16,768]{1,0:T(8,128)(2,1)S(1)} %collective-permute-done.19.refs_0_, bf16[16,768]{1,0:T(8,128)(2,1)S(1)} %collective-permute-done.20.refs_1_, bf16[16,768]{1,0:T(8,128)(2,1)S(1)} %collective-permute-done.21.refs_2_, bf16[16,768]{1,0:T(8,128)(2,1)S(1)} %collective-permute-done.22.refs_3_), custom_call_target="tpu_custom_call" | custom-call | flops 51200 | bytes 51200 | tf_op jit(solution)/shard_map/pallas_call | solution.py:29
  (39 shorter events, 7.3 us)
Async XLA Ops:
  2.5 14.4 %collective-permute-start.7 = (bf16[960,1280]{1,0:T(8,128)(2,1)S(1)}, bf16[960,1280]{1,0:T(8,128)(2,1)S(1)}, u32[]{:S(2)}, u32[]{:S(2)}) collective-permute-start(bf16[960,1280]{1,0:T(8,128)(2,1)S(1)} %get-tuple-element.61.refs_4_.refs_5_), channel_id=1, source_target_pairs={{0,1},{1,0},{2,3},{3,2},{4,5},{5,4},{6,7},{7,6},{8,9},{9,8},{10,11... | collective-permute-start | bytes 7372808 | tf_op jit(solution)/shard_map/ppermute | solution.py:443
  3.0 8.5 %collective-permute-start.3 = (bf16[352,384]{1,0:T(8,128)(2,1)S(1)}, bf16[352,384]{1,0:T(8,128)(2,1)S(1)}, u32[]{:S(2)}, u32[]{:S(2)}) collective-permute-start(bf16[352,384]{1,0:T(8,128)(2,1)S(1)} %get-tuple-element.52.refs_4_), channel_id=1, source_target_pairs={{0,1},{1,0},{2,3},{3,2},{4,5},{5,4},{6,7},{7,6},{8,9},{9,8},{10,11... | collective-permute-start | bytes 811016 | tf_op jit(solution)/shard_map/ppermute | solution.py:443
  3.1 6.0 %collective-permute-start = (bf16[32,640]{1,0:T(8,128)(2,1)S(1)}, bf16[32,640]{1,0:T(8,128)(2,1)S(1)}, u32[]{:S(2)}, u32[]{:S(2)}) collective-permute-start(bf16[32,640]{1,0:T(8,128)(2,1)S(1)} %get-tuple-element.49), channel_id=1, source_target_pairs={{0,2},{1,3},{2,4},{3,5},{4,6},{5,7},{6,0},{7,1},{8,10},{9,11},{10,... | collective-permute-start | bytes 122888 | tf_op jit(solution)/shard_map/ppermute | solution.py:446
  6.0 4.0 %collective-permute-start.1 = (bf16[32,640]{1,0:T(8,128)(2,1)S(1)}, bf16[32,640]{1,0:T(8,128)(2,1)S(1)}, u32[]{:S(2)}, u32[]{:S(2)}) collective-permute-start(bf16[32,640]{1,0:T(8,128)(2,1)S(1)} %get-tuple-element.50), channel_id=1, source_target_pairs={{0,4},{1,5},{2,6},{3,7},{4,0},{5,1},{6,2},{7,3},{8,12},{9,13},{10,... | collective-permute-start | bytes 122888 | tf_op jit(solution)/shard_map/ppermute | solution.py:446
  7.5 4.0 %collective-permute-start.2 = (bf16[32,640]{1,0:T(8,128)(2,1)S(1)}, bf16[32,640]{1,0:T(8,128)(2,1)S(1)}, u32[]{:S(2)}, u32[]{:S(2)}) collective-permute-start(bf16[32,640]{1,0:T(8,128)(2,1)S(1)} %get-tuple-element.51), channel_id=1, source_target_pairs={{0,6},{1,7},{2,0},{3,1},{4,2},{5,3},{6,4},{7,5},{8,14},{9,15},{10,... | collective-permute-start | bytes 122888 | tf_op jit(solution)/shard_map/ppermute | solution.py:446
  12.0 6.3 %collective-permute-start.6 = (bf16[64,384]{1,0:T(8,128)(2,1)S(1)}, bf16[64,384]{1,0:T(8,128)(2,1)S(1)}, u32[]{:S(2)}, u32[]{:S(2)}) collective-permute-start(bf16[64,384]{1,0:T(8,128)(2,1)S(1)} %shard_map.274.refs_16_.refs_0_), channel_id=1, source_target_pairs={{0,2},{1,3},{2,4},{3,5},{4,6},{5,7},{6,0},{7,1},{8,10},{9,11},{10,... | collective-permute-start | bytes 147464 | tf_op jit(solution)/shard_map/ppermute | solution.py:446
  12.9 5.4 %collective-permute-start.5 = (bf16[64,384]{1,0:T(8,128)(2,1)S(1)}, bf16[64,384]{1,0:T(8,128)(2,1)S(1)}, u32[]{:S(2)}, u32[]{:S(2)}) collective-permute-start(bf16[64,384]{1,0:T(8,128)(2,1)S(1)} %shard_map.274.refs_16_.refs_0_), channel_id=1, source_target_pairs={{0,4},{1,5},{2,6},{3,7},{4,0},{5,1},{6,2},{7,3},{8,12},{9,13},{10,... | collective-permute-start | bytes 147464 | tf_op jit(solution)/shard_map/ppermute | solution.py:446
  14.9 4.1 %collective-permute-start.4 = (bf16[64,384]{1,0:T(8,128)(2,1)S(1)}, bf16[64,384]{1,0:T(8,128)(2,1)S(1)}, u32[]{:S(2)}, u32[]{:S(2)}) collective-permute-start(bf16[64,384]{1,0:T(8,128)(2,1)S(1)} %shard_map.274.refs_16_.refs_0_), channel_id=1, source_target_pairs={{0,6},{1,7},{2,0},{3,1},{4,2},{5,3},{6,4},{7,5},{8,14},{9,15},{10,... | collective-permute-start | bytes 147464 | tf_op jit(solution)/shard_map/ppermute | solution.py:446
  16.9 1.5 %copy-start = (bf16[960,1280]{1,0:T(8,128)(2,1)}, bf16[960,1280]{1,0:T(8,128)(2,1)S(1)}, u32[]{:S(2)}) copy-start(bf16[960,1280]{1,0:T(8,128)(2,1)S(1)} %collective-permute-done.7.refs_5_.refs_6_) | copy-start | bytes 7372804
  19.2 3.1 %collective-permute-start.8 = (f32[64,256]{1,0:T(8,128)S(1)}, f32[64,256]{1,0:T(8,128)S(1)}, u32[]{:S(2)}, u32[]{:S(2)}) collective-permute-start(f32[64,256]{1,0:T(8,128)S(1)} %get-tuple-element.63.own_ref.refs_4_.packed), channel_id=1, source_target_pairs={{0,1},{1,0},{2,3},{3,2},{4,5},{5,4},{6,7},{7,6},{8,9},{9,8},{10,11... | collective-permute-start | bytes 196616 | tf_op jit(solution)/shard_map/ppermute | solution.py:443
  19.2 6.8 %collective-permute-start.9 = (bf16[16,2560]{1,0:T(8,128)(2,1)S(1)}, bf16[16,2560]{1,0:T(8,128)(2,1)S(1)}, u32[]{:S(2)}, u32[]{:S(2)}) collective-permute-start(bf16[16,2560]{1,0:T(8,128)(2,1)S(1)} %get-tuple-element.66), channel_id=1, source_target_pairs={{0,6},{1,7},{2,0},{3,1},{4,2},{5,3},{6,4},{7,5},{8,14},{9,15},{10,... | collective-permute-start | bytes 245768 | tf_op jit(solution)/shard_map/ppermute | solution.py:446
  20.7 5.4 %collective-permute-start.10 = (bf16[16,2560]{1,0:T(8,128)(2,1)S(1)}, bf16[16,2560]{1,0:T(8,128)(2,1)S(1)}, u32[]{:S(2)}, u32[]{:S(2)}) collective-permute-start(bf16[16,2560]{1,0:T(8,128)(2,1)S(1)} %get-tuple-element.67), channel_id=1, source_target_pairs={{0,4},{1,5},{2,6},{3,7},{4,0},{5,1},{6,2},{7,3},{8,12},{9,13},{10,... | collective-permute-start | bytes 245768 | tf_op jit(solution)/shard_map/ppermute | solution.py:446
  22.2 5.3 %collective-permute-start.11 = (bf16[16,2560]{1,0:T(8,128)(2,1)S(1)}, bf16[16,2560]{1,0:T(8,128)(2,1)S(1)}, u32[]{:S(2)}, u32[]{:S(2)}) collective-permute-start(bf16[16,2560]{1,0:T(8,128)(2,1)S(1)} %get-tuple-element.68), channel_id=1, source_target_pairs={{0,2},{1,3},{2,4},{3,5},{4,6},{5,7},{6,0},{7,1},{8,10},{9,11},{10,... | collective-permute-start | bytes 245768 | tf_op jit(solution)/shard_map/ppermute | solution.py:446
  22.2 16.7 %copy-start.4 = (bf16[1,3,256]{2,1,0:T(4,128)(2,1)S(1)}, bf16[1,3,256]{2,1,0:T(4,128)(2,1)}, u32[]{:S(2)}) copy-start(bf16[1,3,256]{2,1,0:T(4,128)(2,1)} %history_hbm.1) | copy-start | bytes 4612
  27.6 1.5 %collective-permute-start.12 = (bf16[64,1280]{1,0:T(8,128)(2,1)S(1)}, bf16[64,1280]{1,0:T(8,128)(2,1)S(1)}, u32[]{:S(2)}, u32[]{:S(2)}) collective-permute-start(bf16[64,1280]{1,0:T(8,128)(2,1)S(1)} %get-tuple-element.70), channel_id=1, source_target_pairs={{0,1},{1,0},{2,3},{3,2},{4,5},{5,4},{6,7},{7,6},{8,9},{9,8},{10,11... | collective-permute-start | bytes 491528 | tf_op jit(solution)/shard_map/ppermute | solution.py:443
  29.1 4.1 %collective-permute-start.13 = (bf16[16,1280]{1,0:T(8,128)(2,1)S(1)}, bf16[16,1280]{1,0:T(8,128)(2,1)S(1)}, u32[]{:S(2)}, u32[]{:S(2)}) collective-permute-start(bf16[16,1280]{1,0:T(8,128)(2,1)S(1)} %get-tuple-element.80), channel_id=1, source_target_pairs={{0,6},{1,7},{2,0},{3,1},{4,2},{5,3},{6,4},{7,5},{8,14},{9,15},{10,... | collective-permute-start | bytes 122888 | tf_op jit(solution)/shard_map/ppermute | solution.py:446
  29.9 4.0 %collective-permute-start.14 = (bf16[16,1280]{1,0:T(8,128)(2,1)S(1)}, bf16[16,1280]{1,0:T(8,128)(2,1)S(1)}, u32[]{:S(2)}, u32[]{:S(2)}) collective-permute-start(bf16[16,1280]{1,0:T(8,128)(2,1)S(1)} %get-tuple-element.81), channel_id=1, source_target_pairs={{0,4},{1,5},{2,6},{3,7},{4,0},{5,1},{6,2},{7,3},{8,12},{9,13},{10,... | collective-permute-start | bytes 122888 | tf_op jit(solution)/shard_map/ppermute | solution.py:446
  31.1 4.9 %collective-permute-start.15 = (bf16[16,1280]{1,0:T(8,128)(2,1)S(1)}, bf16[16,1280]{1,0:T(8,128)(2,1)S(1)}, u32[]{:S(2)}, u32[]{:S(2)}) collective-permute-start(bf16[16,1280]{1,0:T(8,128)(2,1)S(1)} %get-tuple-element.82), channel_id=1, source_target_pairs={{0,2},{1,3},{2,4},{3,5},{4,6},{5,7},{6,0},{7,1},{8,10},{9,11},{10,... | collective-permute-start | bytes 122888 | tf_op jit(solution)/shard_map/ppermute | solution.py:446
  36.1 4.1 %collective-permute-start.18 = (bf16[16,1280]{1,0:T(8,128)(2,1)S(1)}, bf16[16,1280]{1,0:T(8,128)(2,1)S(1)}, u32[]{:S(2)}, u32[]{:S(2)}) collective-permute-start(bf16[16,1280]{1,0:T(8,128)(2,1)S(1)} %shard_map.282.refs_0_), channel_id=1, source_target_pairs={{0,6},{1,7},{2,0},{3,1},{4,2},{5,3},{6,4},{7,5},{8,14},{9,15},{10,... | collective-permute-start | bytes 122888 | tf_op jit(solution)/shard_map/ppermute | solution.py:446
  36.8 4.0 %collective-permute-start.17 = (bf16[16,1280]{1,0:T(8,128)(2,1)S(1)}, bf16[16,1280]{1,0:T(8,128)(2,1)S(1)}, u32[]{:S(2)}, u32[]{:S(2)}) collective-permute-start(bf16[16,1280]{1,0:T(8,128)(2,1)S(1)} %shard_map.282.refs_0_), channel_id=1, source_target_pairs={{0,4},{1,5},{2,6},{3,7},{4,0},{5,1},{6,2},{7,3},{8,12},{9,13},{10,... | collective-permute-start | bytes 122888 | tf_op jit(solution)/shard_map/ppermute | solution.py:446
  37.7 4.9 %collective-permute-start.16 = (bf16[16,1280]{1,0:T(8,128)(2,1)S(1)}, bf16[16,1280]{1,0:T(8,128)(2,1)S(1)}, u32[]{:S(2)}, u32[]{:S(2)}) collective-permute-start(bf16[16,1280]{1,0:T(8,128)(2,1)S(1)} %shard_map.282.refs_0_), channel_id=1, source_target_pairs={{0,2},{1,3},{2,4},{3,5},{4,6},{5,7},{6,0},{7,1},{8,10},{9,11},{10,... | collective-permute-start | bytes 122888 | tf_op jit(solution)/shard_map/ppermute | solution.py:446
  42.6 1.7 %copy-start.1 = (bf16[960,1280]{1,0:T(8,128)(2,1)S(1)}, bf16[960,1280]{1,0:T(8,128)(2,1)}, u32[]{:S(2)}) copy-start(bf16[960,1280]{1,0:T(8,128)(2,1)} %copy-done) | copy-start | bytes 7372804
  44.3 9.9 %copy-start.3 = (bf16[1,3,1280]{2,1,0:T(4,128)(2,1)S(1)}, bf16[1,3,1280]{2,1,0:T(4,128)(2,1)}, u32[]{:S(2)}) copy-start(bf16[1,3,1280]{2,1,0:T(4,128)(2,1)} %refs_7_.1) | copy-start | bytes 23044
  44.3 10.5 %copy-start.2 = (f32[1,20,64,128]{3,2,1,0:T(8,128)S(1)}, f32[1,20,64,128]{3,2,1,0:T(8,128)}, u32[]{:S(2)}) copy-start(f32[1,20,64,128]{3,2,1,0:T(8,128)} %param.41) | copy-start | bytes 1966084
  45.0 11.3 %collective-permute-start.19 = (bf16[16,768]{1,0:T(8,128)(2,1)S(1)}, bf16[16,768]{1,0:T(8,128)(2,1)S(1)}, u32[]{:S(2)}, u32[]{:S(2)}) collective-permute-start(bf16[16,768]{1,0:T(8,128)(2,1)S(1)} %get-tuple-element.85), channel_id=1, source_target_pairs={{0,0},{1,1},{2,8},{3,9},{4,16},{5,17},{6,24},{7,25},{8,2},{9,3},{1... | collective-permute-start | bytes 73736 | tf_op jit(solution)/shard_map/ppermute | solution.py:571
  45.6 10.6 %collective-permute-start.20 = (bf16[16,768]{1,0:T(8,128)(2,1)S(1)}, bf16[16,768]{1,0:T(8,128)(2,1)S(1)}, u32[]{:S(2)}, u32[]{:S(2)}) collective-permute-start(bf16[16,768]{1,0:T(8,128)(2,1)S(1)} %get-tuple-element.86), channel_id=1, source_target_pairs={{0,2},{1,3},{2,10},{3,11},{4,18},{5,19},{6,26},{7,27},{8,4},{9,5},... | collective-permute-start | bytes 73736 | tf_op jit(solution)/shard_map/ppermute | solution.py:571
  50.0 7.3 %collective-permute-start.21 = (bf16[16,768]{1,0:T(8,128)(2,1)S(1)}, bf16[16,768]{1,0:T(8,128)(2,1)S(1)}, u32[]{:S(2)}, u32[]{:S(2)}) collective-permute-start(bf16[16,768]{1,0:T(8,128)(2,1)S(1)} %get-tuple-element.87), channel_id=1, source_target_pairs={{0,4},{1,5},{2,12},{3,13},{4,20},{5,21},{6,28},{7,29},{8,6},{9,7},... | collective-permute-start | bytes 73736 | tf_op jit(solution)/shard_map/ppermute | solution.py:571
  52.9 4.5 %collective-permute-start.22 = (bf16[16,768]{1,0:T(8,128)(2,1)S(1)}, bf16[16,768]{1,0:T(8,128)(2,1)S(1)}, u32[]{:S(2)}, u32[]{:S(2)}) collective-permute-start(bf16[16,768]{1,0:T(8,128)(2,1)S(1)} %get-tuple-element.88), channel_id=1, source_target_pairs={{0,6},{1,7},{2,14},{3,15},{4,22},{5,23},{6,30},{7,31},{8,0},{9,1},... | collective-permute-start | bytes 73736 | tf_op jit(solution)/shard_map/ppermute | solution.py:571

commit v3 on v2

--- a/solution.py
+++ b/solution.py
@@ -115,12 +115,13 @@
     past = jnp.concatenate([past, jnp.zeros((length - past.shape[0], past.shape[1]), F32)], axis=0)
     if share % 128:
         width = drafts.shape[2]
-        whole = pltpu.roll(drafts[0].astype(F32), width - pair * share, 1)
+        whole = drafts[0].astype(F32)
     for s, out in enumerate(outs):
         if share % 128:
-            piece = whole[:, s * share : (s + 1) * share].astype(BF)
+            shift = (width - (pair ^ s) * share) % width
+            piece = pltpu.roll(whole, shift, 1)[:, :share].astype(BF)
         else:
-            start = pl.multiple_of(((pair + s) % fan) * share, 128)
+            start = pl.multiple_of((pair ^ s) * share, 128)
             piece = drafts[0, :, pl.ds(start, share)]
         out[0:length, :share] = piece
         out[length : 2 * length, : 2 * NS] = past.astype(BF)
@@ -177,7 +178,7 @@
 def project_xz_kernel(length, fan, *refs):
     blocks = refs[:fan]
     mine, theirs = refs[fan : fan + 2]
-    outs = refs[fan + 2 :]
+    out, out_pair = refs[fan + 2 :]
     half, inner = mine.shape[0] // 3, mine.shape[1]
     own, other = own_and_other(length, half, blocks)
     for i in range(2):
@@ -185,9 +186,11 @@
         v = jnp.dot(own, mine[rows], preferred_element_type=F32) + jnp.dot(
             other, theirs[rows], preferred_element_type=F32
         )
-        v = v.astype(BF)
-        for s, out in enumerate(outs):
-            out[:, i * inner : (i + 1) * inner] = v[s * length : (s + 1) * length]
+        out[:, i * inner : (i + 1) * inner] = v.astype(BF)
+    first = lax.axis_index("req") % 2 == 0
+    a, b = mine[2 * half :], theirs[2 * half :]
+    out_pair[0:half] = jnp.where(first, a, b)
+    out_pair[half:] = jnp.where(first, b, a)
 
 
 def mix_bc_kernel(length, fan, heads, *refs):
@@ -200,7 +203,7 @@
     for t in range(fan):
         acc = None
         for s in range(fan):
-            first = length * ((t + s) % fan)
+            first = length * (t ^ s)
             piece = parts[s][first : first + length].astype(F32)
             acc = piece if acc is None else acc + piece
         bc_raw = acc[:, : 2 * NS].astype(BF)
@@ -238,7 +241,7 @@
     def place(s):
         row = owner_row[request(s)]
         away = jnp.where(row % 2 == me % 2, 0, fan)
-        return (away + (me // 2 - row // 2 + fan) % fan) * length
+        return (away + (me // 2 ^ row // 2)) * length
 
     count = jnp.int32(0)
     for s in range(slots):
@@ -301,30 +304,32 @@
         add(*visit(s))
 
 
-def halve_kernel(total, *refs):
-    mine, other = refs[-2:]
+def halve_kernel(total, mine, other):
     half = mine.shape[0]
     mine[...] = total[0:half].astype(BF)
     other[...] = total[half:].astype(BF)
 
 
-def join_kernel(length, mine, other, _, *outs):
+def join_kernel(length, mine, other, xz, *outs):
+    inner = mine.shape[1]
     for s, out in enumerate(outs):
         rows = slice(s * length, (s + 1) * length)
-        out[...] = (mine[rows].astype(F32) + other[rows].astype(F32)).astype(BF)
+        out[:, :inner] = (mine[rows].astype(F32) + other[rows].astype(F32)).astype(BF)
+        out[:, inner:] = xz[rows]
 
 
 def local_kernel(length, fan, heads, *refs):
     parts = refs[:fan]
     packed, bc_act, dtime_ref, taps, offset, history, sink_x, sink_b = refs[fan : fan + 8]
-    out, x_raw_o, x_act_o, silu_z_o = refs[fan + 8 :]
+    out, x_raw_o, x_act_o = refs[fan + 8 :]
     inner_cols = out.shape[1]
     acc = parts[0][...].astype(F32)
     for s in range(1, fan):
         acc = acc + parts[s][...].astype(F32)
-    x_raw = acc[:, :inner_cols].astype(BF)
+    page_sum = acc[:, :inner_cols]
+    x_raw = acc[:, inner_cols : 2 * inner_cols].astype(BF)
     x_raw_o[...] = x_raw
-    silu_z_o[...] = silu(acc[:, inner_cols:].astype(BF).astype(F32))
+    silu_z = silu(acc[:, 2 * inner_cols :].astype(BF).astype(F32))
     x_act = conv(
         history[0].astype(F32), x_raw.astype(F32), taps[...].astype(F32),
         offset[...].astype(F32)[None],
@@ -357,10 +362,10 @@
                 jnp.where(later, inner * jnp.exp(spread) * dtime_t[h : h + 1, :], 0.0).astype(BF)
             )
         cols = slice(first * HD, last * HD)
-        acc = head_diag(weights, x_act[:, cols])
+        acc = page_sum[:, cols] + head_diag(weights, x_act[:, cols])
         for q in range(sink_values.shape[0]):
             acc = acc + sink_w[:, q : q + 1] * sink_values[q : q + 1, cols]
-        out[:, cols] = acc
+        out[:, cols] = (acc * silu_z[:, cols]).astype(BF)
 
 
 def state_kernel(length, heads, accepted, packed, dtime_ref, x_act, bc_act, ssm, out):
@@ -384,36 +389,25 @@
         out[h] = factor[:, h : h + 1] * ssm[h] + fresh
 
 
-def gate_kernel(fan, *refs):
-    parts, local, silu_z, out = refs[:fan], refs[fan], refs[fan + 1], refs[fan + 2]
-    acc = local[...]
-    for p in parts:
-        acc = acc + p[...].astype(F32)
-    out[...] = (acc * silu_z[...]).astype(BF)
-
-
 def out_kernel(length, fan, *refs):
     blocks = refs[:fan]
-    gain, mine, theirs = refs[fan : fan + 3]
-    outs = refs[fan + 3 : 2 * fan + 3]
-    whole = refs[2 * fan + 3]
-    cols = mine.shape[0] // 3
+    gain, weights = refs[fan : fan + 2]
+    outs = refs[fan + 2 : 2 * fan + 2]
+    whole = refs[2 * fan + 2]
+    cols = weights.shape[0]
     me, zed = lax.axis_index("req"), lax.axis_index("fsdp")
     g = jnp.concatenate([b[...] for b in blocks], axis=0).astype(F32)
     squares = jnp.sum(g * g, axis=1, keepdims=True)
     scaled = (g * gain[...].astype(F32)[None]).astype(BF)
-    turned = (((1,), (1,)), ((), ()))
-    own = lax.dot_general(scaled, mine[2 * cols :], turned, preferred_element_type=F32)
-    other = lax.dot_general(scaled, theirs[2 * cols :], turned, preferred_element_type=F32)
-    first = me % 2 == 0
     high = squares.astype(BF).astype(F32)
     low = squares - high
     lane = lax.broadcasted_iota(jnp.int32, (fan * length, NS), 1)
-    whole[:, :cols] = jnp.where(first, own, other)
-    whole[:, cols : 2 * cols] = jnp.where(first, other, own)
-    whole[:, 2 * cols :] = jnp.where(lane == 0, high, jnp.where(lane == 1, low, 0.0))
+    whole[:, :cols] = lax.dot_general(
+        scaled, weights[...], (((1,), (1,)), ((), ())), preferred_element_type=F32
+    )
+    whole[:, cols:] = jnp.where(lane == 0, high, jnp.where(lane == 1, low, 0.0))
     for s, out in enumerate(outs):
-        block = (me // 2 - zed - s + 2 * fan) % fan
+        block = me // 2 ^ zed ^ s
         rows = pl.ds(pl.multiple_of(block * length, length), length)
         out[...] = whole[rows, :].astype(BF)
 
@@ -443,9 +437,7 @@
         return lax.ppermute(v, "req", [(j, j ^ 1) for j in range(reqs)])
 
     def shift(v, step):
-        return lax.ppermute(
-            v, "req", [(j, 2 * ((j // 2 + step) % fan) + j % 2) for j in range(reqs)]
-        )
+        return lax.ppermute(v, "req", [(j, j ^ 2 * step) for j in range(reqs)])
 
     share = width // fan
     wide = max(share, 2 * NS)
@@ -473,7 +465,7 @@
         *blocks, narrow, swap(narrow),
         flops=2 * fan * length * share * bc_cols, nbytes=2 * share * bc_cols,
     )
-    bc_parts = [bc_part] + [shift(bc_part, -s) for s in range(1, fan)]
+    bc_parts = [bc_part] + [shift(bc_part, s) for s in range(1, fan)]
     (
         bc_taps, bc_offset, step_bias, rate,
         x_taps, x_offset, gain, x_past, sinks_x, sinks_b, page_b_here, page_decay_here, *lists,
@@ -485,14 +477,13 @@
         ),
         bc_part,
     )
-    xz_parts = call(
+    xz_part, out_pair = call(
         functools.partial(project_xz_kernel, length, fan),
-        [sds((length, 2 * inner), BF)] * fan,
+        [sds((fan * length, 2 * inner), BF), sds((2 * half, inner), BF)],
         [vmem()] * (fan + 2),
         *blocks, xz_weight, xz_other,
         flops=4 * fan * length * share * inner, nbytes=4 * share * inner,
     )
-    xz_parts = [xz_parts[0]] + [shift(xz_parts[s], -s) for s in range(1, fan)]
     packed, bc_raw, bc_act, dtime = call(
         functools.partial(mix_bc_kernel, length, fan, heads),
         [
@@ -500,7 +491,7 @@
             sds((length, 2 * NS), BF), sds((length, 2 * NS), BF), sds((length, heads), F32),
         ],
         [vmem()] * (2 * fan + 4) + [pl.BlockSpec(memory_space=pl.ANY)],
-        *bc_parts, *blocks, bc_taps, bc_offset, step_bias, rate, xz_parts[0],
+        *bc_parts, *blocks, bc_taps, bc_offset, step_bias, rate, xz_part,
         flops=100 * length * NS, nbytes=length * NS * 20,
     )
     packed_other = swap(packed)
@@ -520,27 +511,20 @@
     )
     mine, others = call(
         halve_kernel, [sds((fan * length, inner), BF)] * 2,
-        [vmem()] + [pl.BlockSpec(memory_space=pl.ANY)] * fan, total, *xz_parts,
+        [vmem()], total,
     )
     others = swap(others)
-    local, x_raw, x_act, silu_z = call(
-        functools.partial(local_kernel, length, fan, heads),
-        [sds((length, inner), F32), sds((length, inner), BF), sds((length, inner), BF), sds((length, inner), F32)],
-        [vmem()] * (fan + 8),
-        *xz_parts, packed, bc_act, dtime, x_taps, x_offset, x_past, sinks_x, sinks_b,
-        flops=40 * length * inner, nbytes=length * inner * 8,
-    )
     parts = call(
         functools.partial(join_kernel, length),
-        [sds((length, inner), BF)] * fan, [vmem()] * 2 + [pl.BlockSpec(memory_space=pl.ANY)],
-        mine, others, local,
+        [sds((length, 3 * inner), BF)] * fan, [vmem()] * 3, mine, others, xz_part,
         flops=fan * length * inner, nbytes=fan * length * inner * 6,
     )
-    parts = [parts[0]] + [shift(parts[s], -s) for s in range(1, fan)]
-    gated = call(
-        functools.partial(gate_kernel, fan),
-        sds((length, inner), BF), [vmem()] * (fan + 2),
-        *parts, local, silu_z,
+    parts = [parts[0]] + [shift(parts[s], s) for s in range(1, fan)]
+    gated, x_raw, x_act = call(
+        functools.partial(local_kernel, length, fan, heads),
+        [sds((length, inner), BF)] * 3,
+        [vmem()] * (fan + 8),
+        *parts, packed, bc_act, dtime, x_taps, x_offset, x_past, sinks_x, sinks_b,
         flops=40 * length * inner, nbytes=length * inner * 8,
     )
 
@@ -556,15 +540,15 @@
     out_shape = sds((length, 2 * cols + NS), BF)
     out_parts = call(
         functools.partial(out_kernel, length, fan),
-        [out_shape] * fan, [vmem()] * (fan + 3),
-        *gated_all, gain, xz_weight, xz_other,
+        [out_shape] * fan, [vmem()] * (fan + 2),
+        *gated_all, gain, out_pair,
         flops=4 * fan * length * inner * cols, nbytes=4 * inner * cols,
         scratch=[pltpu.VMEM((fan * length, 2 * cols + NS), F32)],
     )
 
     def to_owner(v, step):
         moves = [
-            (f * reqs + j, (j // 2) * reqs + 2 * ((f + step) % fan) + j % 2)
+            (f * reqs + j, (j // 2) * reqs + 2 * (f ^ step) + j % 2)
             for f in range(fan)
             for j in range(reqs)
         ]
@@ -625,7 +609,7 @@
         P("req", None, None),
     )
     reqs, fan = mesh.shape["req"], mesh.shape["fsdp"]
-    assert reqs == 2 * fan
+    assert reqs == 2 * fan and fan & (fan - 1) == 0
     return jax.shard_map(
         functools.partial(per_device, reqs, fan),
         mesh=mesh, in_specs=in_specs, out_specs=out_specs, check_vma=False,

time: 58.3 us -> 57.3 us (0.983)
  waiting for transfers between devices: 13.1 us -> 19 us
  starting transfers between devices: 28.1 us -> 24.3 us
  local copies, waits for them, and re-layouts: 2.29 us -> 0.02 us
  Pallas kernels: 11.9 us -> 11.1 us
    ppermute x15 -> x12, starting transfers between devices: 18.2 us -> 15.3 us  [shift(): return lax.ppermute(v, 'req', [(j, j ^ 2 * step) for j in range(reqs)])]
    ppermute x15 -> x12, waiting for transfers between devices: 11 us -> 13.6 us  [shift(): return lax.ppermute(v, 'req', [(j, j ^ 2 * step) for j in range(reqs)])]
    unnamed x10 -> x6, local copies, waits for them, and re-layouts: 2.29 us -> 0.02 us
    ppermute x4, waiting for transfers between devices: 1.06 us -> 3 us  [to_owner(): return lax.ppermute(v, ('fsdp', 'req'), moves)]
    ppermute x4, waiting for transfers between devices: 0.99 us -> 2.48 us  [swap(): return lax.ppermute(v, 'req', [(j, j ^ 1) for j in range(reqs)])]
    ppermute x4, starting transfers between devices: 9.24 us -> 8.15 us  [to_owner(): return lax.ppermute(v, ('fsdp', 'req'), moves)]
    pallas_call x13 -> x12, Pallas kernels: 11.9 us -> 11.1 us  [call(): pl.pallas_call(body, out_shape=out_shape, in_specs=in_specs, out_specs=ja...]
  transfers between devices with their start and end apart: 23 -> 20, of which waited for: 13 -> 12; matrix products, arithmetic and copies ran while one was open for 2% -> 2% of each run, Pallas kernels for 14% -> 7%
where the time goes in v3:
time: 57.3 us; the launch traced here: 57.1 us
  starting transfers between devices  24.3 us (42%)
  waiting for transfers between devices  19 us (33%)
  Pallas kernels  11.1 us (19%)
  between operations  1.44 us (3%)
  other arithmetic  1.22 us (2%)
    ppermute x12, starting transfers between devices, shift(): return lax.ppermute(v, 'req', [(j, j ^ 2 * step) for j in range(reqs)])  15.3 us
    ppermute x12, waiting for transfers between devices, shift(): return lax.ppermute(v, 'req', [(j, j ^ 2 * step) for j in range(reqs)])  13.6 us
    pallas_call x12, Pallas kernels, call(): pl.pallas_call(body, out_shape=out_shape, in_specs=in_specs, out_specs=ja...  11.1 us
    ppermute x4, starting transfers between devices, to_owner(): return lax.ppermute(v, ('fsdp', 'req'), moves)  8.15 us
    ppermute x4, waiting for transfers between devices, to_owner(): return lax.ppermute(v, ('fsdp', 'req'), moves)  3 us
    ppermute x4, waiting for transfers between devices, swap(): return lax.ppermute(v, 'req', [(j, j ^ 1) for j in range(reqs)])  2.48 us
    broadcast_in_dim x2, other arithmetic, tail_rows(): return lax.dynamic_slice_in_dim(joined, accepted[0], KC - 1, 0)[None]  1.22 us
  transfers between devices with their start and end apart: 20, of which 12 were waited for; matrix products, arithmetic and copies ran while one was open for 2% of the time, Pallas kernels for 7%

profile of v3, /device:TPU:0, one launch (start us, length us, event | category | flops | bytes accessed | tf_op | source)
XLA Modules:
  0.0 57.1 jit_solution(2000349305814342194)
XLA Ops:
  0.6 1.9 %shard_map.273 = (bf16[32,640]{1,0:T(8,128)(2,1)S(1)}, bf16[32,640]{1,0:T(8,128)(2,1)S(1)}, bf16[32,640]{1,0:T(8,128)(2,1)S(1)}, bf16[32,640]{1,0:T(8,128)(2,1)S...) custom-call(bf16[1,16,2560]{2,1,0:T(8,128)(2,1)} %drafts_hbm.1, bf16[1,3,256]{2,1,0:T(4,128)(2,1)} %history_hbm.1, ...), custom_call_target="tpu_custom_call" | custom-call | flops 10 | bytes 81920 | tf_op jit(solution)/shard_map/pallas_call | solution.py:29
  3.1 2.9 %collective-permute-start = (bf16[32,640]{1,0:T(8,128)(2,1)S(1)}, bf16[32,640]{1,0:T(8,128)(2,1)S(1)}, u32[]{:S(2)}, u32[]{:S(2)}) collective-permute-start(bf16[32,640]{1,0:T(8,128)(2,1)S(1)} %get-tuple-element.46), channel_id=1, source_target_pairs={{0,2},{1,3},{2,0},{3,1},{4,6},{5,7},{6,4},{7,5},{8,10},{9,11},{10,... | collective-permute-start | bytes 122888 | tf_op jit(solution)/shard_map/ppermute | solution.py:440
  6.0 1.5 %collective-permute-start.1 = (bf16[32,640]{1,0:T(8,128)(2,1)S(1)}, bf16[32,640]{1,0:T(8,128)(2,1)S(1)}, u32[]{:S(2)}, u32[]{:S(2)}) collective-permute-start(bf16[32,640]{1,0:T(8,128)(2,1)S(1)} %get-tuple-element.47), channel_id=1, source_target_pairs={{0,4},{1,5},{2,6},{3,7},{4,0},{5,1},{6,2},{7,3},{8,12},{9,13},{10,... | collective-permute-start | bytes 122888 | tf_op jit(solution)/shard_map/ppermute | solution.py:440
  8.0 2.0 %collective-permute-done.1.refs_2_.refs_6_ = bf16[32,640]{1,0:T(8,128)(2,1)S(1)} collective-permute-done((bf16[32,640]{1,0:T(8,128)(2,1)S(1)}, bf16[32,640]{1,0:T(8,128)(2,1)S(1)}, u32[]{:S(2)}, u32[]{:S(2)}) %collective-permute-start.1) | collective-permute-done | bytes 40992 | tf_op jit(solution)/shard_map/ppermute | solution.py:440
  10.0 2.4 %collective-permute-done.2.refs_3_.refs_7_ = bf16[32,640]{1,0:T(8,128)(2,1)S(1)} collective-permute-done((bf16[32,640]{1,0:T(8,128)(2,1)S(1)}, bf16[32,640]{1,0:T(8,128)(2,1)S(1)}, u32[]{:S(2)}, u32[]{:S(2)}) %collective-permute-start.2) | collective-permute-done | bytes 40992 | tf_op jit(solution)/shard_map/ppermute | solution.py:440
  13.5 2.9 %collective-permute-start.6 = (bf16[64,384]{1,0:T(8,128)(2,1)S(1)}, bf16[64,384]{1,0:T(8,128)(2,1)S(1)}, u32[]{:S(2)}, u32[]{:S(2)}) collective-permute-start(bf16[64,384]{1,0:T(8,128)(2,1)S(1)} %shard_map.274.refs_16_.refs_0_), channel_id=1, source_target_pairs={{0,6},{1,7},{2,4},{3,5},{4,2},{5,3},{6,0},{7,1},{8,14},{9,15},{10,... | collective-permute-start | bytes 147464 | tf_op jit(solution)/shard_map/ppermute | solution.py:440
  16.4 1.4 %shard_map.275 = (bf16[4,256]{1,0:T(4,128)(2,1)S(1)}, bf16[256]{0:T(256)(128)(2,1)S(1)}, f32[20]{0:T(128)S(1)}, f32[20]{0:T(128)S(1)}, bf16[4,1280]{1,0:T(4,128)...) custom-call(bf16[4,256]{1,0:T(4,128)(2,1)} %refs_0_.1, ...), custom_call_target="tpu_custom_call" | custom-call | bytes 794776 | tf_op jit(solution)/shard_map/pallas_call | solution.py:29
  17.8 1.0 %shard_map.276 = (bf16[64,2560]{1,0:T(8,128)(2,1)S(1)}, bf16[640,1280]{1,0:T(8,128)(2,1)S(1)}) custom-call(bf16[32,640]{1,0:T(8,128)(2,1)S(1)} %get-tuple-element.45.refs_0_.refs_4_, bf16[32,640]{1,0:T(8,128)(2,1)S(1)} %collective-permute-done.refs_1_.refs_5_, bf16[32,640]{1,0:T(8,128)(2,1)S(1)} %collective-permute-done.1.refs_2_.refs_6_, ...), custom_call_target="tpu_custom_call" | custom-call | flops 209715200 | bytes 3276800 | tf_op jit(solution)/shard_map/pallas_call | solution.py:29
  19.1 1.2 %collective-permute-done.8.other_ref = f32[64,256]{1,0:T(8,128)S(1)} collective-permute-done((f32[64,256]{1,0:T(8,128)S(1)}, f32[64,256]{1,0:T(8,128)S(1)}, u32[]{:S(2)}, u32[]{:S(2)}) %collective-permute-start.8) | collective-permute-done | bytes 65568 | tf_op jit(solution)/shard_map/ppermute | solution.py:437
  20.3 3.0 %shard_map.278.total = f32[128,1280]{1,0:T(8,128)S(1)} custom-call(s32[10]{0:T(128)S(1)} %get-tuple-element.50.slot_req, s32[10]{0:T(128)S(1)} %get-tuple-element.51.slot_page, s32[8]{0:T(128)S(1)} %get-tuple-element.52.page_count, s32[8]{0:T(128)S(1)} %get-tuple-element.53.owner_row, f32[64,256]{1,0:T(8,128)S(1)} %get-tuple-element.60.own_ref.refs_4_.packed, ...), custom_call_target="tpu_custom_call" | custom-call | flops 419430400 | bytes 6553600 | tf_op jit(solution)/shard_map/pallas_call | solution.py:29
  23.6 1.2 %collective-permute-done.9.other = bf16[64,1280]{1,0:T(8,128)(2,1)S(1)} collective-permute-done((bf16[64,1280]{1,0:T(8,128)(2,1)S(1)}, bf16[64,1280]{1,0:T(8,128)(2,1)S(1)}, u32[]{:S(2)}, u32[]{:S(2)}) %collective-permute-start.9) | collective-permute-done | bytes 163872 | tf_op jit(solution)/shard_map/ppermute | solution.py:437
  24.9 2.1 %collective-permute-start.10 = (bf16[16,3840]{1,0:T(8,128)(2,1)S(1)}, bf16[16,3840]{1,0:T(8,128)(2,1)S(1)}, u32[]{:S(2)}, u32[]{:S(2)}) collective-permute-start(bf16[16,3840]{1,0:T(8,128)(2,1)S(1)} %get-tuple-element.66), channel_id=1, source_target_pairs={{0,2},{1,3},{2,0},{3,1},{4,6},{5,7},{6,4},{7,5},{8,10},{9,11},{10,... | collective-permute-start | bytes 368648 | tf_op jit(solution)/shard_map/ppermute | solution.py:440
  26.9 1.4 %collective-permute-start.11 = (bf16[16,3840]{1,0:T(8,128)(2,1)S(1)}, bf16[16,3840]{1,0:T(8,128)(2,1)S(1)}, u32[]{:S(2)}, u32[]{:S(2)}) collective-permute-start(bf16[16,3840]{1,0:T(8,128)(2,1)S(1)} %get-tuple-element.67), channel_id=1, source_target_pairs={{0,4},{1,5},{2,6},{3,7},{4,0},{5,1},{6,2},{7,3},{8,12},{9,13},{10,... | collective-permute-start | bytes 368648 | tf_op jit(solution)/shard_map/ppermute | solution.py:440
  29.3 1.3 %collective-permute-done.10.refs_1_ = bf16[16,3840]{1,0:T(8,128)(2,1)S(1)} collective-permute-done((bf16[16,3840]{1,0:T(8,128)(2,1)S(1)}, bf16[16,3840]{1,0:T(8,128)(2,1)S(1)}, u32[]{:S(2)}, u32[]{:S(2)}) %collective-permute-start.10) | collective-permute-done | bytes 122912 | tf_op jit(solution)/shard_map/ppermute | solution.py:440
  30.6 3.1 %collective-permute-done.11.refs_2_ = bf16[16,3840]{1,0:T(8,128)(2,1)S(1)} collective-permute-done((bf16[16,3840]{1,0:T(8,128)(2,1)S(1)}, bf16[16,3840]{1,0:T(8,128)(2,1)S(1)}, u32[]{:S(2)}, u32[]{:S(2)}) %collective-permute-start.11) | collective-permute-done | bytes 122912 | tf_op jit(solution)/shard_map/ppermute | solution.py:440
  33.7 1.1 %collective-permute-done.12.refs_3_ = bf16[16,3840]{1,0:T(8,128)(2,1)S(1)} collective-permute-done((bf16[16,3840]{1,0:T(8,128)(2,1)S(1)}, bf16[16,3840]{1,0:T(8,128)(2,1)S(1)}, u32[]{:S(2)}, u32[]{:S(2)}) %collective-permute-start.12) | collective-permute-done | bytes 122912 | tf_op jit(solution)/shard_map/ppermute | solution.py:440
  35.2 1.1 %collective-permute-start.13 = (bf16[16,1280]{1,0:T(8,128)(2,1)S(1)}, bf16[16,1280]{1,0:T(8,128)(2,1)S(1)}, u32[]{:S(2)}, u32[]{:S(2)}) collective-permute-start(bf16[16,1280]{1,0:T(8,128)(2,1)S(1)} %get-tuple-element.76.refs_0_), channel_id=1, source_target_pairs={{0,2},{1,3},{2,0},{3,1},{4,6},{5,7},{6,4},{7,5},{8,10},{9,11},{10,... | collective-permute-start | bytes 122888 | tf_op jit(solution)/shard_map/ppermute | solution.py:440
  36.3 1.2 %collective-permute-start.14 = (bf16[16,1280]{1,0:T(8,128)(2,1)S(1)}, bf16[16,1280]{1,0:T(8,128)(2,1)S(1)}, u32[]{:S(2)}, u32[]{:S(2)}) collective-permute-start(bf16[16,1280]{1,0:T(8,128)(2,1)S(1)} %get-tuple-element.76.refs_0_), channel_id=1, source_target_pairs={{0,4},{1,5},{2,6},{3,7},{4,0},{5,1},{6,2},{7,3},{8,12},{9,13},{10,... | collective-permute-start | bytes 122888 | tf_op jit(solution)/shard_map/ppermute | solution.py:440
  37.6 1.2 %collective-permute-start.15 = (bf16[16,1280]{1,0:T(8,128)(2,1)S(1)}, bf16[16,1280]{1,0:T(8,128)(2,1)S(1)}, u32[]{:S(2)}, u32[]{:S(2)}) collective-permute-start(bf16[16,1280]{1,0:T(8,128)(2,1)S(1)} %get-tuple-element.76.refs_0_), channel_id=1, source_target_pairs={{0,6},{1,7},{2,4},{3,5},{4,2},{5,3},{6,0},{7,1},{8,14},{9,15},{10,... | collective-permute-start | bytes 122888 | tf_op jit(solution)/shard_map/ppermute | solution.py:440
  38.8 0.6 %fusion.3 = bf16[1,3,256]{2,1,0:T(4,128)(2,1)} fusion(s32[]{:T(128)S(6)} %select_n.4, bf16[16,256]{1,0:T(8,128)(2,1)S(1)} %get-tuple-element.85, bf16[3,256]{1,0:T(4,128)(2,1)S(1)} %bitcast.21), kind=kLoop, calls=%fused_computation.7 | loop fusion | flops 3072 | bytes 11268 | tf_op jit(solution)/shard_map/broadcast_in_dim | solution.py:566
  39.4 1.0 %collective-permute-done.14.refs_2_ = bf16[16,1280]{1,0:T(8,128)(2,1)S(1)} collective-permute-done((bf16[16,1280]{1,0:T(8,128)(2,1)S(1)}, bf16[16,1280]{1,0:T(8,128)(2,1)S(1)}, u32[]{:S(2)}, u32[]{:S(2)}) %collective-permute-start.14) | collective-permute-done | bytes 40992 | tf_op jit(solution)/shard_map/ppermute | solution.py:440
  40.3 2.1 %collective-permute-done.15.refs_3_ = bf16[16,1280]{1,0:T(8,128)(2,1)S(1)} collective-permute-done((bf16[16,1280]{1,0:T(8,128)(2,1)S(1)}, bf16[16,1280]{1,0:T(8,128)(2,1)S(1)}, u32[]{:S(2)}, u32[]{:S(2)}) %collective-permute-start.15) | collective-permute-done | bytes 40992 | tf_op jit(solution)/shard_map/ppermute | solution.py:440
  42.5 0.6 %shard_map.282 = (bf16[16,768]{1,0:T(8,128)(2,1)S(1)}, bf16[16,768]{1,0:T(8,128)(2,1)S(1)}, bf16[16,768]{1,0:T(8,128)(2,1)S(1)}, bf16[16,768]{1,0:T(8,128)(2,1)S(1)}) custom-call(bf16[16,1280]{1,0:T(8,128)(2,1)S(1)} %get-tuple-element.76.refs_0_, bf16[16,1280]{1,0:T(8,128)(2,1)S(1)} %collective-permute-done.13.refs_1_, ...), custom_call_target="tpu_custom_call" | custom-call | flops 104857600 | bytes 1638400 | tf_op jit(solution)/shard_map/pallas_call | solution.py:29
  43.1 0.7 %collective-permute-start.16 = (bf16[16,768]{1,0:T(8,128)(2,1)S(1)}, bf16[16,768]{1,0:T(8,128)(2,1)S(1)}, u32[]{:S(2)}, u32[]{:S(2)}) collective-permute-start(bf16[16,768]{1,0:T(8,128)(2,1)S(1)} %get-tuple-element.79), channel_id=1, source_target_pairs={{0,0},{1,1},{2,8},{3,9},{4,16},{5,17},{6,24},{7,25},{8,2},{9,3},{1... | collective-permute-start | bytes 73736 | tf_op jit(solution)/shard_map/ppermute | solution.py:555
  43.8 4.3 %collective-permute-start.17 = (bf16[16,768]{1,0:T(8,128)(2,1)S(1)}, bf16[16,768]{1,0:T(8,128)(2,1)S(1)}, u32[]{:S(2)}, u32[]{:S(2)}) collective-permute-start(bf16[16,768]{1,0:T(8,128)(2,1)S(1)} %get-tuple-element.80), channel_id=1, source_target_pairs={{0,2},{1,3},{2,10},{3,11},{4,18},{5,19},{6,26},{7,27},{8,0},{9,1},... | collective-permute-start | bytes 73736 | tf_op jit(solution)/shard_map/ppermute | solution.py:555
  48.1 2.6 %collective-permute-start.18 = (bf16[16,768]{1,0:T(8,128)(2,1)S(1)}, bf16[16,768]{1,0:T(8,128)(2,1)S(1)}, u32[]{:S(2)}, u32[]{:S(2)}) collective-permute-start(bf16[16,768]{1,0:T(8,128)(2,1)S(1)} %get-tuple-element.81), channel_id=1, source_target_pairs={{0,4},{1,5},{2,12},{3,13},{4,20},{5,21},{6,28},{7,29},{8,6},{9,7},... | collective-permute-start | bytes 73736 | tf_op jit(solution)/shard_map/ppermute | solution.py:555
  50.7 0.6 collective-permute-start.19
  51.3 0.6 %fusion.1 = bf16[1,3,1280]{2,1,0:T(4,128)(2,1)} fusion(s32[]{:T(128)S(6)} %select_n.4, bf16[16,1280]{1,0:T(8,128)(2,1)S(1)} %get-tuple-element.84, bf16[3,1280]{1,0:T(4,128)(2,1)S(1)} %bitcast.18), kind=kLoop, calls=%fused_computation.5 | loop fusion | flops 15360 | bytes 56324 | tf_op jit(solution)/shard_map/broadcast_in_dim | solution.py:566
  51.9 1.4 %shard_map.284 = f32[20,64,128]{2,1,0:T(8,128)} custom-call(s32[1]{0:T(128)} %copy.30.accepted, f32[64,256]{1,0:T(8,128)S(1)} %get-tuple-element.60.own_ref.refs_4_.packed, f32[16,20]{1,0:T(8,128)S(1)} %get-tuple-element.70.refs_6_.dtime_ref, bf16[16,1280]{1,0:T(8,128)(2,1)S(1)} %get-tuple-element.83.x_act, ...), custom_call_target="tpu_custom_call" | custom-call | flops 10485760 | bytes 1310720 | tf_op jit(solution)/shard_map/pallas_call | solution.py:29
  53.4 2.2 %collective-permute-done.18.refs_2_ = bf16[16,768]{1,0:T(8,128)(2,1)S(1)} collective-permute-done((bf16[16,768]{1,0:T(8,128)(2,1)S(1)}, bf16[16,768]{1,0:T(8,128)(2,1)S(1)}, u32[]{:S(2)}, u32[]{:S(2)}) %collective-permute-start.18) | collective-permute-done | bytes 24608 | tf_op jit(solution)/shard_map/ppermute | solution.py:555
  55.5 0.8 %collective-permute-done.19.refs_3_ = bf16[16,768]{1,0:T(8,128)(2,1)S(1)} collective-permute-done((bf16[16,768]{1,0:T(8,128)(2,1)S(1)}, bf16[16,768]{1,0:T(8,128)(2,1)S(1)}, u32[]{:S(2)}, u32[]{:S(2)}) %collective-permute-start.19) | collective-permute-done | bytes 24608 | tf_op jit(solution)/shard_map/ppermute | solution.py:555
  56.4 0.8 %shard_map.283 = bf16[16,640]{1,0:T(8,128)(2,1)} custom-call(bf16[16,768]{1,0:T(8,128)(2,1)S(1)} %collective-permute-done.16.refs_0_, bf16[16,768]{1,0:T(8,128)(2,1)S(1)} %collective-permute-done.17.refs_1_, bf16[16,768]{1,0:T(8,128)(2,1)S(1)} %collective-permute-done.18.refs_2_, bf16[16,768]{1,0:T(8,128)(2,1)S(1)} %collective-permute-done.19.refs_3_), custom_call_target="tpu_custom_call" | custom-call | flops 51200 | bytes 51200 | tf_op jit(solution)/shard_map/pallas_call | solution.py:29
  (28 shorter events, 3.4 us)
Async XLA Ops:
  2.5 15.3 %collective-permute-start.7 = (bf16[960,1280]{1,0:T(8,128)(2,1)S(1)}, bf16[960,1280]{1,0:T(8,128)(2,1)S(1)}, u32[]{:S(2)}, u32[]{:S(2)}) collective-permute-start(bf16[960,1280]{1,0:T(8,128)(2,1)S(1)} %get-tuple-element.58.refs_4_), channel_id=1, source_target_pairs={{0,1},{1,0},{2,3},{3,2},{4,5},{5,4},{6,7},{7,6},{8,9},{9,8},{10,11... | collective-permute-start | bytes 7372808 | tf_op jit(solution)/shard_map/ppermute | solution.py:437
  3.0 9.4 %collective-permute-start.3 = (bf16[352,384]{1,0:T(8,128)(2,1)S(1)}, bf16[352,384]{1,0:T(8,128)(2,1)S(1)}, u32[]{:S(2)}, u32[]{:S(2)}) collective-permute-start(bf16[352,384]{1,0:T(8,128)(2,1)S(1)} %get-tuple-element.49.refs_4_), channel_id=1, source_target_pairs={{0,1},{1,0},{2,3},{3,2},{4,5},{5,4},{6,7},{7,6},{8,9},{9,8},{10,11... | collective-permute-start | bytes 811016 | tf_op jit(solution)/shard_map/ppermute | solution.py:437
  3.1 4.9 %collective-permute-start = (bf16[32,640]{1,0:T(8,128)(2,1)S(1)}, bf16[32,640]{1,0:T(8,128)(2,1)S(1)}, u32[]{:S(2)}, u32[]{:S(2)}) collective-permute-start(bf16[32,640]{1,0:T(8,128)(2,1)S(1)} %get-tuple-element.46), channel_id=1, source_target_pairs={{0,2},{1,3},{2,0},{3,1},{4,6},{5,7},{6,4},{7,5},{8,10},{9,11},{10,... | collective-permute-start | bytes 122888 | tf_op jit(solution)/shard_map/ppermute | solution.py:440
  6.0 4.0 %collective-permute-start.1 = (bf16[32,640]{1,0:T(8,128)(2,1)S(1)}, bf16[32,640]{1,0:T(8,128)(2,1)S(1)}, u32[]{:S(2)}, u32[]{:S(2)}) collective-permute-start(bf16[32,640]{1,0:T(8,128)(2,1)S(1)} %get-tuple-element.47), channel_id=1, source_target_pairs={{0,4},{1,5},{2,6},{3,7},{4,0},{5,1},{6,2},{7,3},{8,12},{9,13},{10,... | collective-permute-start | bytes 122888 | tf_op jit(solution)/shard_map/ppermute | solution.py:440
  7.5 4.9 %collective-permute-start.2 = (bf16[32,640]{1,0:T(8,128)(2,1)S(1)}, bf16[32,640]{1,0:T(8,128)(2,1)S(1)}, u32[]{:S(2)}, u32[]{:S(2)}) collective-permute-start(bf16[32,640]{1,0:T(8,128)(2,1)S(1)} %get-tuple-element.48), channel_id=1, source_target_pairs={{0,6},{1,7},{2,4},{3,5},{4,2},{5,3},{6,0},{7,1},{8,14},{9,15},{10,... | collective-permute-start | bytes 122888 | tf_op jit(solution)/shard_map/ppermute | solution.py:440
  12.9 5.9 %collective-permute-start.4 = (bf16[64,384]{1,0:T(8,128)(2,1)S(1)}, bf16[64,384]{1,0:T(8,128)(2,1)S(1)}, u32[]{:S(2)}, u32[]{:S(2)}) collective-permute-start(bf16[64,384]{1,0:T(8,128)(2,1)S(1)} %shard_map.274.refs_16_.refs_0_), channel_id=1, source_target_pairs={{0,2},{1,3},{2,0},{3,1},{4,6},{5,7},{6,4},{7,5},{8,10},{9,11},{10,... | collective-permute-start | bytes 147464 | tf_op jit(solution)/shard_map/ppermute | solution.py:440
  13.4 5.4 %collective-permute-start.5 = (bf16[64,384]{1,0:T(8,128)(2,1)S(1)}, bf16[64,384]{1,0:T(8,128)(2,1)S(1)}, u32[]{:S(2)}, u32[]{:S(2)}) collective-permute-start(bf16[64,384]{1,0:T(8,128)(2,1)S(1)} %shard_map.274.refs_16_.refs_0_), channel_id=1, source_target_pairs={{0,4},{1,5},{2,6},{3,7},{4,0},{5,1},{6,2},{7,3},{8,12},{9,13},{10,... | collective-permute-start | bytes 147464 | tf_op jit(solution)/shard_map/ppermute | solution.py:440
  13.5 5.3 %collective-permute-start.6 = (bf16[64,384]{1,0:T(8,128)(2,1)S(1)}, bf16[64,384]{1,0:T(8,128)(2,1)S(1)}, u32[]{:S(2)}, u32[]{:S(2)}) collective-permute-start(bf16[64,384]{1,0:T(8,128)(2,1)S(1)} %shard_map.274.refs_16_.refs_0_), channel_id=1, source_target_pairs={{0,6},{1,7},{2,4},{3,5},{4,2},{5,3},{6,0},{7,1},{8,14},{9,15},{10,... | collective-permute-start | bytes 147464 | tf_op jit(solution)/shard_map/ppermute | solution.py:440
  19.0 1.3 %collective-permute-start.8 = (f32[64,256]{1,0:T(8,128)S(1)}, f32[64,256]{1,0:T(8,128)S(1)}, u32[]{:S(2)}, u32[]{:S(2)}) collective-permute-start(f32[64,256]{1,0:T(8,128)S(1)} %get-tuple-element.60.own_ref.refs_4_.packed), channel_id=1, source_target_pairs={{0,1},{1,0},{2,3},{3,2},{4,5},{5,4},{6,7},{7,6},{8,9},{9,8},{10,11... | collective-permute-start | bytes 196616 | tf_op jit(solution)/shard_map/ppermute | solution.py:437
  20.3 18.5 %copy-start.2 = (bf16[1,3,256]{2,1,0:T(4,128)(2,1)S(1)}, bf16[1,3,256]{2,1,0:T(4,128)(2,1)}, u32[]{:S(2)}) copy-start(bf16[1,3,256]{2,1,0:T(4,128)(2,1)} %history_hbm.1) | copy-start | bytes 4612
  23.3 28.0 %copy-start.1 = (bf16[1,3,1280]{2,1,0:T(4,128)(2,1)S(1)}, bf16[1,3,1280]{2,1,0:T(4,128)(2,1)}, u32[]{:S(2)}) copy-start(bf16[1,3,1280]{2,1,0:T(4,128)(2,1)} %refs_7_.1) | copy-start | bytes 23044
  23.3 28.6 %copy-start = (f32[1,20,64,128]{3,2,1,0:T(8,128)S(1)}, f32[1,20,64,128]{3,2,1,0:T(8,128)}, u32[]{:S(2)}) copy-start(f32[1,20,64,128]{3,2,1,0:T(8,128)} %param.41) | copy-start | bytes 1966084
  23.3 1.5 %collective-permute-start.9 = (bf16[64,1280]{1,0:T(8,128)(2,1)S(1)}, bf16[64,1280]{1,0:T(8,128)(2,1)S(1)}, u32[]{:S(2)}, u32[]{:S(2)}) collective-permute-start(bf16[64,1280]{1,0:T(8,128)(2,1)S(1)} %get-tuple-element.64), channel_id=1, source_target_pairs={{0,1},{1,0},{2,3},{3,2},{4,5},{5,4},{6,7},{7,6},{8,9},{9,8},{10,11... | collective-permute-start | bytes 491528 | tf_op jit(solution)/shard_map/ppermute | solution.py:437
  24.9 5.8 %collective-permute-start.10 = (bf16[16,3840]{1,0:T(8,128)(2,1)S(1)}, bf16[16,3840]{1,0:T(8,128)(2,1)S(1)}, u32[]{:S(2)}, u32[]{:S(2)}) collective-permute-start(bf16[16,3840]{1,0:T(8,128)(2,1)S(1)} %get-tuple-element.66), channel_id=1, source_target_pairs={{0,2},{1,3},{2,0},{3,1},{4,6},{5,7},{6,4},{7,5},{8,10},{9,11},{10,... | collective-permute-start | bytes 368648 | tf_op jit(solution)/shard_map/ppermute | solution.py:440
  26.9 6.8 %collective-permute-start.11 = (bf16[16,3840]{1,0:T(8,128)(2,1)S(1)}, bf16[16,3840]{1,0:T(8,128)(2,1)S(1)}, u32[]{:S(2)}, u32[]{:S(2)}) collective-permute-start(bf16[16,3840]{1,0:T(8,128)(2,1)S(1)} %get-tuple-element.67), channel_id=1, source_target_pairs={{0,4},{1,5},{2,6},{3,7},{4,0},{5,1},{6,2},{7,3},{8,12},{9,13},{10,... | collective-permute-start | bytes 368648 | tf_op jit(solution)/shard_map/ppermute | solution.py:440
  28.3 6.5 %collective-permute-start.12 = (bf16[16,3840]{1,0:T(8,128)(2,1)S(1)}, bf16[16,3840]{1,0:T(8,128)(2,1)S(1)}, u32[]{:S(2)}, u32[]{:S(2)}) collective-permute-start(bf16[16,3840]{1,0:T(8,128)(2,1)S(1)} %get-tuple-element.68), channel_id=1, source_target_pairs={{0,6},{1,7},{2,4},{3,5},{4,2},{5,3},{6,0},{7,1},{8,14},{9,15},{10,... | collective-permute-start | bytes 368648 | tf_op jit(solution)/shard_map/ppermute | solution.py:440
  35.2 4.2 %collective-permute-start.13 = (bf16[16,1280]{1,0:T(8,128)(2,1)S(1)}, bf16[16,1280]{1,0:T(8,128)(2,1)S(1)}, u32[]{:S(2)}, u32[]{:S(2)}) collective-permute-start(bf16[16,1280]{1,0:T(8,128)(2,1)S(1)} %get-tuple-element.76.refs_0_), channel_id=1, source_target_pairs={{0,2},{1,3},{2,0},{3,1},{4,6},{5,7},{6,4},{7,5},{8,10},{9,11},{10,... | collective-permute-start | bytes 122888 | tf_op jit(solution)/shard_map/ppermute | solution.py:440
  36.3 4.0 %collective-permute-start.14 = (bf16[16,1280]{1,0:T(8,128)(2,1)S(1)}, bf16[16,1280]{1,0:T(8,128)(2,1)S(1)}, u32[]{:S(2)}, u32[]{:S(2)}) collective-permute-start(bf16[16,1280]{1,0:T(8,128)(2,1)S(1)} %get-tuple-element.76.refs_0_), channel_id=1, source_target_pairs={{0,4},{1,5},{2,6},{3,7},{4,0},{5,1},{6,2},{7,3},{8,12},{9,13},{10,... | collective-permute-start | bytes 122888 | tf_op jit(solution)/shard_map/ppermute | solution.py:440
  37.6 4.9 %collective-permute-start.15 = (bf16[16,1280]{1,0:T(8,128)(2,1)S(1)}, bf16[16,1280]{1,0:T(8,128)(2,1)S(1)}, u32[]{:S(2)}, u32[]{:S(2)}) collective-permute-start(bf16[16,1280]{1,0:T(8,128)(2,1)S(1)} %get-tuple-element.76.refs_0_), channel_id=1, source_target_pairs={{0,6},{1,7},{2,4},{3,5},{4,2},{5,3},{6,0},{7,1},{8,14},{9,15},{10,... | collective-permute-start | bytes 122888 | tf_op jit(solution)/shard_map/ppermute | solution.py:440
  43.1 10.2 %collective-permute-start.16 = (bf16[16,768]{1,0:T(8,128)(2,1)S(1)}, bf16[16,768]{1,0:T(8,128)(2,1)S(1)}, u32[]{:S(2)}, u32[]{:S(2)}) collective-permute-start(bf16[16,768]{1,0:T(8,128)(2,1)S(1)} %get-tuple-element.79), channel_id=1, source_target_pairs={{0,0},{1,1},{2,8},{3,9},{4,16},{5,17},{6,24},{7,25},{8,2},{9,3},{1... | collective-permute-start | bytes 73736 | tf_op jit(solution)/shard_map/ppermute | solution.py:555
  43.8 9.6 %collective-permute-start.17 = (bf16[16,768]{1,0:T(8,128)(2,1)S(1)}, bf16[16,768]{1,0:T(8,128)(2,1)S(1)}, u32[]{:S(2)}, u32[]{:S(2)}) collective-permute-start(bf16[16,768]{1,0:T(8,128)(2,1)S(1)} %get-tuple-element.80), channel_id=1, source_target_pairs={{0,2},{1,3},{2,10},{3,11},{4,18},{5,19},{6,26},{7,27},{8,0},{9,1},... | collective-permute-start | bytes 73736 | tf_op jit(solution)/shard_map/ppermute | solution.py:555
  48.1 7.4 %collective-permute-start.18 = (bf16[16,768]{1,0:T(8,128)(2,1)S(1)}, bf16[16,768]{1,0:T(8,128)(2,1)S(1)}, u32[]{:S(2)}, u32[]{:S(2)}) collective-permute-start(bf16[16,768]{1,0:T(8,128)(2,1)S(1)} %get-tuple-element.81), channel_id=1, source_target_pairs={{0,4},{1,5},{2,12},{3,13},{4,20},{5,21},{6,28},{7,29},{8,6},{9,7},... | collective-permute-start | bytes 73736 | tf_op jit(solution)/shard_map/ppermute | solution.py:555
  50.7 5.6 %collective-permute-start.19 = (bf16[16,768]{1,0:T(8,128)(2,1)S(1)}, bf16[16,768]{1,0:T(8,128)(2,1)S(1)}, u32[]{:S(2)}, u32[]{:S(2)}) collective-permute-start(bf16[16,768]{1,0:T(8,128)(2,1)S(1)} %get-tuple-element.82), channel_id=1, source_target_pairs={{0,6},{1,7},{2,14},{3,15},{4,22},{5,23},{6,30},{7,31},{8,4},{9,5},... | collective-permute-start | bytes 73736 | tf_op jit(solution)/shard_map/ppermute | solution.py:555

commit v4 on v3

--- a/solution.py
+++ b/solution.py
@@ -47,6 +47,10 @@
 
 def sds(shape, dtype):
     return jax.ShapeDtypeStruct(shape, dtype)
+
+
+def by_pair(refs):
+    return [refs[0]] + list(reversed(refs[1:]))
 
 
 def silu(v):
@@ -89,7 +93,10 @@
 
 
 def draft_kernel(fan, share, drafts_hbm, history_hbm, bc_hbm, dt_hbm, x_hbm, z_hbm, out_hbm, *refs):
-    outs, (narrow_out, xz_out, drafts, history, steps, sems) = refs[:fan], refs[fan:]
+    lists_hbm, refs = refs[:4], refs[4:]
+    outs, lists = refs[:fan], refs[fan + 2 : fan + 6]
+    narrow_out, xz_out = refs[fan : fan + 2]
+    drafts, history, steps, sems = refs[fan + 6 :]
     half, heads = bc_hbm.shape[0], steps.shape[0]
     copies = [
         pltpu.make_async_copy(source, target, sems.at[i])
@@ -98,7 +105,7 @@
                 (drafts_hbm, drafts), (history_hbm, history), (dt_hbm, steps),
                 (bc_hbm, narrow_out.at[0:half, 0 : 2 * NS]),
                 (x_hbm, xz_out.at[0:half]), (z_hbm, xz_out.at[half : 2 * half]),
-                (out_hbm, xz_out.at[2 * half : 3 * half]),
+                (out_hbm, xz_out.at[2 * half : 3 * half]), *zip(lists_hbm, lists),
             )
         )
     ]
@@ -157,8 +164,8 @@
 
 
 def project_bc_kernel(length, fan, half, heads, *refs):
-    blocks = refs[:fan]
-    mine, theirs, out = refs[fan:]
+    blocks = by_pair(refs[:fan])
+    mine, theirs, _, out = refs[fan:]
     own, other = own_and_other(length, half, blocks)
     bc = jnp.dot(own, mine[:half, : 2 * NS], preferred_element_type=F32) + jnp.dot(
         other, theirs[:half, : 2 * NS], preferred_element_type=F32
@@ -176,7 +183,7 @@
 
 
 def project_xz_kernel(length, fan, *refs):
-    blocks = refs[:fan]
+    blocks = by_pair(refs[:fan])
     mine, theirs = refs[fan : fan + 2]
     out, out_pair = refs[fan + 2 :]
     half, inner = mine.shape[0] // 3, mine.shape[1]
@@ -194,8 +201,8 @@
 
 
 def mix_bc_kernel(length, fan, heads, *refs):
-    parts = refs[:fan]
-    blocks = refs[fan : 2 * fan]
+    parts = by_pair(refs[:fan])
+    blocks = by_pair(refs[fan : 2 * fan])
     taps_ref, offset_ref, bias_ref, rate_ref = refs[2 * fan : 2 * fan + 4]
     packed, bc_raw_o, bc_act_o, dtime_o = refs[2 * fan + 5 :]
     taps, offset = taps_ref[...].astype(F32), offset_ref[...].astype(F32)[None]
@@ -222,52 +229,29 @@
             dtime_o[...] = dtime
 
 
-def page_kernel(
-    length, heads, slot_req, slot_page, page_count, owner_row,
-    own_ref, other_ref, b_ref, decay_ref, x_hbm, total,
-    query, pages, order, scores_ref, sems,
-):
-    slots = x_hbm.shape[0]
-    half = own_ref.shape[0]
-    fan = half // length
-    me = lax.axis_index("req")
-
-    def request(s):
-        return jnp.maximum(slot_req[s], 0)
-
-    def copy(s):
-        return pltpu.make_async_copy(x_hbm.at[s], pages.at[s], sems.at[s])
-
-    def place(s):
-        row = owner_row[request(s)]
-        away = jnp.where(row % 2 == me % 2, 0, fan)
-        return (away + (me // 2 ^ row // 2)) * length
-
-    count = jnp.int32(0)
+def is_live(s, slot_req, slot_page, page_count):
+    return (slot_req[s] >= 0) & (slot_page[s] < page_count[jnp.maximum(slot_req[s], 0)])
+
+
+def page_terms(chosen, lists, heads, packed, b_ref, decay_ref, pages, total, order, scores_ref):
+    slots, length = scores_ref.shape[:2]
+    pair = lax.axis_index("req") // 2
+    slot_req, _, _, owner_row = lists
+
+    def rows_of(s):
+        row = owner_row[jnp.maximum(slot_req[s], 0)]
+        return pl.ds(pl.multiple_of((pair ^ row // 2) * length, length), length)
+
     for s in range(slots):
-        live = (slot_req[s] >= 0) & (slot_page[s] < page_count[request(s)])
-
-        @pl.when(live)
-        def _():
-            copy(s).start()
-            order[count] = s
-
-        count = count + live.astype(jnp.int32)
-
-    query[0:half] = own_ref[...]
-    query[half:] = other_ref[...]
-    total[...] = jnp.zeros_like(total)
-    for s in range(slots):
-        at = pl.ds(pl.multiple_of(place(s), length), length)
         scores_ref[s] = lax.dot_general(
-            query[at, :NS].astype(BF), b_ref[s], (((1,), (1,)), ((), ())),
+            packed[rows_of(s), :NS].astype(BF), b_ref[s], (((1,), (1,)), ((), ())),
             preferred_element_type=F32,
         )
 
     def visit(s):
-        rows = pl.ds(pl.multiple_of(place(s), length), length)
+        rows = rows_of(s)
         scores = scores_ref[s]
-        cumul = query[rows, NS:]
+        cumul = packed[rows, NS:]
         decay = decay_ref[s]
         terms = []
         for first in range(0, heads, 4):
@@ -287,27 +271,77 @@
             first += term.shape[1]
 
     def two(i, carry):
-        one, other = order[2 * i], order[2 * i + 1]
-        copy(one).wait()
-        copy(other).wait()
-        first, second = visit(one), visit(other)
-        add(*first)
-        add(*second)
+        one, other = visit(order[2 * i]), visit(order[2 * i + 1])
+        add(*one)
+        add(*other)
         return carry
 
-    lax.fori_loop(0, count // 2, two, 0)
-
-    @pl.when(count % 2 == 1)
+    lax.fori_loop(0, chosen // 2, two, 0)
+
+    @pl.when(chosen % 2 == 1)
     def _():
-        s = order[count - 1]
-        copy(s).wait()
-        add(*visit(s))
-
-
-def halve_kernel(total, mine, other):
-    half = mine.shape[0]
-    mine[...] = total[0:half].astype(BF)
-    other[...] = total[half:].astype(BF)
+        add(*visit(order[chosen - 1]))
+
+
+def choose(slots, lists, own, order):
+    slot_req, slot_page, page_count, owner_row = lists
+    side = lax.axis_index("req") % 2
+    count = jnp.int32(0)
+    for s in slots:
+        row = owner_row[jnp.maximum(slot_req[s], 0)]
+        wanted = is_live(s, slot_req, slot_page, page_count) & ((row % 2 == side) == own)
+
+        @pl.when(wanted)
+        def _():
+            order[count] = s
+
+        count = count + wanted.astype(jnp.int32)
+    return count
+
+
+def fetch_kernel(req, slot, count, x_hbm, _, pages, sems):
+    for s in range(x_hbm.shape[0]):
+        @pl.when(is_live(s, req, slot, count))
+        def _():
+            pltpu.make_async_copy(x_hbm.at[s], pages.at[s], sems.at[s]).start()
+
+    for s in range(x_hbm.shape[0]):
+        @pl.when(is_live(s, req, slot, count))
+        def _():
+            pltpu.make_async_copy(x_hbm.at[s], pages.at[s], sems.at[s]).wait()
+
+
+def first_pages_kernel(
+    heads, slot_req, slot_page, page_count, owner_row, packed, b_ref, decay_ref, pages,
+    total, order, scores_ref,
+):
+    lists = (slot_req, slot_page, page_count, owner_row)
+    count = choose(range(pages.shape[0] // 2), lists, True, order)
+    total[...] = jnp.zeros_like(total)
+    page_terms(count, lists, heads, packed, b_ref, decay_ref, pages, total, order, scores_ref)
+
+
+def other_pages_kernel(
+    heads, slot_req, slot_page, page_count, owner_row, packed, b_ref, decay_ref, pages, _,
+    out, total, order, scores_ref,
+):
+    lists = (slot_req, slot_page, page_count, owner_row)
+    count = choose(range(pages.shape[0]), lists, False, order)
+    total[...] = jnp.zeros_like(total)
+    page_terms(count, lists, heads, packed, b_ref, decay_ref, pages, total, order, scores_ref)
+    out[...] = total[...].astype(BF)
+
+
+def last_pages_kernel(
+    heads, slot_req, slot_page, page_count, owner_row, packed, b_ref, decay_ref, pages, begun,
+    out, total, order, scores_ref,
+):
+    lists = (slot_req, slot_page, page_count, owner_row)
+    slots = pages.shape[0]
+    count = choose(range(slots // 2, slots), lists, True, order)
+    total[...] = begun[...]
+    page_terms(count, lists, heads, packed, b_ref, decay_ref, pages, total, order, scores_ref)
+    out[...] = total[...].astype(BF)
 
 
 def join_kernel(length, mine, other, xz, *outs):
@@ -390,7 +424,7 @@
 
 
 def out_kernel(length, fan, *refs):
-    blocks = refs[:fan]
+    blocks = by_pair(refs[:fan])
     gain, weights = refs[fan : fan + 2]
     outs = refs[fan + 2 : 2 * fan + 2]
     whole = refs[2 * fan + 2]
@@ -439,41 +473,52 @@
     def shift(v, step):
         return lax.ppermute(v, "req", [(j, j ^ 2 * step) for j in range(reqs)])
 
+    def exchange(own, messages):
+        return [own] + [shift(messages[s], s) for s in reversed(range(1, fan))]
+
     share = width // fan
     wide = max(share, 2 * NS)
     dt_turned = dt_weight.T
     half = x_weight.shape[0]
-    *blocks, narrow, xz_weight = call(
+    places = (slot_req, slot_page, page_count, owner_row)
+    packs = call(
         functools.partial(draft_kernel, fan, share),
         [sds((2 * length, wide), BF)] * fan
-        + [sds((half + 2 * length, max(2 * NS, -(-half // 128) * 128)), BF), sds((3 * half, inner), BF)],
-        [hbm()] * 7,
-        *[in_hbm(v) for v in (drafts, conv_bc_state, bc_weight, dt_turned, x_weight, z_weight, out_weight.T)],
+        + [sds((half + 2 * length, max(2 * NS, -(-half // 128) * 128)), BF), sds((3 * half, inner), BF)]
+        + [sds(v.shape, v.dtype) for v in places],
+        [hbm()] * 11,
+        *[in_hbm(v) for v in (drafts, conv_bc_state, bc_weight, dt_turned, x_weight, z_weight, out_weight.T) + places],
         flops=10, nbytes=2 * length * width,
         scratch=[
             pltpu.VMEM(drafts.shape, BF), pltpu.VMEM(conv_bc_state.shape, BF),
-            pltpu.VMEM(dt_turned.shape, BF), pltpu.SemaphoreType.DMA((7,)),
+            pltpu.VMEM(dt_turned.shape, BF), pltpu.SemaphoreType.DMA((11,)),
         ],
     )
-    blocks = [blocks[0]] + [shift(blocks[s], s) for s in range(1, fan)]
-
+    blocks, (narrow, xz_weight), lists = packs[:fan], packs[fan : fan + 2], packs[fan + 2 :]
+    blocks = exchange(blocks[0], blocks)
+    pages = call(
+        fetch_kernel, sds(page_x.shape, BF),
+        [smem()] * 3 + [hbm(), pl.BlockSpec(memory_space=pl.ANY)],
+        *lists[:3], in_hbm(page_x), blocks[3],
+        nbytes=2 * page_x.size, scratch=[pltpu.SemaphoreType.DMA((slots,))],
+    )
     xz_other = swap(xz_weight)
     bc_cols = 2 * NS + heads
     bc_part = call(
         functools.partial(project_bc_kernel, length, fan, x_weight.shape[0], heads),
-        sds((fan * length, BCW), BF), [vmem()] * (fan + 2),
-        *blocks, narrow, swap(narrow),
+        sds((fan * length, BCW), BF), [vmem()] * (fan + 2) + [pl.BlockSpec(memory_space=pl.ANY)],
+        *blocks, narrow, swap(narrow), pages,
         flops=2 * fan * length * share * bc_cols, nbytes=2 * share * bc_cols,
     )
-    bc_parts = [bc_part] + [shift(bc_part, s) for s in range(1, fan)]
+    bc_parts = exchange(bc_part, [bc_part] * fan)
     (
         bc_taps, bc_offset, step_bias, rate,
-        x_taps, x_offset, gain, x_past, sinks_x, sinks_b, page_b_here, page_decay_here, *lists,
+        x_taps, x_offset, gain, x_past, sinks_x, sinks_b, page_b_here, page_decay_here,
     ) = stage(
         (
             conv_bc_weight, conv_bc_bias, dt_bias,
             decay_rate, conv_x_weight, conv_x_bias, norm_gain, conv_x_state, sink_x, sink_b,
-            page_b, page_decay, slot_req, slot_page, page_count, owner_row,
+            page_b, page_decay,
         ),
         bc_part,
     )
@@ -496,30 +541,37 @@
     )
     packed_other = swap(packed)
 
-    total = call(
-        functools.partial(page_kernel, length, heads),
-        sds((2 * fan * length, inner), F32), [smem()] * 4 + [vmem()] * 4 + [hbm()],
-        *lists, packed, packed_other, page_b_here, page_decay_here, in_hbm(page_x),
-        flops=8 * slots * length * page_x.shape[1] * inner, nbytes=2 * page_x.size,
-        scratch=[
-            pltpu.VMEM((2 * fan * length, 2 * NS), F32),
-            pltpu.VMEM(page_x.shape, BF),
-            pltpu.SMEM((slots,), jnp.int32),
-            pltpu.VMEM((slots, length, page_x.shape[1]), F32),
-            pltpu.SemaphoreType.DMA((slots,)),
-        ],
-    )
-    mine, others = call(
-        halve_kernel, [sds((fan * length, inner), BF)] * 2,
-        [vmem()], total,
+    whole = sds((fan * length, inner), F32)
+    scratch = [pltpu.SMEM((slots,), jnp.int32), pltpu.VMEM((slots, length, page_x.shape[1]), F32)]
+    half_out = sds((fan * length, inner), BF)
+    begun = call(
+        functools.partial(first_pages_kernel, heads),
+        whole, [smem()] * 4 + [vmem()] * 4,
+        *lists, packed, page_b_here, page_decay_here, pages,
+        flops=2 * slots * length * page_x.shape[1] * inner, nbytes=2 * page_x.size,
+        scratch=scratch,
+    )
+    others = call(
+        functools.partial(other_pages_kernel, heads),
+        half_out, [smem()] * 4 + [vmem()] * 4 + [pl.BlockSpec(memory_space=pl.ANY)],
+        *lists, packed_other, page_b_here, page_decay_here, pages, begun,
+        flops=4 * slots * length * page_x.shape[1] * inner, nbytes=2 * page_x.size,
+        scratch=[pltpu.VMEM(whole.shape, F32)] + scratch,
     )
     others = swap(others)
+    mine = call(
+        functools.partial(last_pages_kernel, heads),
+        half_out, [smem()] * 4 + [vmem()] * 5,
+        *lists, packed, page_b_here, page_decay_here, pages, begun,
+        flops=2 * slots * length * page_x.shape[1] * inner, nbytes=2 * page_x.size,
+        scratch=[pltpu.VMEM(whole.shape, F32)] + scratch,
+    )
     parts = call(
         functools.partial(join_kernel, length),
         [sds((length, 3 * inner), BF)] * fan, [vmem()] * 3, mine, others, xz_part,
         flops=fan * length * inner, nbytes=fan * length * inner * 6,
     )
-    parts = [parts[0]] + [shift(parts[s], s) for s in range(1, fan)]
+    parts = exchange(parts[0], parts)
     gated, x_raw, x_act = call(
         functools.partial(local_kernel, length, fan, heads),
         [sds((length, inner), BF)] * 3,
@@ -528,7 +580,7 @@
         flops=40 * length * inner, nbytes=length * inner * 8,
     )
 
-    gated_all = [gated] + [shift(gated, s) for s in range(1, fan)]
+    gated_all = exchange(gated, [gated] * fan)
     new_state = call(
         functools.partial(state_kernel, length, heads),
         sds(ssm_state.shape[1:], F32), [smem()] + [vmem()] * 5,
@@ -554,7 +606,7 @@
         ]
         return lax.ppermute(v, ("fsdp", "req"), moves)
 
-    arrived = [to_owner(out_parts[s], s) for s in range(fan)]
+    arrived = [to_owner(out_parts[s], s) for s in reversed(range(fan))]
     mixed = call(
         functools.partial(final_kernel, 2 * cols, inner * fan),
         sds((length, 2 * cols), BF), [vmem()] * fan, *arrived,

time: 57.3 us -> 55.3 us (0.965)
  the two profiles are of different devices: /device:TPU:0 before, /device:TPU:24 now
where the time goes in v4:
time: 55.3 us; the launch traced here: 54.9 us
  starting transfers between devices  24.4 us (44%)
  Pallas kernels  14.5 us (26%)
  waiting for transfers between devices  13.3 us (24%)
  between operations  1.48 us (3%)
  other arithmetic  1.23 us (2%)
    pallas_call x14, Pallas kernels, call(): pl.pallas_call(body, out_shape=out_shape, in_specs=in_specs, out_specs=ja...  14.5 us
    ppermute x12, starting transfers between devices, shift(): return lax.ppermute(v, 'req', [(j, j ^ 2 * step) for j in range(reqs)])  14.1 us
    ppermute x12, waiting for transfers between devices, shift(): return lax.ppermute(v, 'req', [(j, j ^ 2 * step) for j in range(reqs)])  9.79 us
    ppermute x4, starting transfers between devices, to_owner(): return lax.ppermute(v, ('fsdp', 'req'), moves)  9 us
    ppermute x4, waiting for transfers between devices, to_owner(): return lax.ppermute(v, ('fsdp', 'req'), moves)  3.35 us
    ppermute x4, starting transfers between devices, swap(): return lax.ppermute(v, 'req', [(j, j ^ 1) for j in range(reqs)])  1.27 us
    broadcast_in_dim x2, other arithmetic, tail_rows(): return lax.dynamic_slice_in_dim(joined, accepted[0], KC - 1, 0)[None]  1.23 us
  transfers between devices with their start and end apart: 20, of which 11 were waited for; matrix products, arithmetic and copies ran while one was open for 2% of the time, Pallas kernels for 16%

profile of v4, /device:TPU:24, one launch (start us, length us, event | category | flops | bytes accessed | tf_op | source)
XLA Modules:
  0.0 54.9 jit_solution(10108328936431543112)
XLA Ops:
  0.6 1.9 %shard_map.273 = (bf16[32,640]{1,0:T(8,128)(2,1)S(1)}, bf16[32,640]{1,0:T(8,128)(2,1)S(1)}, bf16[32,640]{1,0:T(8,128)(2,1)S(1)}, bf16[32,640]{1,0:T(8,128)(2,1)S...) custom-call(bf16[1,16,2560]{2,1,0:T(8,128)(2,1)} %drafts_hbm.1, ...), custom_call_target="tpu_custom_call" | custom-call | flops 10 | bytes 81920 | tf_op jit(solution)/shard_map/pallas_call | solution.py:29
  3.1 1.5 %collective-permute-start.2 = (bf16[32,640]{1,0:T(8,128)(2,1)S(1)}, bf16[32,640]{1,0:T(8,128)(2,1)S(1)}, u32[]{:S(2)}, u32[]{:S(2)}) collective-permute-start(bf16[32,640]{1,0:T(8,128)(2,1)S(1)} %get-tuple-element.50), channel_id=1, source_target_pairs={{0,2},{1,3},{2,0},{3,1},{4,6},{5,7},{6,4},{7,5},{8,10},{9,11},{10,... | collective-permute-start | bytes 122888 | tf_op jit(solution)/shard_map/ppermute | solution.py:474
  4.6 1.5 %collective-permute-start = (bf16[32,640]{1,0:T(8,128)(2,1)S(1)}, bf16[32,640]{1,0:T(8,128)(2,1)S(1)}, u32[]{:S(2)}, u32[]{:S(2)}) collective-permute-start(bf16[32,640]{1,0:T(8,128)(2,1)S(1)} %get-tuple-element.48), channel_id=1, source_target_pairs={{0,6},{1,7},{2,4},{3,5},{4,2},{5,3},{6,0},{7,1},{8,14},{9,15},{10,... | collective-permute-start | bytes 122888 | tf_op jit(solution)/shard_map/ppermute | solution.py:474
  7.1 2.5 %shard_map.274.refs_6_.pages = bf16[10,256,1280]{2,1,0:T(8,128)(2,1)S(1)} custom-call(s32[10]{0:T(128)S(1)} %get-tuple-element.43.req.slot_req, s32[10]{0:T(128)S(1)} %get-tuple-element.44.slot.slot_page, s32[8]{0:T(128)S(1)} %get-tuple-element.45.count.page_count, bf16[10,256,1280]{2,1,0:T(8,128)(2,1)} %x_hbm.3, ...), custom_call_target="tpu_custom_call" | custom-call | bytes 6553600 | tf_op jit(solution)/shard_map/pallas_call | solution.py:29
  10.6 1.5 %collective-permute-start.6 = (bf16[64,384]{1,0:T(8,128)(2,1)S(1)}, bf16[64,384]{1,0:T(8,128)(2,1)S(1)}, u32[]{:S(2)}, u32[]{:S(2)}) collective-permute-start(bf16[64,384]{1,0:T(8,128)(2,1)S(1)} %shard_map.275.refs_12_.refs_0_), channel_id=1, source_target_pairs={{0,2},{1,3},{2,0},{3,1},{4,6},{5,7},{6,4},{7,5},{8,10},{9,11},{10,... | collective-permute-start | bytes 147464 | tf_op jit(solution)/shard_map/ppermute | solution.py:474
  12.1 0.7 %collective-permute-start.5 = (bf16[64,384]{1,0:T(8,128)(2,1)S(1)}, bf16[64,384]{1,0:T(8,128)(2,1)S(1)}, u32[]{:S(2)}, u32[]{:S(2)}) collective-permute-start(bf16[64,384]{1,0:T(8,128)(2,1)S(1)} %shard_map.275.refs_12_.refs_0_), channel_id=1, source_target_pairs={{0,4},{1,5},{2,6},{3,7},{4,0},{5,1},{6,2},{7,3},{8,12},{9,13},{10,... | collective-permute-start | bytes 147464 | tf_op jit(solution)/shard_map/ppermute | solution.py:474
  12.8 1.3 %collective-permute-start.4 = (bf16[64,384]{1,0:T(8,128)(2,1)S(1)}, bf16[64,384]{1,0:T(8,128)(2,1)S(1)}, u32[]{:S(2)}, u32[]{:S(2)}) collective-permute-start(bf16[64,384]{1,0:T(8,128)(2,1)S(1)} %shard_map.275.refs_12_.refs_0_), channel_id=1, source_target_pairs={{0,6},{1,7},{2,4},{3,5},{4,2},{5,3},{6,0},{7,1},{8,14},{9,15},{10,... | collective-permute-start | bytes 147464 | tf_op jit(solution)/shard_map/ppermute | solution.py:474
  14.1 1.4 %shard_map.276 = (bf16[4,256]{1,0:T(4,128)(2,1)S(1)}, bf16[256]{0:T(256)(128)(2,1)S(1)}, f32[20]{0:T(128)S(1)}, f32[20]{0:T(128)S(1)}, bf16[4,1280]{1,0:T(4,128)...) custom-call(bf16[4,256]{1,0:T(4,128)(2,1)} %refs_0_.3, ...), custom_call_target="tpu_custom_call" | custom-call | bytes 794704 | tf_op jit(solution)/shard_map/pallas_call | solution.py:29
  15.5 1.0 %shard_map.277 = (bf16[64,2560]{1,0:T(8,128)(2,1)S(1)}, bf16[640,1280]{1,0:T(8,128)(2,1)S(1)}) custom-call(bf16[32,640]{1,0:T(8,128)(2,1)S(1)} %get-tuple-element.47.refs_0_.refs_4_, bf16[32,640]{1,0:T(8,128)(2,1)S(1)} %collective-permute-done.refs_1_.refs_5_, bf16[32,640]{1,0:T(8,128)(2,1)S(1)} %collective-permute-done.1.refs_2_.refs_6_, ...), custom_call_target="tpu_custom_call" | custom-call | flops 209715200 | bytes 3276800 | tf_op jit(solution)/shard_map/pallas_call | solution.py:29
  16.5 1.3 %collective-permute-done.4.refs_1_ = bf16[64,384]{1,0:T(8,128)(2,1)S(1)} collective-permute-done((bf16[64,384]{1,0:T(8,128)(2,1)S(1)}, bf16[64,384]{1,0:T(8,128)(2,1)S(1)}, u32[]{:S(2)}, u32[]{:S(2)}) %collective-permute-start.4) | collective-permute-done | bytes 49184 | tf_op jit(solution)/shard_map/ppermute | solution.py:474
  18.0 1.2 %shard_map.279.begun._ = f32[64,1280]{1,0:T(8,128)S(1)} custom-call(s32[10]{0:T(128)S(1)} %get-tuple-element.43.req.slot_req, s32[10]{0:T(128)S(1)} %get-tuple-element.44.slot.slot_page, s32[8]{0:T(128)S(1)} %get-tuple-element.45.count.page_count, s32[8]{0:T(128)S(1)} %get-tuple-element.46.owner_row, f32[64,256]{1,0:T(8,128)S(1)} %get-tuple-element.58.packed.refs_4_, ...), custom_call_target="tpu_custom_call" | custom-call | flops 104857600 | bytes 6553600 | tf_op jit(solution)/shard_map/pallas_call | solution.py:29
  19.3 1.8 %shard_map.281 = bf16[64,1280]{1,0:T(8,128)(2,1)S(1)} custom-call(s32[10]{0:T(128)S(1)} %get-tuple-element.43.req.slot_req, s32[10]{0:T(128)S(1)} %get-tuple-element.44.slot.slot_page, s32[8]{0:T(128)S(1)} %get-tuple-element.45.count.page_count, s32[8]{0:T(128)S(1)} %get-tuple-element.46.owner_row, f32[64,256]{1,0:T(8,128)S(1)} %collective-permute-done.8.packed, ...), custom_call_target="tpu_custom_call" | custom-call | flops 209715200 | bytes 6553600 | tf_op jit(solution)/shard_map/pallas_call | solution.py:29
  21.0 0.6 %collective-permute-start.9 = (bf16[64,1280]{1,0:T(8,128)(2,1)S(1)}, bf16[64,1280]{1,0:T(8,128)(2,1)S(1)}, u32[]{:S(2)}, u32[]{:S(2)}) collective-permute-start(bf16[64,1280]{1,0:T(8,128)(2,1)S(1)} %shard_map.281), channel_id=1, source_target_pairs={{0,1},{1,0},{2,3},{3,2},{4,5},{5,4},{6,7},{7,6},{8,9},{9,8},{10,11... | collective-permute-start | bytes 491528 | tf_op jit(solution)/shard_map/ppermute | solution.py:471
  21.7 0.9 %shard_map.280.mine = bf16[64,1280]{1,0:T(8,128)(2,1)S(1)} custom-call(s32[10]{0:T(128)S(1)} %get-tuple-element.43.req.slot_req, s32[10]{0:T(128)S(1)} %get-tuple-element.44.slot.slot_page, s32[8]{0:T(128)S(1)} %get-tuple-element.45.count.page_count, s32[8]{0:T(128)S(1)} %get-tuple-element.46.owner_row, f32[64,256]{1,0:T(8,128)S(1)} %get-tuple-element.58.packed.refs_4_, ...), custom_call_target="tpu_custom_call" | custom-call | flops 104857600 | bytes 6553600 | tf_op jit(solution)/shard_map/pallas_call | solution.py:29
  22.8 1.5 %collective-permute-start.10 = (bf16[16,3840]{1,0:T(8,128)(2,1)S(1)}, bf16[16,3840]{1,0:T(8,128)(2,1)S(1)}, u32[]{:S(2)}, u32[]{:S(2)}) collective-permute-start(bf16[16,3840]{1,0:T(8,128)(2,1)S(1)} %get-tuple-element.62), channel_id=1, source_target_pairs={{0,6},{1,7},{2,4},{3,5},{4,2},{5,3},{6,0},{7,1},{8,14},{9,15},{10,... | collective-permute-start | bytes 368648 | tf_op jit(solution)/shard_map/ppermute | solution.py:474
  24.2 0.9 %collective-permute-start.11 = (bf16[16,3840]{1,0:T(8,128)(2,1)S(1)}, bf16[16,3840]{1,0:T(8,128)(2,1)S(1)}, u32[]{:S(2)}, u32[]{:S(2)}) collective-permute-start(bf16[16,3840]{1,0:T(8,128)(2,1)S(1)} %get-tuple-element.63), channel_id=1, source_target_pairs={{0,4},{1,5},{2,6},{3,7},{4,0},{5,1},{6,2},{7,3},{8,12},{9,13},{10,... | collective-permute-start | bytes 368648 | tf_op jit(solution)/shard_map/ppermute | solution.py:474
  25.1 1.2 %collective-permute-start.12 = (bf16[16,3840]{1,0:T(8,128)(2,1)S(1)}, bf16[16,3840]{1,0:T(8,128)(2,1)S(1)}, u32[]{:S(2)}, u32[]{:S(2)}) collective-permute-start(bf16[16,3840]{1,0:T(8,128)(2,1)S(1)} %get-tuple-element.64), channel_id=1, source_target_pairs={{0,2},{1,3},{2,0},{3,1},{4,6},{5,7},{6,4},{7,5},{8,10},{9,11},{10,... | collective-permute-start | bytes 368648 | tf_op jit(solution)/shard_map/ppermute | solution.py:474
  27.0 2.9 %collective-permute-done.10.refs_1_ = bf16[16,3840]{1,0:T(8,128)(2,1)S(1)} collective-permute-done((bf16[16,3840]{1,0:T(8,128)(2,1)S(1)}, bf16[16,3840]{1,0:T(8,128)(2,1)S(1)}, u32[]{:S(2)}, u32[]{:S(2)}) %collective-permute-start.10) | collective-permute-done | bytes 122912 | tf_op jit(solution)/shard_map/ppermute | solution.py:474
  29.9 2.0 %collective-permute-done.11.refs_2_ = bf16[16,3840]{1,0:T(8,128)(2,1)S(1)} collective-permute-done((bf16[16,3840]{1,0:T(8,128)(2,1)S(1)}, bf16[16,3840]{1,0:T(8,128)(2,1)S(1)}, u32[]{:S(2)}, u32[]{:S(2)}) %collective-permute-start.11) | collective-permute-done | bytes 122912 | tf_op jit(solution)/shard_map/ppermute | solution.py:474
  32.5 0.7 %collective-permute-start.15 = (bf16[16,1280]{1,0:T(8,128)(2,1)S(1)}, bf16[16,1280]{1,0:T(8,128)(2,1)S(1)}, u32[]{:S(2)}, u32[]{:S(2)}) collective-permute-start(bf16[16,1280]{1,0:T(8,128)(2,1)S(1)} %get-tuple-element.72.refs_0_), channel_id=1, source_target_pairs={{0,2},{1,3},{2,0},{3,1},{4,6},{5,7},{6,4},{7,5},{8,10},{9,11},{10,... | collective-permute-start | bytes 122888 | tf_op jit(solution)/shard_map/ppermute | solution.py:474
  33.2 0.9 %collective-permute-start.14 = (bf16[16,1280]{1,0:T(8,128)(2,1)S(1)}, bf16[16,1280]{1,0:T(8,128)(2,1)S(1)}, u32[]{:S(2)}, u32[]{:S(2)}) collective-permute-start(bf16[16,1280]{1,0:T(8,128)(2,1)S(1)} %get-tuple-element.72.refs_0_), channel_id=1, source_target_pairs={{0,4},{1,5},{2,6},{3,7},{4,0},{5,1},{6,2},{7,3},{8,12},{9,13},{10,... | collective-permute-start | bytes 122888 | tf_op jit(solution)/shard_map/ppermute | solution.py:474
  34.1 2.0 %collective-permute-start.13 = (bf16[16,1280]{1,0:T(8,128)(2,1)S(1)}, bf16[16,1280]{1,0:T(8,128)(2,1)S(1)}, u32[]{:S(2)}, u32[]{:S(2)}) collective-permute-start(bf16[16,1280]{1,0:T(8,128)(2,1)S(1)} %get-tuple-element.72.refs_0_), channel_id=1, source_target_pairs={{0,6},{1,7},{2,4},{3,5},{4,2},{5,3},{6,0},{7,1},{8,14},{9,15},{10,... | collective-permute-start | bytes 122888 | tf_op jit(solution)/shard_map/ppermute | solution.py:474
  36.1 0.6 %fusion.3 = bf16[1,3,256]{2,1,0:T(4,128)(2,1)} fusion(s32[]{:T(128)S(6)} %select_n.4, bf16[16,256]{1,0:T(8,128)(2,1)S(1)} %get-tuple-element.81, bf16[3,256]{1,0:T(4,128)(2,1)S(1)} %bitcast.21), kind=kLoop, calls=%fused_computation.7 | loop fusion | flops 3072 | bytes 11268 | tf_op jit(solution)/shard_map/broadcast_in_dim | solution.py:618
  37.2 1.8 %collective-permute-done.13.refs_1_ = bf16[16,1280]{1,0:T(8,128)(2,1)S(1)} collective-permute-done((bf16[16,1280]{1,0:T(8,128)(2,1)S(1)}, bf16[16,1280]{1,0:T(8,128)(2,1)S(1)}, u32[]{:S(2)}, u32[]{:S(2)}) %collective-permute-start.13) | collective-permute-done | bytes 40992 | tf_op jit(solution)/shard_map/ppermute | solution.py:474
  39.0 0.6 %shard_map.284 = (bf16[16,768]{1,0:T(8,128)(2,1)S(1)}, bf16[16,768]{1,0:T(8,128)(2,1)S(1)}, bf16[16,768]{1,0:T(8,128)(2,1)S(1)}, bf16[16,768]{1,0:T(8,128)(2,1)S(1)}) custom-call(bf16[16,1280]{1,0:T(8,128)(2,1)S(1)} %get-tuple-element.72.refs_0_, bf16[16,1280]{1,0:T(8,128)(2,1)S(1)} %collective-permute-done.13.refs_1_, ...), custom_call_target="tpu_custom_call" | custom-call | flops 104857600 | bytes 1638400 | tf_op jit(solution)/shard_map/pallas_call | solution.py:29
  39.9 3.0 %collective-permute-start.17 = (bf16[16,768]{1,0:T(8,128)(2,1)S(1)}, bf16[16,768]{1,0:T(8,128)(2,1)S(1)}, u32[]{:S(2)}, u32[]{:S(2)}) collective-permute-start(bf16[16,768]{1,0:T(8,128)(2,1)S(1)} %get-tuple-element.76), channel_id=1, source_target_pairs={{0,4},{1,5},{2,12},{3,13},{4,20},{5,21},{6,28},{7,29},{8,6},{9,7},... | collective-permute-start | bytes 73736 | tf_op jit(solution)/shard_map/ppermute | solution.py:607
  42.9 1.9 %collective-permute-start.18 = (bf16[16,768]{1,0:T(8,128)(2,1)S(1)}, bf16[16,768]{1,0:T(8,128)(2,1)S(1)}, u32[]{:S(2)}, u32[]{:S(2)}) collective-permute-start(bf16[16,768]{1,0:T(8,128)(2,1)S(1)} %get-tuple-element.77), channel_id=1, source_target_pairs={{0,2},{1,3},{2,10},{3,11},{4,18},{5,19},{6,26},{7,27},{8,0},{9,1},... | collective-permute-start | bytes 73736 | tf_op jit(solution)/shard_map/ppermute | solution.py:607
  44.8 3.9 %collective-permute-start.19 = (bf16[16,768]{1,0:T(8,128)(2,1)S(1)}, bf16[16,768]{1,0:T(8,128)(2,1)S(1)}, u32[]{:S(2)}, u32[]{:S(2)}) collective-permute-start(bf16[16,768]{1,0:T(8,128)(2,1)S(1)} %get-tuple-element.78), channel_id=1, source_target_pairs={{0,0},{1,1},{2,8},{3,9},{4,16},{5,17},{6,24},{7,25},{8,2},{9,3},{1... | collective-permute-start | bytes 73736 | tf_op jit(solution)/shard_map/ppermute | solution.py:607
  48.7 0.6 %fusion.1 = bf16[1,3,1280]{2,1,0:T(4,128)(2,1)} fusion(s32[]{:T(128)S(6)} %select_n.4, bf16[16,1280]{1,0:T(8,128)(2,1)S(1)} %get-tuple-element.80, bf16[3,1280]{1,0:T(4,128)(2,1)S(1)} %bitcast.18), kind=kLoop, calls=%fused_computation.5 | loop fusion | flops 15360 | bytes 56324 | tf_op jit(solution)/shard_map/broadcast_in_dim | solution.py:618
  49.3 1.4 %shard_map.286 = f32[20,64,128]{2,1,0:T(8,128)} custom-call(s32[1]{0:T(128)} %copy.30.accepted, f32[64,256]{1,0:T(8,128)S(1)} %get-tuple-element.58.packed.refs_4_, f32[16,20]{1,0:T(8,128)S(1)} %get-tuple-element.66.refs_6_.dtime_ref, bf16[16,1280]{1,0:T(8,128)(2,1)S(1)} %get-tuple-element.79.x_act, bf16[16,256]{1,0:T(8,128)(2,1)S(1)} %get-tuple-element.65.refs_5_.bc_act, ...), custom_call_target="tpu_custom_call" | custom-call | flops 10485760 | bytes 1310720 | tf_op jit(solution)/shard_map/pallas_call | solution.py:29
  50.8 3.3 %collective-permute-done.19.refs_3_ = bf16[16,768]{1,0:T(8,128)(2,1)S(1)} collective-permute-done((bf16[16,768]{1,0:T(8,128)(2,1)S(1)}, bf16[16,768]{1,0:T(8,128)(2,1)S(1)}, u32[]{:S(2)}, u32[]{:S(2)}) %collective-permute-start.19) | collective-permute-done | bytes 24608 | tf_op jit(solution)/shard_map/ppermute | solution.py:607
  54.1 0.8 %shard_map.285 = bf16[16,640]{1,0:T(8,128)(2,1)} custom-call(bf16[16,768]{1,0:T(8,128)(2,1)S(1)} %collective-permute-done.16.refs_0_, bf16[16,768]{1,0:T(8,128)(2,1)S(1)} %collective-permute-done.17.refs_1_, bf16[16,768]{1,0:T(8,128)(2,1)S(1)} %collective-permute-done.18.refs_2_, bf16[16,768]{1,0:T(8,128)(2,1)S(1)} %collective-permute-done.19.refs_3_), custom_call_target="tpu_custom_call" | custom-call | flops 51200 | bytes 51200 | tf_op jit(solution)/shard_map/pallas_call | solution.py:29
  (30 shorter events, 4.3 us)
Async XLA Ops:
  2.6 12.9 %collective-permute-start.7 = (bf16[960,1280]{1,0:T(8,128)(2,1)S(1)}, bf16[960,1280]{1,0:T(8,128)(2,1)S(1)}, u32[]{:S(2)}, u32[]{:S(2)}) collective-permute-start(bf16[960,1280]{1,0:T(8,128)(2,1)S(1)} %get-tuple-element.56.refs_4_), channel_id=1, source_target_pairs={{0,1},{1,0},{2,3},{3,2},{4,5},{5,4},{6,7},{7,6},{8,9},{9,8},{10,11... | collective-permute-start | bytes 7372808 | tf_op jit(solution)/shard_map/ppermute | solution.py:471
  2.6 7.5 %collective-permute-start.3 = (bf16[352,384]{1,0:T(8,128)(2,1)S(1)}, bf16[352,384]{1,0:T(8,128)(2,1)S(1)}, u32[]{:S(2)}, u32[]{:S(2)}) collective-permute-start(bf16[352,384]{1,0:T(8,128)(2,1)S(1)} %get-tuple-element.51.refs_4_), channel_id=1, source_target_pairs={{0,1},{1,0},{2,3},{3,2},{4,5},{5,4},{6,7},{7,6},{8,9},{9,8},{10,11... | collective-permute-start | bytes 811016 | tf_op jit(solution)/shard_map/ppermute | solution.py:471
  3.1 4.0 %collective-permute-start.2 = (bf16[32,640]{1,0:T(8,128)(2,1)S(1)}, bf16[32,640]{1,0:T(8,128)(2,1)S(1)}, u32[]{:S(2)}, u32[]{:S(2)}) collective-permute-start(bf16[32,640]{1,0:T(8,128)(2,1)S(1)} %get-tuple-element.50), channel_id=1, source_target_pairs={{0,2},{1,3},{2,0},{3,1},{4,6},{5,7},{6,4},{7,5},{8,10},{9,11},{10,... | collective-permute-start | bytes 122888 | tf_op jit(solution)/shard_map/ppermute | solution.py:474
  4.6 5.1 %collective-permute-start = (bf16[32,640]{1,0:T(8,128)(2,1)S(1)}, bf16[32,640]{1,0:T(8,128)(2,1)S(1)}, u32[]{:S(2)}, u32[]{:S(2)}) collective-permute-start(bf16[32,640]{1,0:T(8,128)(2,1)S(1)} %get-tuple-element.48), channel_id=1, source_target_pairs={{0,6},{1,7},{2,4},{3,5},{4,2},{5,3},{6,0},{7,1},{8,14},{9,15},{10,... | collective-permute-start | bytes 122888 | tf_op jit(solution)/shard_map/ppermute | solution.py:474
  6.1 4.0 %collective-permute-start.1 = (bf16[32,640]{1,0:T(8,128)(2,1)S(1)}, bf16[32,640]{1,0:T(8,128)(2,1)S(1)}, u32[]{:S(2)}, u32[]{:S(2)}) collective-permute-start(bf16[32,640]{1,0:T(8,128)(2,1)S(1)} %get-tuple-element.49), channel_id=1, source_target_pairs={{0,4},{1,5},{2,6},{3,7},{4,0},{5,1},{6,2},{7,3},{8,12},{9,13},{10,... | collective-permute-start | bytes 122888 | tf_op jit(solution)/shard_map/ppermute | solution.py:474
  10.6 5.9 %collective-permute-start.6 = (bf16[64,384]{1,0:T(8,128)(2,1)S(1)}, bf16[64,384]{1,0:T(8,128)(2,1)S(1)}, u32[]{:S(2)}, u32[]{:S(2)}) collective-permute-start(bf16[64,384]{1,0:T(8,128)(2,1)S(1)} %shard_map.275.refs_12_.refs_0_), channel_id=1, source_target_pairs={{0,2},{1,3},{2,0},{3,1},{4,6},{5,7},{6,4},{7,5},{8,10},{9,11},{10,... | collective-permute-start | bytes 147464 | tf_op jit(solution)/shard_map/ppermute | solution.py:474
  12.1 4.4 %collective-permute-start.5 = (bf16[64,384]{1,0:T(8,128)(2,1)S(1)}, bf16[64,384]{1,0:T(8,128)(2,1)S(1)}, u32[]{:S(2)}, u32[]{:S(2)}) collective-permute-start(bf16[64,384]{1,0:T(8,128)(2,1)S(1)} %shard_map.275.refs_12_.refs_0_), channel_id=1, source_target_pairs={{0,4},{1,5},{2,6},{3,7},{4,0},{5,1},{6,2},{7,3},{8,12},{9,13},{10,... | collective-permute-start | bytes 147464 | tf_op jit(solution)/shard_map/ppermute | solution.py:474
  12.8 5.0 %collective-permute-start.4 = (bf16[64,384]{1,0:T(8,128)(2,1)S(1)}, bf16[64,384]{1,0:T(8,128)(2,1)S(1)}, u32[]{:S(2)}, u32[]{:S(2)}) collective-permute-start(bf16[64,384]{1,0:T(8,128)(2,1)S(1)} %shard_map.275.refs_12_.refs_0_), channel_id=1, source_target_pairs={{0,6},{1,7},{2,4},{3,5},{4,2},{5,3},{6,0},{7,1},{8,14},{9,15},{10,... | collective-permute-start | bytes 147464 | tf_op jit(solution)/shard_map/ppermute | solution.py:474
  17.9 1.3 %collective-permute-start.8 = (f32[64,256]{1,0:T(8,128)S(1)}, f32[64,256]{1,0:T(8,128)S(1)}, u32[]{:S(2)}, u32[]{:S(2)}) collective-permute-start(f32[64,256]{1,0:T(8,128)S(1)} %get-tuple-element.58.packed.refs_4_), channel_id=1, source_target_pairs={{0,1},{1,0},{2,3},{3,2},{4,5},{5,4},{6,7},{7,6},{8,9},{9,8},{10,11... | collective-permute-start | bytes 196616 | tf_op jit(solution)/shard_map/ppermute | solution.py:471
  21.0 15.1 %copy-start.2 = (bf16[1,3,256]{2,1,0:T(4,128)(2,1)S(1)}, bf16[1,3,256]{2,1,0:T(4,128)(2,1)}, u32[]{:S(2)}) copy-start(bf16[1,3,256]{2,1,0:T(4,128)(2,1)} %history_hbm.1) | copy-start | bytes 4612
  21.0 1.7 %collective-permute-start.9 = (bf16[64,1280]{1,0:T(8,128)(2,1)S(1)}, bf16[64,1280]{1,0:T(8,128)(2,1)S(1)}, u32[]{:S(2)}, u32[]{:S(2)}) collective-permute-start(bf16[64,1280]{1,0:T(8,128)(2,1)S(1)} %shard_map.281), channel_id=1, source_target_pairs={{0,1},{1,0},{2,3},{3,2},{4,5},{5,4},{6,7},{7,6},{8,9},{9,8},{10,11... | collective-permute-start | bytes 491528 | tf_op jit(solution)/shard_map/ppermute | solution.py:471
  22.6 26.1 %copy-start.1 = (bf16[1,3,1280]{2,1,0:T(4,128)(2,1)S(1)}, bf16[1,3,1280]{2,1,0:T(4,128)(2,1)}, u32[]{:S(2)}) copy-start(bf16[1,3,1280]{2,1,0:T(4,128)(2,1)} %refs_7_.1) | copy-start | bytes 23044
  22.6 26.7 %copy-start = (f32[1,20,64,128]{3,2,1,0:T(8,128)S(1)}, f32[1,20,64,128]{3,2,1,0:T(8,128)}, u32[]{:S(2)}) copy-start(f32[1,20,64,128]{3,2,1,0:T(8,128)} %param.41) | copy-start | bytes 1966084
  22.8 7.2 %collective-permute-start.10 = (bf16[16,3840]{1,0:T(8,128)(2,1)S(1)}, bf16[16,3840]{1,0:T(8,128)(2,1)S(1)}, u32[]{:S(2)}, u32[]{:S(2)}) collective-permute-start(bf16[16,3840]{1,0:T(8,128)(2,1)S(1)} %get-tuple-element.62), channel_id=1, source_target_pairs={{0,6},{1,7},{2,4},{3,5},{4,2},{5,3},{6,0},{7,1},{8,14},{9,15},{10,... | collective-permute-start | bytes 368648 | tf_op jit(solution)/shard_map/ppermute | solution.py:474
  24.2 7.7 %collective-permute-start.11 = (bf16[16,3840]{1,0:T(8,128)(2,1)S(1)}, bf16[16,3840]{1,0:T(8,128)(2,1)S(1)}, u32[]{:S(2)}, u32[]{:S(2)}) collective-permute-start(bf16[16,3840]{1,0:T(8,128)(2,1)S(1)} %get-tuple-element.63), channel_id=1, source_target_pairs={{0,4},{1,5},{2,6},{3,7},{4,0},{5,1},{6,2},{7,3},{8,12},{9,13},{10,... | collective-permute-start | bytes 368648 | tf_op jit(solution)/shard_map/ppermute | solution.py:474
  25.1 7.1 %collective-permute-start.12 = (bf16[16,3840]{1,0:T(8,128)(2,1)S(1)}, bf16[16,3840]{1,0:T(8,128)(2,1)S(1)}, u32[]{:S(2)}, u32[]{:S(2)}) collective-permute-start(bf16[16,3840]{1,0:T(8,128)(2,1)S(1)} %get-tuple-element.64), channel_id=1, source_target_pairs={{0,2},{1,3},{2,0},{3,1},{4,6},{5,7},{6,4},{7,5},{8,10},{9,11},{10,... | collective-permute-start | bytes 368648 | tf_op jit(solution)/shard_map/ppermute | solution.py:474
  32.5 4.2 %collective-permute-start.15 = (bf16[16,1280]{1,0:T(8,128)(2,1)S(1)}, bf16[16,1280]{1,0:T(8,128)(2,1)S(1)}, u32[]{:S(2)}, u32[]{:S(2)}) collective-permute-start(bf16[16,1280]{1,0:T(8,128)(2,1)S(1)} %get-tuple-element.72.refs_0_), channel_id=1, source_target_pairs={{0,2},{1,3},{2,0},{3,1},{4,6},{5,7},{6,4},{7,5},{8,10},{9,11},{10,... | collective-permute-start | bytes 122888 | tf_op jit(solution)/shard_map/ppermute | solution.py:474
  33.2 4.0 %collective-permute-start.14 = (bf16[16,1280]{1,0:T(8,128)(2,1)S(1)}, bf16[16,1280]{1,0:T(8,128)(2,1)S(1)}, u32[]{:S(2)}, u32[]{:S(2)}) collective-permute-start(bf16[16,1280]{1,0:T(8,128)(2,1)S(1)} %get-tuple-element.72.refs_0_), channel_id=1, source_target_pairs={{0,4},{1,5},{2,6},{3,7},{4,0},{5,1},{6,2},{7,3},{8,12},{9,13},{10,... | collective-permute-start | bytes 122888 | tf_op jit(solution)/shard_map/ppermute | solution.py:474
  34.1 4.9 %collective-permute-start.13 = (bf16[16,1280]{1,0:T(8,128)(2,1)S(1)}, bf16[16,1280]{1,0:T(8,128)(2,1)S(1)}, u32[]{:S(2)}, u32[]{:S(2)}) collective-permute-start(bf16[16,1280]{1,0:T(8,128)(2,1)S(1)} %get-tuple-element.72.refs_0_), channel_id=1, source_target_pairs={{0,6},{1,7},{2,4},{3,5},{4,2},{5,3},{6,0},{7,1},{8,14},{9,15},{10,... | collective-permute-start | bytes 122888 | tf_op jit(solution)/shard_map/ppermute | solution.py:474
  39.7 11.1 %collective-permute-start.16 = (bf16[16,768]{1,0:T(8,128)(2,1)S(1)}, bf16[16,768]{1,0:T(8,128)(2,1)S(1)}, u32[]{:S(2)}, u32[]{:S(2)}) collective-permute-start(bf16[16,768]{1,0:T(8,128)(2,1)S(1)} %get-tuple-element.75), channel_id=1, source_target_pairs={{0,6},{1,7},{2,14},{3,15},{4,22},{5,23},{6,30},{7,31},{8,4},{9,5},... | collective-permute-start | bytes 73736 | tf_op jit(solution)/shard_map/ppermute | solution.py:607
  39.9 10.8 %collective-permute-start.17 = (bf16[16,768]{1,0:T(8,128)(2,1)S(1)}, bf16[16,768]{1,0:T(8,128)(2,1)S(1)}, u32[]{:S(2)}, u32[]{:S(2)}) collective-permute-start(bf16[16,768]{1,0:T(8,128)(2,1)S(1)} %get-tuple-element.76), channel_id=1, source_target_pairs={{0,4},{1,5},{2,12},{3,13},{4,20},{5,21},{6,28},{7,29},{8,6},{9,7},... | collective-permute-start | bytes 73736 | tf_op jit(solution)/shard_map/ppermute | solution.py:607
  42.9 7.8 %collective-permute-start.18 = (bf16[16,768]{1,0:T(8,128)(2,1)S(1)}, bf16[16,768]{1,0:T(8,128)(2,1)S(1)}, u32[]{:S(2)}, u32[]{:S(2)}) collective-permute-start(bf16[16,768]{1,0:T(8,128)(2,1)S(1)} %get-tuple-element.77), channel_id=1, source_target_pairs={{0,2},{1,3},{2,10},{3,11},{4,18},{5,19},{6,26},{7,27},{8,0},{9,1},... | collective-permute-start | bytes 73736 | tf_op jit(solution)/shard_map/ppermute | solution.py:607
  44.8 9.3 %collective-permute-start.19 = (bf16[16,768]{1,0:T(8,128)(2,1)S(1)}, bf16[16,768]{1,0:T(8,128)(2,1)S(1)}, u32[]{:S(2)}, u32[]{:S(2)}) collective-permute-start(bf16[16,768]{1,0:T(8,128)(2,1)S(1)} %get-tuple-element.78), channel_id=1, source_target_pairs={{0,0},{1,1},{2,8},{3,9},{4,16},{5,17},{6,24},{7,25},{8,2},{9,3},{1... | collective-permute-start | bytes 73736 | tf_op jit(solution)/shard_map/ppermute | solution.py:607

commit v5 on v4

--- a/solution.py
+++ b/solution.py
@@ -233,8 +233,7 @@
     return (slot_req[s] >= 0) & (slot_page[s] < page_count[jnp.maximum(slot_req[s], 0)])
 
 
-def page_terms(chosen, lists, heads, packed, b_ref, decay_ref, pages, total, order, scores_ref):
-    slots, length = scores_ref.shape[:2]
+def page_terms(chosen, length, lists, heads, packed, b_ref, decay_ref, pages, total, order):
     pair = lax.axis_index("req") // 2
     slot_req, _, _, owner_row = lists
 
@@ -242,15 +241,12 @@
         row = owner_row[jnp.maximum(slot_req[s], 0)]
         return pl.ds(pl.multiple_of((pair ^ row // 2) * length, length), length)
 
-    for s in range(slots):
-        scores_ref[s] = lax.dot_general(
-            packed[rows_of(s), :NS].astype(BF), b_ref[s], (((1,), (1,)), ((), ())),
+    def visit(s):
+        rows = rows_of(s)
+        scores = lax.dot_general(
+            packed[rows, :NS].astype(BF), b_ref[s], (((1,), (1,)), ((), ())),
             preferred_element_type=F32,
         )
-
-    def visit(s):
-        rows = rows_of(s)
-        scores = scores_ref[s]
         cumul = packed[rows, NS:]
         decay = decay_ref[s]
         terms = []
@@ -312,35 +308,35 @@
 
 
 def first_pages_kernel(
-    heads, slot_req, slot_page, page_count, owner_row, packed, b_ref, decay_ref, pages,
-    total, order, scores_ref,
+    length, heads, slot_req, slot_page, page_count, owner_row, packed, b_ref, decay_ref, pages,
+    total, order,
 ):
     lists = (slot_req, slot_page, page_count, owner_row)
     count = choose(range(pages.shape[0] // 2), lists, True, order)
     total[...] = jnp.zeros_like(total)
-    page_terms(count, lists, heads, packed, b_ref, decay_ref, pages, total, order, scores_ref)
+    page_terms(count, length, lists, heads, packed, b_ref, decay_ref, pages, total, order)
 
 
 def other_pages_kernel(
-    heads, slot_req, slot_page, page_count, owner_row, packed, b_ref, decay_ref, pages, _,
-    out, total, order, scores_ref,
+    length, heads, slot_req, slot_page, page_count, owner_row, packed, b_ref, decay_ref, pages, _,
+    out, total, order,
 ):
     lists = (slot_req, slot_page, page_count, owner_row)
     count = choose(range(pages.shape[0]), lists, False, order)
     total[...] = jnp.zeros_like(total)
-    page_terms(count, lists, heads, packed, b_ref, decay_ref, pages, total, order, scores_ref)
+    page_terms(count, length, lists, heads, packed, b_ref, decay_ref, pages, total, order)
     out[...] = total[...].astype(BF)
 
 
 def last_pages_kernel(
-    heads, slot_req, slot_page, page_count, owner_row, packed, b_ref, decay_ref, pages, begun,
-    out, total, order, scores_ref,
+    length, heads, slot_req, slot_page, page_count, owner_row, packed, b_ref, decay_ref, pages, begun,
+    out, total, order,
 ):
     lists = (slot_req, slot_page, page_count, owner_row)
     slots = pages.shape[0]
     count = choose(range(slots // 2, slots), lists, True, order)
     total[...] = begun[...]
-    page_terms(count, lists, heads, packed, b_ref, decay_ref, pages, total, order, scores_ref)
+    page_terms(count, length, lists, heads, packed, b_ref, decay_ref, pages, total, order)
     out[...] = total[...].astype(BF)
 
 
@@ -441,7 +437,7 @@
     )
     whole[:, cols:] = jnp.where(lane == 0, high, jnp.where(lane == 1, low, 0.0))
     for s, out in enumerate(outs):
-        block = me // 2 ^ zed ^ s
+        block = me // 2 ^ (zed + s) % fan
         rows = pl.ds(pl.multiple_of(block * length, length), length)
         out[...] = whole[rows, :].astype(BF)
 
@@ -542,17 +538,17 @@
     packed_other = swap(packed)
 
     whole = sds((fan * length, inner), F32)
-    scratch = [pltpu.SMEM((slots,), jnp.int32), pltpu.VMEM((slots, length, page_x.shape[1]), F32)]
+    scratch = [pltpu.SMEM((slots,), jnp.int32)]
     half_out = sds((fan * length, inner), BF)
     begun = call(
-        functools.partial(first_pages_kernel, heads),
+        functools.partial(first_pages_kernel, length, heads),
         whole, [smem()] * 4 + [vmem()] * 4,
         *lists, packed, page_b_here, page_decay_here, pages,
         flops=2 * slots * length * page_x.shape[1] * inner, nbytes=2 * page_x.size,
         scratch=scratch,
     )
     others = call(
-        functools.partial(other_pages_kernel, heads),
+        functools.partial(other_pages_kernel, length, heads),
         half_out, [smem()] * 4 + [vmem()] * 4 + [pl.BlockSpec(memory_space=pl.ANY)],
         *lists, packed_other, page_b_here, page_decay_here, pages, begun,
         flops=4 * slots * length * page_x.shape[1] * inner, nbytes=2 * page_x.size,
@@ -560,7 +556,7 @@
     )
     others = swap(others)
     mine = call(
-        functools.partial(last_pages_kernel, heads),
+        functools.partial(last_pages_kernel, length, heads),
         half_out, [smem()] * 4 + [vmem()] * 5,
         *lists, packed, page_b_here, page_decay_here, pages, begun,
         flops=2 * slots * length * page_x.shape[1] * inner, nbytes=2 * page_x.size,
@@ -600,13 +596,13 @@
 
     def to_owner(v, step):
         moves = [
-            (f * reqs + j, (j // 2) * reqs + 2 * (f ^ step) + j % 2)
+            (f * reqs + j, (j // 2) * reqs + 2 * ((f + step) % fan) + j % 2)
             for f in range(fan)
             for j in range(reqs)
         ]
         return lax.ppermute(v, ("fsdp", "req"), moves)
 
-    arrived = [to_owner(out_parts[s], s) for s in reversed(range(fan))]
+    arrived = [to_owner(out_parts[s], s) for s in range(fan)]
     mixed = call(
         functools.partial(final_kernel, 2 * cols, inner * fan),
         sds((length, 2 * cols), BF), [vmem()] * fan, *arrived,

time: 55.3 us -> 54.7 us (0.989)
  the two profiles are of different devices: /device:TPU:24 before, /device:TPU:0 now
where the time goes in v5:
time: 54.7 us; the launch traced here: 54.6 us
  starting transfers between devices  25.4 us (46%)
  Pallas kernels  14.1 us (26%)
  waiting for transfers between devices  12.5 us (23%)
  between operations  1.47 us (3%)
  other arithmetic  1.22 us (2%)
    ppermute x12, starting transfers between devices, shift(): return lax.ppermute(v, 'req', [(j, j ^ 2 * step) for j in range(reqs)])  15 us
    pallas_call x14, Pallas kernels, call(): pl.pallas_call(body, out_shape=out_shape, in_specs=in_specs, out_specs=ja...  14.1 us
    ppermute x12, waiting for transfers between devices, shift(): return lax.ppermute(v, 'req', [(j, j ^ 2 * step) for j in range(reqs)])  9.92 us
    ppermute x4, starting transfers between devices, to_owner(): return lax.ppermute(v, ('fsdp', 'req'), moves)  9.57 us
    ppermute x4, waiting for transfers between devices, swap(): return lax.ppermute(v, 'req', [(j, j ^ 1) for j in range(reqs)])  1.32 us
    ppermute x4, waiting for transfers between devices, to_owner(): return lax.ppermute(v, ('fsdp', 'req'), moves)  1.23 us
    broadcast_in_dim x2, other arithmetic, tail_rows(): return lax.dynamic_slice_in_dim(joined, accepted[0], KC - 1, 0)[None]  1.22 us
  transfers between devices with their start and end apart: 20, of which 13 were waited for; matrix products, arithmetic and copies ran while one was open for 2% of the time, Pallas kernels for 15%

profile of v5, /device:TPU:0, one launch (start us, length us, event | category | flops | bytes accessed | tf_op | source)
XLA Modules:
  0.0 54.6 jit_solution(4591985669652897990)
XLA Ops:
  0.6 1.9 %shard_map.273 = (bf16[32,640]{1,0:T(8,128)(2,1)S(1)}, bf16[32,640]{1,0:T(8,128)(2,1)S(1)}, bf16[32,640]{1,0:T(8,128)(2,1)S(1)}, bf16[32,640]{1,0:T(8,128)(2,1)S...) custom-call(bf16[1,16,2560]{2,1,0:T(8,128)(2,1)} %drafts_hbm.1, ...), custom_call_target="tpu_custom_call" | custom-call | flops 10 | bytes 81920 | tf_op jit(solution)/shard_map/pallas_call | solution.py:29
  3.2 2.9 %collective-permute-start.2 = (bf16[32,640]{1,0:T(8,128)(2,1)S(1)}, bf16[32,640]{1,0:T(8,128)(2,1)S(1)}, u32[]{:S(2)}, u32[]{:S(2)}) collective-permute-start(bf16[32,640]{1,0:T(8,128)(2,1)S(1)} %get-tuple-element.50), channel_id=1, source_target_pairs={{0,2},{1,3},{2,0},{3,1},{4,6},{5,7},{6,4},{7,5},{8,10},{9,11},{10,... | collective-permute-start | bytes 122888 | tf_op jit(solution)/shard_map/ppermute | solution.py:470
  6.1 1.5 %collective-permute-start = (bf16[32,640]{1,0:T(8,128)(2,1)S(1)}, bf16[32,640]{1,0:T(8,128)(2,1)S(1)}, u32[]{:S(2)}, u32[]{:S(2)}) collective-permute-start(bf16[32,640]{1,0:T(8,128)(2,1)S(1)} %get-tuple-element.48), channel_id=1, source_target_pairs={{0,6},{1,7},{2,4},{3,5},{4,2},{5,3},{6,0},{7,1},{8,14},{9,15},{10,... | collective-permute-start | bytes 122888 | tf_op jit(solution)/shard_map/ppermute | solution.py:470
  8.0 2.5 %shard_map.274.refs_6_.pages = bf16[10,256,1280]{2,1,0:T(8,128)(2,1)S(1)} custom-call(s32[10]{0:T(128)S(1)} %get-tuple-element.43.req.slot_req, s32[10]{0:T(128)S(1)} %get-tuple-element.44.slot.slot_page, s32[8]{0:T(128)S(1)} %get-tuple-element.45.count.page_count, bf16[10,256,1280]{2,1,0:T(8,128)(2,1)} %x_hbm.3, ...), custom_call_target="tpu_custom_call" | custom-call | bytes 6553600 | tf_op jit(solution)/shard_map/pallas_call | solution.py:29
  12.0 1.5 %collective-permute-start.6 = (bf16[64,384]{1,0:T(8,128)(2,1)S(1)}, bf16[64,384]{1,0:T(8,128)(2,1)S(1)}, u32[]{:S(2)}, u32[]{:S(2)}) collective-permute-start(bf16[64,384]{1,0:T(8,128)(2,1)S(1)} %shard_map.275.refs_12_.refs_0_), channel_id=1, source_target_pairs={{0,2},{1,3},{2,0},{3,1},{4,6},{5,7},{6,4},{7,5},{8,10},{9,11},{10,... | collective-permute-start | bytes 147464 | tf_op jit(solution)/shard_map/ppermute | solution.py:470
  13.5 0.9 %collective-permute-start.5 = (bf16[64,384]{1,0:T(8,128)(2,1)S(1)}, bf16[64,384]{1,0:T(8,128)(2,1)S(1)}, u32[]{:S(2)}, u32[]{:S(2)}) collective-permute-start(bf16[64,384]{1,0:T(8,128)(2,1)S(1)} %shard_map.275.refs_12_.refs_0_), channel_id=1, source_target_pairs={{0,4},{1,5},{2,6},{3,7},{4,0},{5,1},{6,2},{7,3},{8,12},{9,13},{10,... | collective-permute-start | bytes 147464 | tf_op jit(solution)/shard_map/ppermute | solution.py:470
  14.4 1.1 %collective-permute-start.4 = (bf16[64,384]{1,0:T(8,128)(2,1)S(1)}, bf16[64,384]{1,0:T(8,128)(2,1)S(1)}, u32[]{:S(2)}, u32[]{:S(2)}) collective-permute-start(bf16[64,384]{1,0:T(8,128)(2,1)S(1)} %shard_map.275.refs_12_.refs_0_), channel_id=1, source_target_pairs={{0,6},{1,7},{2,4},{3,5},{4,2},{5,3},{6,0},{7,1},{8,14},{9,15},{10,... | collective-permute-start | bytes 147464 | tf_op jit(solution)/shard_map/ppermute | solution.py:470
  15.5 1.4 %shard_map.276 = (bf16[4,256]{1,0:T(4,128)(2,1)S(1)}, bf16[256]{0:T(256)(128)(2,1)S(1)}, f32[20]{0:T(128)S(1)}, f32[20]{0:T(128)S(1)}, bf16[4,1280]{1,0:T(4,128)...) custom-call(bf16[4,256]{1,0:T(4,128)(2,1)} %refs_0_.3, ...), custom_call_target="tpu_custom_call" | custom-call | bytes 794704 | tf_op jit(solution)/shard_map/pallas_call | solution.py:29
  16.9 1.0 %shard_map.277 = (bf16[64,2560]{1,0:T(8,128)(2,1)S(1)}, bf16[640,1280]{1,0:T(8,128)(2,1)S(1)}) custom-call(bf16[32,640]{1,0:T(8,128)(2,1)S(1)} %get-tuple-element.47.refs_0_.refs_4_, bf16[32,640]{1,0:T(8,128)(2,1)S(1)} %collective-permute-done.refs_1_.refs_5_, bf16[32,640]{1,0:T(8,128)(2,1)S(1)} %collective-permute-done.1.refs_2_.refs_6_, ...), custom_call_target="tpu_custom_call" | custom-call | flops 209715200 | bytes 3276800 | tf_op jit(solution)/shard_map/pallas_call | solution.py:29
  17.9 1.5 %collective-permute-done.4.refs_1_ = bf16[64,384]{1,0:T(8,128)(2,1)S(1)} collective-permute-done((bf16[64,384]{1,0:T(8,128)(2,1)S(1)}, bf16[64,384]{1,0:T(8,128)(2,1)S(1)}, u32[]{:S(2)}, u32[]{:S(2)}) %collective-permute-start.4) | collective-permute-done | bytes 49184 | tf_op jit(solution)/shard_map/ppermute | solution.py:470
  19.7 0.6 %shard_map.279.begun._ = f32[64,1280]{1,0:T(8,128)S(1)} custom-call(s32[10]{0:T(128)S(1)} %get-tuple-element.43.req.slot_req, s32[10]{0:T(128)S(1)} %get-tuple-element.44.slot.slot_page, s32[8]{0:T(128)S(1)} %get-tuple-element.45.count.page_count, s32[8]{0:T(128)S(1)} %get-tuple-element.46.owner_row, f32[64,256]{1,0:T(8,128)S(1)} %get-tuple-element.58.packed.refs_4_, ...), custom_call_target="tpu_custom_call" | custom-call | flops 104857600 | bytes 6553600 | tf_op jit(solution)/shard_map/pallas_call | solution.py:29
  20.3 0.6 %collective-permute-done.8.packed = f32[64,256]{1,0:T(8,128)S(1)} collective-permute-done((f32[64,256]{1,0:T(8,128)S(1)}, f32[64,256]{1,0:T(8,128)S(1)}, u32[]{:S(2)}, u32[]{:S(2)}) %collective-permute-start.8) | collective-permute-done | bytes 65568 | tf_op jit(solution)/shard_map/ppermute | solution.py:467
  20.9 2.2 %shard_map.281 = bf16[64,1280]{1,0:T(8,128)(2,1)S(1)} custom-call(s32[10]{0:T(128)S(1)} %get-tuple-element.43.req.slot_req, s32[10]{0:T(128)S(1)} %get-tuple-element.44.slot.slot_page, s32[8]{0:T(128)S(1)} %get-tuple-element.45.count.page_count, s32[8]{0:T(128)S(1)} %get-tuple-element.46.owner_row, f32[64,256]{1,0:T(8,128)S(1)} %collective-permute-done.8.packed, ...), custom_call_target="tpu_custom_call" | custom-call | flops 209715200 | bytes 6553600 | tf_op jit(solution)/shard_map/pallas_call | solution.py:29
  23.2 0.6 %shard_map.280.mine = bf16[64,1280]{1,0:T(8,128)(2,1)S(1)} custom-call(s32[10]{0:T(128)S(1)} %get-tuple-element.43.req.slot_req, s32[10]{0:T(128)S(1)} %get-tuple-element.44.slot.slot_page, s32[8]{0:T(128)S(1)} %get-tuple-element.45.count.page_count, s32[8]{0:T(128)S(1)} %get-tuple-element.46.owner_row, f32[64,256]{1,0:T(8,128)S(1)} %get-tuple-element.58.packed.refs_4_, ...), custom_call_target="tpu_custom_call" | custom-call | flops 104857600 | bytes 6553600 | tf_op jit(solution)/shard_map/pallas_call | solution.py:29
  23.9 0.7 %collective-permute-done.9.other = bf16[64,1280]{1,0:T(8,128)(2,1)S(1)} collective-permute-done((bf16[64,1280]{1,0:T(8,128)(2,1)S(1)}, bf16[64,1280]{1,0:T(8,128)(2,1)S(1)}, u32[]{:S(2)}, u32[]{:S(2)}) %collective-permute-start.9) | collective-permute-done | bytes 163872 | tf_op jit(solution)/shard_map/ppermute | solution.py:467
  24.9 1.5 %collective-permute-start.11 = (bf16[16,3840]{1,0:T(8,128)(2,1)S(1)}, bf16[16,3840]{1,0:T(8,128)(2,1)S(1)}, u32[]{:S(2)}, u32[]{:S(2)}) collective-permute-start(bf16[16,3840]{1,0:T(8,128)(2,1)S(1)} %get-tuple-element.63), channel_id=1, source_target_pairs={{0,4},{1,5},{2,6},{3,7},{4,0},{5,1},{6,2},{7,3},{8,12},{9,13},{10,... | collective-permute-start | bytes 368648 | tf_op jit(solution)/shard_map/ppermute | solution.py:470
  26.4 1.8 %collective-permute-start.12 = (bf16[16,3840]{1,0:T(8,128)(2,1)S(1)}, bf16[16,3840]{1,0:T(8,128)(2,1)S(1)}, u32[]{:S(2)}, u32[]{:S(2)}) collective-permute-start(bf16[16,3840]{1,0:T(8,128)(2,1)S(1)} %get-tuple-element.64), channel_id=1, source_target_pairs={{0,2},{1,3},{2,0},{3,1},{4,6},{5,7},{6,4},{7,5},{8,10},{9,11},{10,... | collective-permute-start | bytes 368648 | tf_op jit(solution)/shard_map/ppermute | solution.py:470
  28.9 3.0 %collective-permute-done.10.refs_1_ = bf16[16,3840]{1,0:T(8,128)(2,1)S(1)} collective-permute-done((bf16[16,3840]{1,0:T(8,128)(2,1)S(1)}, bf16[16,3840]{1,0:T(8,128)(2,1)S(1)}, u32[]{:S(2)}, u32[]{:S(2)}) %collective-permute-start.10) | collective-permute-done | bytes 122912 | tf_op jit(solution)/shard_map/ppermute | solution.py:470
  31.8 1.1 %collective-permute-done.11.refs_2_ = bf16[16,3840]{1,0:T(8,128)(2,1)S(1)} collective-permute-done((bf16[16,3840]{1,0:T(8,128)(2,1)S(1)}, bf16[16,3840]{1,0:T(8,128)(2,1)S(1)}, u32[]{:S(2)}, u32[]{:S(2)}) %collective-permute-start.11) | collective-permute-done | bytes 122912 | tf_op jit(solution)/shard_map/ppermute | solution.py:470
  33.4 1.4 %collective-permute-start.15 = (bf16[16,1280]{1,0:T(8,128)(2,1)S(1)}, bf16[16,1280]{1,0:T(8,128)(2,1)S(1)}, u32[]{:S(2)}, u32[]{:S(2)}) collective-permute-start(bf16[16,1280]{1,0:T(8,128)(2,1)S(1)} %get-tuple-element.72.refs_0_), channel_id=1, source_target_pairs={{0,2},{1,3},{2,0},{3,1},{4,6},{5,7},{6,4},{7,5},{8,10},{9,11},{10,... | collective-permute-start | bytes 122888 | tf_op jit(solution)/shard_map/ppermute | solution.py:470
  35.4 1.5 %collective-permute-start.13 = (bf16[16,1280]{1,0:T(8,128)(2,1)S(1)}, bf16[16,1280]{1,0:T(8,128)(2,1)S(1)}, u32[]{:S(2)}, u32[]{:S(2)}) collective-permute-start(bf16[16,1280]{1,0:T(8,128)(2,1)S(1)} %get-tuple-element.72.refs_0_), channel_id=1, source_target_pairs={{0,6},{1,7},{2,4},{3,5},{4,2},{5,3},{6,0},{7,1},{8,14},{9,15},{10,... | collective-permute-start | bytes 122888 | tf_op jit(solution)/shard_map/ppermute | solution.py:470
  37.6 1.6 %collective-permute-done.14.refs_2_ = bf16[16,1280]{1,0:T(8,128)(2,1)S(1)} collective-permute-done((bf16[16,1280]{1,0:T(8,128)(2,1)S(1)}, bf16[16,1280]{1,0:T(8,128)(2,1)S(1)}, u32[]{:S(2)}, u32[]{:S(2)}) %collective-permute-start.14) | collective-permute-done | bytes 40992 | tf_op jit(solution)/shard_map/ppermute | solution.py:470
  39.2 1.2 %collective-permute-done.13.refs_1_ = bf16[16,1280]{1,0:T(8,128)(2,1)S(1)} collective-permute-done((bf16[16,1280]{1,0:T(8,128)(2,1)S(1)}, bf16[16,1280]{1,0:T(8,128)(2,1)S(1)}, u32[]{:S(2)}, u32[]{:S(2)}) %collective-permute-start.13) | collective-permute-done | bytes 40992 | tf_op jit(solution)/shard_map/ppermute | solution.py:470
  40.3 0.6 %shard_map.284 = (bf16[16,768]{1,0:T(8,128)(2,1)S(1)}, bf16[16,768]{1,0:T(8,128)(2,1)S(1)}, bf16[16,768]{1,0:T(8,128)(2,1)S(1)}, bf16[16,768]{1,0:T(8,128)(2,1)S(1)}) custom-call(bf16[16,1280]{1,0:T(8,128)(2,1)S(1)} %get-tuple-element.72.refs_0_, bf16[16,1280]{1,0:T(8,128)(2,1)S(1)} %collective-permute-done.13.refs_1_, ...), custom_call_target="tpu_custom_call" | custom-call | flops 104857600 | bytes 1638400 | tf_op jit(solution)/shard_map/pallas_call | solution.py:29
  41.0 0.7 %collective-permute-start.16 = (bf16[16,768]{1,0:T(8,128)(2,1)S(1)}, bf16[16,768]{1,0:T(8,128)(2,1)S(1)}, u32[]{:S(2)}, u32[]{:S(2)}) collective-permute-start(bf16[16,768]{1,0:T(8,128)(2,1)S(1)} %get-tuple-element.75), channel_id=1, source_target_pairs={{0,0},{1,1},{2,8},{3,9},{4,16},{5,17},{6,24},{7,25},{8,2},{9,3},{1... | collective-permute-start | bytes 73736 | tf_op jit(solution)/shard_map/ppermute | solution.py:603
  41.7 4.4 %collective-permute-start.17 = (bf16[16,768]{1,0:T(8,128)(2,1)S(1)}, bf16[16,768]{1,0:T(8,128)(2,1)S(1)}, u32[]{:S(2)}, u32[]{:S(2)}) collective-permute-start(bf16[16,768]{1,0:T(8,128)(2,1)S(1)} %get-tuple-element.76), channel_id=1, source_target_pairs={{0,2},{1,3},{2,10},{3,11},{4,18},{5,19},{6,26},{7,27},{8,4},{9,5},... | collective-permute-start | bytes 73736 | tf_op jit(solution)/shard_map/ppermute | solution.py:603
  46.0 3.2 %collective-permute-start.18 = (bf16[16,768]{1,0:T(8,128)(2,1)S(1)}, bf16[16,768]{1,0:T(8,128)(2,1)S(1)}, u32[]{:S(2)}, u32[]{:S(2)}) collective-permute-start(bf16[16,768]{1,0:T(8,128)(2,1)S(1)} %get-tuple-element.77), channel_id=1, source_target_pairs={{0,4},{1,5},{2,12},{3,13},{4,20},{5,21},{6,28},{7,29},{8,6},{9,7},... | collective-permute-start | bytes 73736 | tf_op jit(solution)/shard_map/ppermute | solution.py:603
  49.2 1.3 %collective-permute-start.19 = (bf16[16,768]{1,0:T(8,128)(2,1)S(1)}, bf16[16,768]{1,0:T(8,128)(2,1)S(1)}, u32[]{:S(2)}, u32[]{:S(2)}) collective-permute-start(bf16[16,768]{1,0:T(8,128)(2,1)S(1)} %get-tuple-element.78), channel_id=1, source_target_pairs={{0,6},{1,7},{2,14},{3,15},{4,22},{5,23},{6,30},{7,31},{8,0},{9,1},... | collective-permute-start | bytes 73736 | tf_op jit(solution)/shard_map/ppermute | solution.py:603
  50.6 0.6 %fusion.1 = bf16[1,3,1280]{2,1,0:T(4,128)(2,1)} fusion(s32[]{:T(128)S(6)} %select_n.4, bf16[16,1280]{1,0:T(8,128)(2,1)S(1)} %get-tuple-element.80, bf16[3,1280]{1,0:T(4,128)(2,1)S(1)} %bitcast.18), kind=kLoop, calls=%fused_computation.5 | loop fusion | flops 15360 | bytes 56324 | tf_op jit(solution)/shard_map/broadcast_in_dim | solution.py:614
  51.2 1.4 %shard_map.286 = f32[20,64,128]{2,1,0:T(8,128)} custom-call(s32[1]{0:T(128)} %copy.30.accepted, f32[64,256]{1,0:T(8,128)S(1)} %get-tuple-element.58.packed.refs_4_, f32[16,20]{1,0:T(8,128)S(1)} %get-tuple-element.66.refs_6_.dtime_ref, bf16[16,1280]{1,0:T(8,128)(2,1)S(1)} %get-tuple-element.79.x_act, bf16[16,256]{1,0:T(8,128)(2,1)S(1)} %get-tuple-element.65.refs_5_.bc_act, ...), custom_call_target="tpu_custom_call" | custom-call | flops 10485760 | bytes 1310720 | tf_op jit(solution)/shard_map/pallas_call | solution.py:29
  52.6 0.8 %collective-permute-done.18.refs_2_ = bf16[16,768]{1,0:T(8,128)(2,1)S(1)} collective-permute-done((bf16[16,768]{1,0:T(8,128)(2,1)S(1)}, bf16[16,768]{1,0:T(8,128)(2,1)S(1)}, u32[]{:S(2)}, u32[]{:S(2)}) %collective-permute-start.18) | collective-permute-done | bytes 24608 | tf_op jit(solution)/shard_map/ppermute | solution.py:603
  53.9 0.8 %shard_map.285 = bf16[16,640]{1,0:T(8,128)(2,1)} custom-call(bf16[16,768]{1,0:T(8,128)(2,1)S(1)} %collective-permute-done.16.refs_0_, bf16[16,768]{1,0:T(8,128)(2,1)S(1)} %collective-permute-done.17.refs_1_, bf16[16,768]{1,0:T(8,128)(2,1)S(1)} %collective-permute-done.18.refs_2_, bf16[16,768]{1,0:T(8,128)(2,1)S(1)} %collective-permute-done.19.refs_3_), custom_call_target="tpu_custom_call" | custom-call | flops 51200 | bytes 51200 | tf_op jit(solution)/shard_map/pallas_call | solution.py:29
  (30 shorter events, 5.2 us)
Async XLA Ops:
  2.6 14.4 %collective-permute-start.7 = (bf16[960,1280]{1,0:T(8,128)(2,1)S(1)}, bf16[960,1280]{1,0:T(8,128)(2,1)S(1)}, u32[]{:S(2)}, u32[]{:S(2)}) collective-permute-start(bf16[960,1280]{1,0:T(8,128)(2,1)S(1)} %get-tuple-element.56.refs_4_), channel_id=1, source_target_pairs={{0,1},{1,0},{2,3},{3,2},{4,5},{5,4},{6,7},{7,6},{8,9},{9,8},{10,11... | collective-permute-start | bytes 7372808 | tf_op jit(solution)/shard_map/ppermute | solution.py:467
  3.1 8.5 %collective-permute-start.3 = (bf16[352,384]{1,0:T(8,128)(2,1)S(1)}, bf16[352,384]{1,0:T(8,128)(2,1)S(1)}, u32[]{:S(2)}, u32[]{:S(2)}) collective-permute-start(bf16[352,384]{1,0:T(8,128)(2,1)S(1)} %get-tuple-element.51.refs_4_), channel_id=1, source_target_pairs={{0,1},{1,0},{2,3},{3,2},{4,5},{5,4},{6,7},{7,6},{8,9},{9,8},{10,11... | collective-permute-start | bytes 811016 | tf_op jit(solution)/shard_map/ppermute | solution.py:467
  3.2 4.9 %collective-permute-start.2 = (bf16[32,640]{1,0:T(8,128)(2,1)S(1)}, bf16[32,640]{1,0:T(8,128)(2,1)S(1)}, u32[]{:S(2)}, u32[]{:S(2)}) collective-permute-start(bf16[32,640]{1,0:T(8,128)(2,1)S(1)} %get-tuple-element.50), channel_id=1, source_target_pairs={{0,2},{1,3},{2,0},{3,1},{4,6},{5,7},{6,4},{7,5},{8,10},{9,11},{10,... | collective-permute-start | bytes 122888 | tf_op jit(solution)/shard_map/ppermute | solution.py:470
  6.1 4.9 %collective-permute-start = (bf16[32,640]{1,0:T(8,128)(2,1)S(1)}, bf16[32,640]{1,0:T(8,128)(2,1)S(1)}, u32[]{:S(2)}, u32[]{:S(2)}) collective-permute-start(bf16[32,640]{1,0:T(8,128)(2,1)S(1)} %get-tuple-element.48), channel_id=1, source_target_pairs={{0,6},{1,7},{2,4},{3,5},{4,2},{5,3},{6,0},{7,1},{8,14},{9,15},{10,... | collective-permute-start | bytes 122888 | tf_op jit(solution)/shard_map/ppermute | solution.py:470
  7.6 4.0 %collective-permute-start.1 = (bf16[32,640]{1,0:T(8,128)(2,1)S(1)}, bf16[32,640]{1,0:T(8,128)(2,1)S(1)}, u32[]{:S(2)}, u32[]{:S(2)}) collective-permute-start(bf16[32,640]{1,0:T(8,128)(2,1)S(1)} %get-tuple-element.49), channel_id=1, source_target_pairs={{0,4},{1,5},{2,6},{3,7},{4,0},{5,1},{6,2},{7,3},{8,12},{9,13},{10,... | collective-permute-start | bytes 122888 | tf_op jit(solution)/shard_map/ppermute | solution.py:470
  12.0 5.9 %collective-permute-start.6 = (bf16[64,384]{1,0:T(8,128)(2,1)S(1)}, bf16[64,384]{1,0:T(8,128)(2,1)S(1)}, u32[]{:S(2)}, u32[]{:S(2)}) collective-permute-start(bf16[64,384]{1,0:T(8,128)(2,1)S(1)} %shard_map.275.refs_12_.refs_0_), channel_id=1, source_target_pairs={{0,2},{1,3},{2,0},{3,1},{4,6},{5,7},{6,4},{7,5},{8,10},{9,11},{10,... | collective-permute-start | bytes 147464 | tf_op jit(solution)/shard_map/ppermute | solution.py:470
  13.5 4.4 %collective-permute-start.5 = (bf16[64,384]{1,0:T(8,128)(2,1)S(1)}, bf16[64,384]{1,0:T(8,128)(2,1)S(1)}, u32[]{:S(2)}, u32[]{:S(2)}) collective-permute-start(bf16[64,384]{1,0:T(8,128)(2,1)S(1)} %shard_map.275.refs_12_.refs_0_), channel_id=1, source_target_pairs={{0,4},{1,5},{2,6},{3,7},{4,0},{5,1},{6,2},{7,3},{8,12},{9,13},{10,... | collective-permute-start | bytes 147464 | tf_op jit(solution)/shard_map/ppermute | solution.py:470
  14.4 5.0 %collective-permute-start.4 = (bf16[64,384]{1,0:T(8,128)(2,1)S(1)}, bf16[64,384]{1,0:T(8,128)(2,1)S(1)}, u32[]{:S(2)}, u32[]{:S(2)}) collective-permute-start(bf16[64,384]{1,0:T(8,128)(2,1)S(1)} %shard_map.275.refs_12_.refs_0_), channel_id=1, source_target_pairs={{0,6},{1,7},{2,4},{3,5},{4,2},{5,3},{6,0},{7,1},{8,14},{9,15},{10,... | collective-permute-start | bytes 147464 | tf_op jit(solution)/shard_map/ppermute | solution.py:470
  19.6 1.3 %collective-permute-start.8 = (f32[64,256]{1,0:T(8,128)S(1)}, f32[64,256]{1,0:T(8,128)S(1)}, u32[]{:S(2)}, u32[]{:S(2)}) collective-permute-start(f32[64,256]{1,0:T(8,128)S(1)} %get-tuple-element.58.packed.refs_4_), channel_id=1, source_target_pairs={{0,1},{1,0},{2,3},{3,2},{4,5},{5,4},{6,7},{7,6},{8,9},{9,8},{10,11... | collective-permute-start | bytes 196616 | tf_op jit(solution)/shard_map/ppermute | solution.py:467
  23.1 13.9 %copy-start.2 = (bf16[1,3,256]{2,1,0:T(4,128)(2,1)S(1)}, bf16[1,3,256]{2,1,0:T(4,128)(2,1)}, u32[]{:S(2)}) copy-start(bf16[1,3,256]{2,1,0:T(4,128)(2,1)} %history_hbm.1) | copy-start | bytes 4612
  23.1 1.5 %collective-permute-start.9 = (bf16[64,1280]{1,0:T(8,128)(2,1)S(1)}, bf16[64,1280]{1,0:T(8,128)(2,1)S(1)}, u32[]{:S(2)}, u32[]{:S(2)}) collective-permute-start(bf16[64,1280]{1,0:T(8,128)(2,1)S(1)} %shard_map.281), channel_id=1, source_target_pairs={{0,1},{1,0},{2,3},{3,2},{4,5},{5,4},{6,7},{7,6},{8,9},{9,8},{10,11... | collective-permute-start | bytes 491528 | tf_op jit(solution)/shard_map/ppermute | solution.py:467
  23.9 26.7 %copy-start.1 = (bf16[1,3,1280]{2,1,0:T(4,128)(2,1)S(1)}, bf16[1,3,1280]{2,1,0:T(4,128)(2,1)}, u32[]{:S(2)}) copy-start(bf16[1,3,1280]{2,1,0:T(4,128)(2,1)} %refs_7_.1) | copy-start | bytes 23044
  23.9 27.3 %copy-start = (f32[1,20,64,128]{3,2,1,0:T(8,128)S(1)}, f32[1,20,64,128]{3,2,1,0:T(8,128)}, u32[]{:S(2)}) copy-start(f32[1,20,64,128]{3,2,1,0:T(8,128)} %param.41) | copy-start | bytes 1966084
  24.6 7.2 %collective-permute-start.10 = (bf16[16,3840]{1,0:T(8,128)(2,1)S(1)}, bf16[16,3840]{1,0:T(8,128)(2,1)S(1)}, u32[]{:S(2)}, u32[]{:S(2)}) collective-permute-start(bf16[16,3840]{1,0:T(8,128)(2,1)S(1)} %get-tuple-element.62), channel_id=1, source_target_pairs={{0,6},{1,7},{2,4},{3,5},{4,2},{5,3},{6,0},{7,1},{8,14},{9,15},{10,... | collective-permute-start | bytes 368648 | tf_op jit(solution)/shard_map/ppermute | solution.py:470
  24.9 8.1 %collective-permute-start.11 = (bf16[16,3840]{1,0:T(8,128)(2,1)S(1)}, bf16[16,3840]{1,0:T(8,128)(2,1)S(1)}, u32[]{:S(2)}, u32[]{:S(2)}) collective-permute-start(bf16[16,3840]{1,0:T(8,128)(2,1)S(1)} %get-tuple-element.63), channel_id=1, source_target_pairs={{0,4},{1,5},{2,6},{3,7},{4,0},{5,1},{6,2},{7,3},{8,12},{9,13},{10,... | collective-permute-start | bytes 368648 | tf_op jit(solution)/shard_map/ppermute | solution.py:470
  26.4 6.7 %collective-permute-start.12 = (bf16[16,3840]{1,0:T(8,128)(2,1)S(1)}, bf16[16,3840]{1,0:T(8,128)(2,1)S(1)}, u32[]{:S(2)}, u32[]{:S(2)}) collective-permute-start(bf16[16,3840]{1,0:T(8,128)(2,1)S(1)} %get-tuple-element.64), channel_id=1, source_target_pairs={{0,2},{1,3},{2,0},{3,1},{4,6},{5,7},{6,4},{7,5},{8,10},{9,11},{10,... | collective-permute-start | bytes 368648 | tf_op jit(solution)/shard_map/ppermute | solution.py:470
  33.4 4.2 %collective-permute-start.15 = (bf16[16,1280]{1,0:T(8,128)(2,1)S(1)}, bf16[16,1280]{1,0:T(8,128)(2,1)S(1)}, u32[]{:S(2)}, u32[]{:S(2)}) collective-permute-start(bf16[16,1280]{1,0:T(8,128)(2,1)S(1)} %get-tuple-element.72.refs_0_), channel_id=1, source_target_pairs={{0,2},{1,3},{2,0},{3,1},{4,6},{5,7},{6,4},{7,5},{8,10},{9,11},{10,... | collective-permute-start | bytes 122888 | tf_op jit(solution)/shard_map/ppermute | solution.py:470
  34.8 4.3 %collective-permute-start.14 = (bf16[16,1280]{1,0:T(8,128)(2,1)S(1)}, bf16[16,1280]{1,0:T(8,128)(2,1)S(1)}, u32[]{:S(2)}, u32[]{:S(2)}) collective-permute-start(bf16[16,1280]{1,0:T(8,128)(2,1)S(1)} %get-tuple-element.72.refs_0_), channel_id=1, source_target_pairs={{0,4},{1,5},{2,6},{3,7},{4,0},{5,1},{6,2},{7,3},{8,12},{9,13},{10,... | collective-permute-start | bytes 122888 | tf_op jit(solution)/shard_map/ppermute | solution.py:470
  35.4 4.9 %collective-permute-start.13 = (bf16[16,1280]{1,0:T(8,128)(2,1)S(1)}, bf16[16,1280]{1,0:T(8,128)(2,1)S(1)}, u32[]{:S(2)}, u32[]{:S(2)}) collective-permute-start(bf16[16,1280]{1,0:T(8,128)(2,1)S(1)} %get-tuple-element.72.refs_0_), channel_id=1, source_target_pairs={{0,6},{1,7},{2,4},{3,5},{4,2},{5,3},{6,0},{7,1},{8,14},{9,15},{10,... | collective-permute-start | bytes 122888 | tf_op jit(solution)/shard_map/ppermute | solution.py:470
  41.0 11.6 %collective-permute-start.16 = (bf16[16,768]{1,0:T(8,128)(2,1)S(1)}, bf16[16,768]{1,0:T(8,128)(2,1)S(1)}, u32[]{:S(2)}, u32[]{:S(2)}) collective-permute-start(bf16[16,768]{1,0:T(8,128)(2,1)S(1)} %get-tuple-element.75), channel_id=1, source_target_pairs={{0,0},{1,1},{2,8},{3,9},{4,16},{5,17},{6,24},{7,25},{8,2},{9,3},{1... | collective-permute-start | bytes 73736 | tf_op jit(solution)/shard_map/ppermute | solution.py:603
  41.7 11.0 %collective-permute-start.17 = (bf16[16,768]{1,0:T(8,128)(2,1)S(1)}, bf16[16,768]{1,0:T(8,128)(2,1)S(1)}, u32[]{:S(2)}, u32[]{:S(2)}) collective-permute-start(bf16[16,768]{1,0:T(8,128)(2,1)S(1)} %get-tuple-element.76), channel_id=1, source_target_pairs={{0,2},{1,3},{2,10},{3,11},{4,18},{5,19},{6,26},{7,27},{8,4},{9,5},... | collective-permute-start | bytes 73736 | tf_op jit(solution)/shard_map/ppermute | solution.py:603
  46.0 7.5 %collective-permute-start.18 = (bf16[16,768]{1,0:T(8,128)(2,1)S(1)}, bf16[16,768]{1,0:T(8,128)(2,1)S(1)}, u32[]{:S(2)}, u32[]{:S(2)}) collective-permute-start(bf16[16,768]{1,0:T(8,128)(2,1)S(1)} %get-tuple-element.77), channel_id=1, source_target_pairs={{0,4},{1,5},{2,12},{3,13},{4,20},{5,21},{6,28},{7,29},{8,6},{9,7},... | collective-permute-start | bytes 73736 | tf_op jit(solution)/shard_map/ppermute | solution.py:603
  49.2 4.6 %collective-permute-start.19 = (bf16[16,768]{1,0:T(8,128)(2,1)S(1)}, bf16[16,768]{1,0:T(8,128)(2,1)S(1)}, u32[]{:S(2)}, u32[]{:S(2)}) collective-permute-start(bf16[16,768]{1,0:T(8,128)(2,1)S(1)} %get-tuple-element.78), channel_id=1, source_target_pairs={{0,6},{1,7},{2,14},{3,15},{4,22},{5,23},{6,30},{7,31},{8,0},{9,1},... | collective-permute-start | bytes 73736 | tf_op jit(solution)/shard_map/ppermute | solution.py:603
